TPU v7x, 32 devices: a whole 2x2x4 slice. The times are simulated.
32 devices in a mesh: order: 4 (over y, x), lat: 8 (over z, core).
Axes of the slice: x: 2, y: 2, z: 4, core: 2. Of those that a mesh axis runs over, the one named last changes fastest.
Arguments:
- fourier: bfloat16 [128, 64, 2048], P('order', None, 'lat'), may hold values from -6 to 6
- quad_weights: float32 [2048], P('lat'), may hold values from 0.5 to 1.5
- leaf_basis: bfloat16 [128, 64, 2048], P('order', None, 'lat'), may hold values from -0.375 to 0.375
- level_factors: bfloat16 [128, 3, 2, 8, 64, 64], P('order', None, None, 'lat'), may hold values from -0.5 to 0.5
- sparsity: int32 [128, 3, 8], P('order', None, 'lat'), may hold values 0 or 1
- root_basis: bfloat16 [128, 64, 2048], P(None, None, 'lat'), may hold values from -0.75 to 0.75
- order_of_slot: int32 [128], replicated, may hold values from 0 to 127, each once
Outputs:
- spectra: bfloat16 [32, 2, 2048, 128], P('order', None, 'lat')
Inputs may be any that keep to these rules, and one draw needn't show every extreme that they name: `order_of_slot`: every window index appears in exactly one slot.
All inputs are finite; a program needn't handle non-finite values. No bound on the sum of `sparsity` on one device may be relied on, other than what follows from the above.
Results may differ from a plain program's by a relative error of at most 0.0081.
Values may be sent and summed in bfloat16 or wider, within the bound.
No kernel may reach another device: no remote copies, remote signals or barrier semaphores. Data moves between devices by JAX's collectives and lax.ppermute only.
A program may use at most 64 MiB of HBM per device.

v0:
```python
import functools

import jax
import jax.numpy as jnp
from jax import lax
from jax.experimental import pallas as pl
from jax.experimental.pallas import tpu as pltpu
from jax.sharding import PartitionSpec as P

DEGREES = 2048
F32, BF16 = jnp.float32, jnp.bfloat16
MIB = 1 << 20
IN_HBM = pl.BlockSpec(memory_space=pltpu.HBM)
IN_SMEM = pl.BlockSpec(memory_space=pltpu.SMEM)
ANYWHERE = pl.BlockSpec(memory_space=pl.ANY)


def contract(lhs, rhs, dims):
    return lax.dot_general(lhs, rhs, (dims, ((), ())), preferred_element_type=F32)


def in_hbm(array):
    return pltpu.with_memory_space_constraint(array, pltpu.HBM)


def call(kernel, name, out_shape, in_specs, flops, size, scratch=(), mib=16, **more):
    return pl.pallas_call(
        kernel,
        out_shape=out_shape,
        in_specs=in_specs,
        scratch_shapes=list(scratch),
        compiler_params=pltpu.CompilerParams(vmem_limit_bytes=mib * MIB),
        cost_estimate=pl.CostEstimate(flops=flops // 1000, bytes_accessed=size // 1000, transcendentals=0),
        name=name,
        **more,
    )


def whole_blocks(count):
    return [pl.BlockSpec()] * count


def fetch_roots(k, root_hbm, root_ref, sem):
    here = root_ref.shape[0]
    me = lax.axis_index("order")
    return pltpu.make_async_copy(root_hbm.at[pl.ds((me ^ k) * here, here)], root_ref, sem)


def leaf_kernel(
    pieces, group, fourier_hbm, weight_hbm, leaf_hbm, root_hbm, state_ref, root_ref, fourier_ref, weight_ref, leaf_ref, sems
):
    side = lax.axis_index("order") & 1
    slots, columns, lats = fourier_ref.shape
    rank = leaf_ref.shape[1]
    per = slots // pieces
    copies = [pltpu.make_async_copy(weight_hbm, weight_ref, sems.at[0])]
    for piece in range(pieces):
        part = pl.ds(piece * per, per)
        copies.append(pltpu.make_async_copy(fourier_hbm.at[part], fourier_ref.at[part], sems.at[1 + 2 * piece]))
        copies.append(pltpu.make_async_copy(leaf_hbm.at[part], leaf_ref.at[part], sems.at[2 + 2 * piece]))
    copies.append(fetch_roots(0, root_hbm, root_ref, sems.at[1 + 2 * pieces]))
    for copy in copies:
        copy.start()
    copies[0].wait()
    weight = weight_ref[...]
    mine = lax.broadcasted_iota(jnp.int32, (columns, 2 * rank), 1) < rank
    for pair in range(slots // 2):
        if 2 * pair % per == 0:
            copies[1 + 2 * (2 * pair // per)].wait()
            copies[2 + 2 * (2 * pair // per)].wait()
        both = pl.ds(2 * pair, 2)
        weighted = (fourier_ref[both].astype(F32) * weight[None]).astype(BF16)
        product = contract(
            weighted.reshape(2 * columns, lats), leaf_ref[both].reshape(2 * rank, lats), ((1,), (1,))
        )
        state = jnp.where(mine, product[:columns], product[columns:]).astype(BF16)
        if group % 16:
            state_ref[pair] = state
            continue
        for owner in range(columns // group):
            rows = pl.ds(owner // 2 * group, group)
            state_ref[pair, owner % 2 ^ side, rows] = state[owner * group : (owner + 1) * group]
    copies[-1].wait()


def leaf_states(fourier, quad_weights, leaf_basis, root_basis, owners):
    slots, columns, lats = fourier.shape
    rank = leaf_basis.shape[1]
    pairs, half, lanes, group = slots // 2, columns // 2, 2 * rank, columns // owners
    pieces = 2
    shape = (pairs, columns, lanes) if group % 16 else (pairs, 2, half, lanes)
    state, root = call(
        functools.partial(leaf_kernel, pieces, group),
        "leaf",
        [
            jax.ShapeDtypeStruct(shape, BF16),
            jax.ShapeDtypeStruct((root_basis.shape[0] // owners, *root_basis.shape[1:]), BF16),
        ],
        [IN_HBM] * 4,
        2 * slots * columns * rank * lats,
        4 * slots * columns * lats,
        [
            pltpu.VMEM((slots, columns, lats), BF16),
            pltpu.VMEM((1, lats), F32),
            pltpu.VMEM((slots, rank, lats), BF16),
            pltpu.SemaphoreType.DMA((2 + 2 * pieces,)),
        ],
    )(fourier, quad_weights, leaf_basis, root_basis)
    if group % 16:
        side = lax.axis_index("order") & 1
        state = state.reshape(pairs, owners // 2, 2, group, lanes)
        sides = [lax.dynamic_index_in_dim(state, side ^ i, 2, False).reshape(pairs, half, lanes) for i in range(2)]
        state = jnp.stack(sides, axis=1)
    return state, root


def factor_kernel(levels, pieces, roots, factor_hbm, present_hbm, after, *refs):
    del after
    weight_refs, (factor_ref, present_ref, sems) = list(refs[:-3]), refs[-3:]
    fetches = []
    if roots:
        root_hbm, root_ref = weight_refs.pop(0), weight_refs.pop()
        fetches.append(fetch_roots(1, root_hbm, root_ref, sems.at[len(levels) * pieces + 1]))
    present_copy = pltpu.make_async_copy(present_hbm, present_ref, sems.at[len(levels) * pieces])
    present_copy.start()
    _, slots, _, rank, _ = factor_ref.shape
    per = slots // pieces
    copies = {}
    for i, level in enumerate(levels):
        for piece in range(pieces):
            part = pl.ds(piece * per, per)
            copies[i, piece] = pltpu.make_async_copy(
                factor_hbm.at[part, level, :, 0], factor_ref.at[i, part], sems.at[i * pieces + piece]
            )
            copies[i, piece].start()
    for fetch in fetches:
        fetch.start()
    empty = jnp.zeros((rank, rank), BF16)
    present_copy.wait()
    for i, level in enumerate(levels):
        for pair in range(slots // 2):
            if 2 * pair % per == 0:
                copies[i, 2 * pair // per].wait()
            for half in range(2):
                first, second = (factor_ref[i, slot, half] for slot in (2 * pair, 2 * pair + 1))
                if half:
                    first = jnp.where(present_ref[level, 0, 2 * pair] != 0, first, empty)
                    second = jnp.where(present_ref[level, 0, 2 * pair + 1] != 0, second, empty)
                if weight_refs[i].shape[1] == rank:
                    weight_refs[i + half][pair] = jnp.concatenate([first, second], axis=1)
                    continue
                lanes = pl.ds(half * 2 * rank, 2 * rank)
                weight_refs[i][pair, :rank, lanes] = jnp.concatenate([first, empty], axis=1)
                weight_refs[i][pair, rank:, lanes] = jnp.concatenate([empty, second], axis=1)
    for fetch in fetches:
        fetch.wait()


def level_weights(level_factors, present, levels, after, root_basis=None):
    slots, last, _, _, rank, _ = level_factors.shape
    count, pieces = len(levels), 2
    roots = []
    if root_basis is not None:
        roots = [jax.ShapeDtypeStruct((root_basis.shape[0] // lax.axis_size("order"), *root_basis.shape[1:]), BF16)]
    return call(
        functools.partial(factor_kernel, levels, pieces, root_basis is not None),
        "factors",
        [
            jax.ShapeDtypeStruct((slots // 2, *((rank, 2 * rank) if level == last - 1 else (2 * rank, 4 * rank))), BF16)
            for level in levels
            for _ in range(1 + (level == last - 1))
        ]
        + roots,
        [IN_HBM, IN_HBM, ANYWHERE] + [IN_HBM] * len(roots),
        slots * rank * rank * 4 * count,
        slots * rank * rank * 16 * count,
        [
            pltpu.VMEM((count, slots, 2, rank, rank), BF16),
            pltpu.SMEM(present.shape, jnp.int32),
            pltpu.SemaphoreType.DMA((count * pieces + 1 + len(roots),)),
        ],
        mib=24,
    )(level_factors, present, after, *([root_basis] if roots else []))


def level_kernel(side, axis, state_ref, partner_ref, weight_ref, *refs):
    if len(refs) > 1:
        own_ref, *refs = refs
    out_ref = refs[0]
    me = lax.axis_index(axis) // 2
    for pair in range(weight_ref.shape[0]):
        at = pair if side is None else (pair, side)
        both = jnp.concatenate([state_ref[at], partner_ref[at]], axis=1)
        result = contract(both, weight_ref[pair], ((1,), (1,))).astype(BF16)
        if len(refs) == 1:
            out_ref[pair] = result
            continue
        early_ref, term_ref, groups_ref = refs[1:]
        owners, group, _ = groups_ref.shape[1:]
        for owner in range(owners):
            groups_ref[pair, owner] = result[owner * group : (owner + 1) * group]
        for k in range(owners):
            rows = pl.ds((k - 1) % owners * group, group)
            part = groups_ref[pair, me ^ k]
            out_ref[pair, rows] = part
            if k:
                early_ref[pair, rows] = part
        term_ref[pair] = contract(out_ref[pair], by_slot(own_ref[pair]), ((1,), (1,))).astype(BF16)


def next_states(name, state, partner, weights, side=None, owners=1, own=None):
    pairs, rows, lanes = state.shape[0], *state.shape[-2:]
    group = rows // owners
    split = owners > 1 and group % 16 == 0
    shapes = [(pairs, rows, lanes)] + [(pairs, rows - group, lanes), (pairs, rows, lanes)] * split
    outs = call(
        functools.partial(level_kernel, side, "order"),
        name,
        [jax.ShapeDtypeStruct(shape, BF16) for shape in shapes],
        whole_blocks(3 + split),
        4 * pairs * rows * lanes * lanes,
        6 * pairs * rows * lanes,
        [pltpu.VMEM((pairs, owners, group, lanes), BF16)] if split else [],
    )(state, partner, weights, *([own] if split else []))
    if owners > 1 and not split:
        me = lax.axis_index("order") // 2
        parts = [lax.dynamic_slice_in_dim(outs[0], (me ^ k) * group, group, 1) for k in range(owners)]
        early = jnp.concatenate(parts[1:], axis=1)
        state = jnp.concatenate([early, parts[0]], axis=1)
        return [state, early, own_term(state, own)]
    return outs if split else outs[0]


def late_kernel(after, state_ref, out_ref):
    del after
    rows = out_ref.shape[1]
    for pair in range(state_ref.shape[0]):
        out_ref[pair] = state_ref[pair, state_ref.shape[1] - rows :]


def late_columns(after, state, rows):
    pairs, columns, lanes = state.shape
    if rows % 16:
        return state[:, columns - rows :]
    return call(
        late_kernel,
        "late_columns",
        jax.ShapeDtypeStruct((pairs, rows, lanes), BF16),
        [ANYWHERE] + whole_blocks(1),
        1,
        4 * pairs * rows * lanes,
    )(after, state)


def by_slot(packed):
    first = lax.broadcasted_iota(jnp.int32, packed.shape, 1) < packed.shape[0]
    empty = jnp.zeros(packed.shape, BF16)
    return jnp.concatenate([jnp.where(first, packed, empty), jnp.where(first, empty, packed)], axis=0)


def own_term_kernel(state_ref, own_ref, out_ref):
    for pair in range(state_ref.shape[0]):
        out_ref[pair] = contract(state_ref[pair], by_slot(own_ref[pair]), ((1,), (1,))).astype(BF16)


def own_term(state, own):
    pairs, rows, lanes = state.shape
    return call(
        own_term_kernel,
        "own_term",
        jax.ShapeDtypeStruct(state.shape, BF16),
        whole_blocks(2),
        2 * pairs * rows * lanes * lanes,
        6 * pairs * rows * lanes,
    )(state, own)


def last_level_kernel(turn, begin, axis, after, own_ref, partner_ref, cross_ref, *refs):
    del after
    refs = list(refs)
    own_factor_ref = refs.pop(0) if refs[0].shape == cross_ref.shape else None
    out_refs, groups_ref = refs[:-1], refs[-1]
    me = lax.axis_index(axis) // 2 if turn else 0
    pairs, owners, group, _ = groups_ref.shape
    for pair in range(pairs):
        cross = by_slot(cross_ref[pair])
        own = own_ref[pair, begin : begin + owners * group]
        if own_factor_ref is None:
            result = own.astype(F32) + contract(partner_ref[pair], cross, ((1,), (1,)))
        else:
            weight = jnp.concatenate([by_slot(own_factor_ref[pair]), cross], axis=1)
            both = jnp.concatenate([own, partner_ref[pair]], axis=1)
            result = contract(both, weight, ((1,), (1,)))
        result = result.astype(BF16)
        if group % 16:
            out_refs[0][pair] = result
            continue
        for owner in range(owners):
            groups_ref[pair, owner] = result[owner * group : (owner + 1) * group]
    if group % 16 == 0:
        for k, out_ref in enumerate(out_refs):
            for pair in range(pairs):
                out_ref[pl.ds(pair * group, group)] = groups_ref[pair, me ^ k]


def last_states(name, after, own, partner, factors, owners, turn, begin=0):
    pairs, columns, lanes = partner.shape
    group = columns // owners
    rows = pairs * group
    aligned = group % 16 == 0
    if not aligned:
        own = own[:, begin : begin + columns]
        begin = 0
    parts = call(
        functools.partial(last_level_kernel, turn, begin, "order"),
        name,
        [jax.ShapeDtypeStruct((rows, lanes), BF16)] * owners if aligned else [jax.ShapeDtypeStruct(own.shape, BF16)],
        [ANYWHERE] + whole_blocks(2 + len(factors)),
        4 * pairs * columns * lanes * lanes,
        6 * pairs * columns * lanes,
        [pltpu.VMEM((pairs, owners, group, lanes), BF16)],
    )(after, own, partner, *factors)
    if aligned:
        return parts
    me = lax.axis_index("order") // 2 if turn else 0
    parts = [lax.dynamic_slice_in_dim(parts[0], (me ^ k) * group, group, 1) for k in range(owners)]
    return [part.reshape(rows, lanes) for part in parts]


def near_kernel(group, root_hbm, order_ref, after, root_ref, place_ref, alive_ref, rows_ref, sems):
    del after
    early = root_ref.shape[0]
    owners, here, slots = place_ref.shape
    degrees = alive_ref.shape[0]
    me = lax.axis_index("order")
    copies = []
    for k in range(early):
        copies.append(fetch_roots(2 + k, root_hbm, root_ref.at[k], sems.at[k]))
        copies[-1].start()
    lane = lax.broadcasted_iota(jnp.int32, (1, slots), 1)
    for k in range(owners):
        for slot in range(here):
            pair, half = slot // 2, slot % 2
            row = (pair // group * 2 + half) * group + pair % group
            rows_ref[pl.ds(row, 1), :] = (lane == order_ref[(me ^ k) * here + slot]).astype(F32)
        place_ref[k] = rows_ref[...].astype(BF16)
    degree = lax.axis_index("lat") * degrees + lax.broadcasted_iota(jnp.int32, (degrees, slots), 0)
    window = DEGREES // slots * lax.broadcasted_iota(jnp.int32, (degrees, slots), 1)
    alive_ref[...] = (degree >= window).astype(F32).astype(BF16)
    for copy in copies:
        copy.wait()


def near_roots(root_basis, order_of_slot, owners, early, group, after):
    slots, rank, degrees = root_basis.shape
    here = slots // owners
    return call(
        functools.partial(near_kernel, group),
        "near_roots",
        [
            jax.ShapeDtypeStruct((early, here, rank, degrees), BF16),
            jax.ShapeDtypeStruct((owners, here, slots), BF16),
            jax.ShapeDtypeStruct((degrees, slots), BF16),
        ],
        [IN_HBM, IN_SMEM, ANYWHERE],
        slots * slots,
        4 * slots * rank * degrees,
        [pltpu.VMEM((here, slots), F32), pltpu.SemaphoreType.DMA((early,))],
    )(root_basis, order_of_slot, after)


def root_kernel(group, first, last, *refs):
    refs = list(refs)
    so_far_ref = refs.pop(0) if last else None
    place_ref, alive_ref = refs.pop(0), refs.pop(0)
    count = place_ref.shape[0] - first if last else first
    first = first if last else 0
    root_refs = refs[:count]
    if last:
        root_refs = [refs[0].at[i] for i in range(count)]
    elif count > 2:
        root_refs = refs[:2] + [refs[2].at[i] for i in range(count - 2)]
    refs = refs[1:] if last else refs[3:]
    state_refs, refs = refs[:count], refs[count:]
    copies = []
    if last:
        out_ref, rows_ref, natural_ref, sems = refs
    else:
        root_hbm, out_ref, later_ref, rows_ref, sems = refs
        natural_ref = out_ref
        for i in range(later_ref.shape[0]):
            copies.append(fetch_roots(count + i, root_hbm, later_ref.at[i], sems.at[i]))
            copies[-1].start()
    fields, parts, degrees, slots = out_ref.shape
    columns = fields * parts
    rank = root_refs[0].shape[1]
    group_rows = group * columns
    here = place_ref.shape[1]
    steps = state_refs[0].shape[0] // group_rows
    shape = (group_rows, 2 * rank)
    row_pair = lax.broadcasted_iota(jnp.int32, shape, 0) // columns
    row_half = lax.broadcasted_iota(jnp.int32, shape, 1) // rank
    masks = [[(row_pair == pair) & (row_half == half) for pair in range(group)] for half in range(2)]
    empty = jnp.zeros(shape, BF16)
    for i, state_ref in enumerate(state_refs):
        for step in range(steps):
            state = state_ref[pl.ds(step * group_rows, group_rows)]
            left = jnp.concatenate(
                [jnp.concatenate([jnp.where(m, state, empty) for m in line], axis=1) for line in masks], axis=0
            )
            right = root_refs[i][pl.ds(step * group * 2, group * 2)].reshape(group * 2 * rank, degrees)
            product = contract(left, right, ((1,), (0,)))
            begin = (i * steps + step) * 2 * group_rows
            for tile in range(degrees // 128):
                rows_ref[tile, pl.ds(begin, 2 * group_rows), :] = product[:, tile * 128 : (tile + 1) * 128]
    place = place_ref[pl.ds(first, count)].reshape(count * here, slots)
    per = max(1, fields // 4)
    for column in range(columns):
        for tile in range(degrees // 128):
            span = slice(tile * 128, (tile + 1) * 128)
            one = rows_ref[tile, pl.ds(column, count * here, stride=columns), :].astype(BF16)
            natural = contract(one.T, place, ((1,), (0,))).astype(BF16)
            where = (column // 2, column % 2, span)
            if last:
                natural = natural + so_far_ref[where]
                natural = jnp.where(alive_ref[span] != 0, natural, jnp.zeros((), BF16))
            natural_ref[where] = natural
        if last and (column + 1) % (2 * per) == 0:
            done = column // (2 * per)
            where = pl.ds(done * per, per)
            copies.append(pltpu.make_async_copy(natural_ref.at[where], out_ref.at[where], sems.at[done]))
            copies[-1].start()
    for copy in copies:
        copy.wait()


def spectra_of(states, roots, places, alive, so_far, first, group):
    state_rows = states[0].shape[0]
    rank, degrees = roots[0].shape[-2:]
    owners, here, slots = places.shape
    count = len(states)
    columns = state_rows * 2 // here
    last = so_far is not None
    out = jax.ShapeDtypeStruct((columns // 2, 2, degrees, slots), BF16)
    root_basis = roots[-1]
    inputs = [places, alive, *(roots if so_far is not None else roots[:-1]), *states]
    in_specs = whole_blocks(len(inputs))
    scratch = [pltpu.VMEM((degrees // 128, count * here * columns, 128), F32)]
    more = {}
    if last:
        inputs = [so_far, *inputs]
        in_specs = whole_blocks(len(inputs))
        scratch += [pltpu.VMEM(out.shape, BF16), pltpu.SemaphoreType.DMA((columns // 2,))]
        more["out_specs"] = IN_HBM
    else:
        inputs.append(root_basis)
        in_specs.append(IN_HBM)
        out = [out, jax.ShapeDtypeStruct((owners - count, here, rank, degrees), BF16)]
        scratch.append(pltpu.SemaphoreType.DMA((owners - count,)))
    return call(
        functools.partial(root_kernel, group, first, last),
        "root",
        out,
        in_specs,
        2 * count * here * rank * degrees * columns,
        2 * count * here * rank * degrees,
        scratch,
        mib=24,
        **more,
    )(*inputs)


def per_device(
    fourier, quad_weights, leaf_basis, level_factors, sparsity, root_basis, order_of_slot
):
    slots, columns, lats = fourier.shape
    owners = lax.axis_size("order")
    levels = level_factors.shape[1]
    group = max(2, 16 * owners // columns)
    present = in_hbm(sparsity.transpose(1, 2, 0))
    fourier, leaf_basis, level_factors, root_basis = map(in_hbm, (fourier, leaf_basis, level_factors, root_basis))
    quad_weights = in_hbm(quad_weights.reshape(1, lats))

    def swap(array, axis, bits):
        return lax.ppermute(array, axis, [(i, i ^ bits) for i in range(lax.axis_size(axis))])

    def swap_both(array, order_bits, lat_bits):
        blocks = lax.axis_size("lat")
        pairs = [
            (o * blocks + b, (o ^ order_bits) * blocks + (b ^ lat_bits)) for o in range(owners) for b in range(blocks)
        ]
        return lax.ppermute(array, ("order", "lat"), pairs)

    state, root_0 = leaf_states(fourier, quad_weights, leaf_basis, root_basis, owners)
    partner = swap(state, "lat", 1)
    weights = level_weights(level_factors, present, (0,), state)
    states = [next_states(f"level0_{c}", state, partner, weights[0], c) for c in range(2)]
    weights += level_weights(level_factors, present, tuple(range(1, levels)), states[1], root_basis)
    own_factors, cross_factors, root_1 = weights[-3:]
    other_cross = swap(cross_factors, "order", 1)
    early_pieces = 3 * owners // 4
    high = owners // 2
    own_columns = columns // owners
    for level in range(1, levels - 1):
        partners = [swap(state, "lat", 1 << level) for state in states]
        parts = high if level == levels - 2 else 1
        states = [
            next_states(f"level{level}_{c}", states[c], partners[c], weights[level], None, parts if c else 1, own_factors)
            for c in range(2)
        ]
    top = 1 << levels - 1
    mine, (other, early, term) = states
    mine_partner = swap(mine, "lat", top)
    early_partner = swap_both(early, 1, top)
    other_own = swap(term, "order", 1)
    roots, places, alive = near_roots(root_basis, order_of_slot, owners, early_pieces - 2, group, other)
    late_partner = swap_both(late_columns(alive, other, own_columns), 1, top)
    even = last_states("last_own", alive, mine, mine_partner, (cross_factors, own_factors), high, True)
    begin = columns // 2 - own_columns
    odd = last_states("last_early", alive, other_own, early_partner, (other_cross,), high - 1, False)
    odd = [*last_states("last_late", alive, other_own, late_partner, (other_cross,), 1, False, begin), *odd]
    arrived = [swap((odd if k % 2 else even)[k // 2], "order", k // 2 * 2) if k > 1 else (even, odd)[k][0] for k in range(owners)]
    roots = [root_0, root_1, roots, root_basis]
    spectra, later_roots = spectra_of(arrived[:early_pieces], roots, places, alive, None, early_pieces, group)
    return spectra_of(arrived[early_pieces:], [later_roots], places, alive, spectra, early_pieces, group)


def solution(mesh):
    return jax.shard_map(
        per_device,
        mesh=mesh,
        in_specs=(
            P("order", None, "lat"),
            P("lat"),
            P("order", None, "lat"),
            P("order", None, None, "lat", None, None),
            P("order", None, "lat"),
            P(None, None, "lat"),
            P(),
        ),
        out_specs=P("order", None, "lat", None),
        check_vma=False,
    )
```

profile of v0, /device:TPU:0, one launch (start us, length us, event | category | flops | bytes accessed | tf_op | source)
XLA Modules:
  0.0 31.3 jit_solution(12625139665523824922)
XLA Ops:
  0.0 1.9 %leaf.1 = (bf16[16,2,32,128]{3,2,1,0:T(8,128)(2,1)S(1)}, bf16[32,64,256]{2,1,0:T(8,128)(2,1)S(1)}) custom-call(bf16[32,64,256]{2,1,0:T(8,128)(2,1)} %fourier_hbm.1, f32[1,256]{1,0:T(1,128)} %bitcast.4, bf16[32,64,256]{2,1,0:T(8,128)(2,1)} %leaf_hbm.1, bf16[128,64,256]{2,1,0:T(8,128)(2,1)} %refs_8_.1), custom_call_target="tpu_custom_call" | custom-call | flops 67108 | bytes 2097 | tf_op jit(solution)/shard_map/leaf/pallas_call | solution.py:92
  1.9 0.5 %collective-permute-start = (bf16[16,2,32,128]{3,2,1,0:T(8,128)(2,1)S(1)}, bf16[16,2,32,128]{3,2,1,0:T(8,128)(2,1)S(1)}, u32[]{:S(2)}, u32[]{:S(2)}) collective-permute-start(bf16[16,2,32,128]{3,2,1,0:T(8,128)(2,1)S(1)} %get-tuple-element.21.after.state_ref), channel_id=1, source_target_pairs={{0,1},{1,0},{2,3},{3,2},{4,5},{5,4},{6,7},{7,6},{8,9},{9,8},{10,11... | collective-permute-start | bytes 786440 | tf_op jit(solution)/shard_map/ppermute | solution.py:485
  2.5 1.4 %factors.2.weight_ref = bf16[16,128,256]{2,1,0:T(8,128)(2,1)S(1)} custom-call(bf16[32,3,2,1,64,64]{5,4,3,2,1,0:T(8,128)(2,1)} %factor_hbm.3, s32[3,1,32]{2,1,0:T(1,128)} %bitcast.2, bf16[16,2,32,128]{3,2,1,0:T(8,128)(2,1)S(1)} %get-tuple-element.21.after.state_ref), custom_call_target="tpu_custom_call" | custom-call | flops 524 | bytes 2097 | tf_op jit(solution)/shard_map/factors/pallas_call | solution.py:165
  3.9 0.0 collective-permute-done.partner_ref
  3.9 0.4 %level0_0.1.state_ref = bf16[16,32,128]{2,1,0:T(8,128)(2,1)S(1)} custom-call(bf16[16,2,32,128]{3,2,1,0:T(8,128)(2,1)S(1)} %get-tuple-element.21.after.state_ref, bf16[16,2,32,128]{3,2,1,0:T(8,128)(2,1)S(1)} %collective-permute-done.partner_ref, bf16[16,128,256]{2,1,0:T(8,128)(2,1)S(1)} %factors.2.weight_ref), custom_call_target="tpu_custom_call" | custom-call | flops 33554 | bytes 393 | tf_op jit(solution)/shard_map/level0_0/pallas_call | solution.py:216
  4.4 2.7 %collective-permute-start.2 = (bf16[16,32,128]{2,1,0:T(8,128)(2,1)S(1)}, bf16[16,32,128]{2,1,0:T(8,128)(2,1)S(1)}, u32[]{:S(2)}, u32[]{:S(2)}) collective-permute-start(bf16[16,32,128]{2,1,0:T(8,128)(2,1)S(1)} %level0_0.1.state_ref), channel_id=1, source_target_pairs={{0,2},{1,3},{2,0},{3,1},{4,6},{5,7},{6,4},{7,5},{8,10},{9,11},{10,... | collective-permute-start | bytes 393224 | tf_op jit(solution)/shard_map/ppermute | solution.py:485
  7.0 0.4 %level0_1.1.after.state_ref = bf16[16,32,128]{2,1,0:T(8,128)(2,1)S(1)} custom-call(bf16[16,2,32,128]{3,2,1,0:T(8,128)(2,1)S(1)} %get-tuple-element.21.after.state_ref, bf16[16,2,32,128]{3,2,1,0:T(8,128)(2,1)S(1)} %collective-permute-done.partner_ref, bf16[16,128,256]{2,1,0:T(8,128)(2,1)S(1)} %factors.2.weight_ref), custom_call_target="tpu_custom_call" | custom-call | flops 33554 | bytes 393 | tf_op jit(solution)/shard_map/level0_1/pallas_call | solution.py:216
  7.5 0.0 copy-start
  7.5 0.1 collective-permute-start.1
  7.6 1.9 %factors.3 = (bf16[16,128,256]{2,1,0:T(8,128)(2,1)S(1)}, bf16[16,64,128]{2,1,0:T(8,128)(2,1)S(1)}, bf16[16,64,128]{2,1,0:T(8,128)(2,1)S(1)}, bf16[32,64,256]{2,1,0:T(8,128)(2,1)S(1)}) custom-call(bf16[32,3,2,1,64,64]{5,4,3,2,1,0:T(8,128)(2,1)} %factor_hbm.3, s32[3,1,32]{2,1,0:T(1,128)} %bitcast.3, bf16[16,32,128]{2,1,0:T(8,128)(2,1)S(1)} %level0_1.1.after.state_ref, ...), custom_call_target="tpu_custom_call" | custom-call | flops 1048 | bytes 4194 | tf_op jit(solution)/shard_map/factors/pallas_call | solution.py:165
  9.5 2.0 %collective-permute-start.6 = (bf16[16,64,128]{2,1,0:T(8,128)(2,1)S(1)}, bf16[16,64,128]{2,1,0:T(8,128)(2,1)S(1)}, u32[]{:S(2)}, u32[]{:S(2)}) collective-permute-start(bf16[16,64,128]{2,1,0:T(8,128)(2,1)S(1)} %get-tuple-element.30.cross_ref), channel_id=1, source_target_pairs={{0,8},{8,0},{16,24},{24,16},{1,9},{9,1},{17,25},{25,17},{2,10},{10... | collective-permute-start | bytes 786440 | tf_op jit(solution)/shard_map/ppermute | solution.py:485
  11.5 0.0 collective-permute-done.2.partner_ref
  11.5 0.4 %level1_0.1.own_ref = bf16[16,32,128]{2,1,0:T(8,128)(2,1)S(1)} custom-call(bf16[16,32,128]{2,1,0:T(8,128)(2,1)S(1)} %level0_0.1.state_ref, bf16[16,32,128]{2,1,0:T(8,128)(2,1)S(1)} %collective-permute-done.2.partner_ref, bf16[16,128,256]{2,1,0:T(8,128)(2,1)S(1)} %get-tuple-element.22.weight_ref), custom_call_target="tpu_custom_call" | custom-call | flops 33554 | bytes 393 | tf_op jit(solution)/shard_map/level1_0/pallas_call | solution.py:216
  11.9 2.9 %collective-permute-start.3 = (bf16[16,32,128]{2,1,0:T(8,128)(2,1)S(1)}, bf16[16,32,128]{2,1,0:T(8,128)(2,1)S(1)}, u32[]{:S(2)}, u32[]{:S(2)}) collective-permute-start(bf16[16,32,128]{2,1,0:T(8,128)(2,1)S(1)} %level1_0.1.own_ref), channel_id=1, source_target_pairs={{0,4},{1,5},{2,6},{3,7},{4,0},{5,1},{6,2},{7,3},{8,12},{9,13},{10,... | collective-permute-start | bytes 393224 | tf_op jit(solution)/shard_map/ppermute | solution.py:485
  14.9 0.0 collective-permute-done.1.partner_ref
  14.9 0.8 %level1_1.1 = (bf16[16,32,128]{2,1,0:T(8,128)(2,1)S(1)}, bf16[16,16,128]{2,1,0:T(8,128)(2,1)S(1)}, bf16[16,32,128]{2,1,0:T(8,128)(2,1)S(1)}) custom-call(bf16[16,32,128]{2,1,0:T(8,128)(2,1)S(1)} %level0_1.1.after.state_ref, bf16[16,32,128]{2,1,0:T(8,128)(2,1)S(1)} %collective-permute-done.1.partner_ref, ...), custom_call_target="tpu_custom_call" | custom-call | flops 33554 | bytes 393 | tf_op jit(solution)/shard_map/level1_1/pallas_call | solution.py:216
  15.7 1.5 %collective-permute-start.4 = (bf16[16,32,128]{2,1,0:T(8,128)(2,1)S(1)}, bf16[16,32,128]{2,1,0:T(8,128)(2,1)S(1)}, u32[]{:S(2)}, u32[]{:S(2)}) collective-permute-start(bf16[16,32,128]{2,1,0:T(8,128)(2,1)S(1)} %get-tuple-element.32), channel_id=1, source_target_pairs={{0,8},{8,0},{16,24},{24,16},{1,9},{9,1},{17,25},{25,17},{2,10},{10... | collective-permute-start | bytes 393224 | tf_op jit(solution)/shard_map/ppermute | solution.py:485
  17.2 1.8 %collective-permute-start.8 = (bf16[16,16,128]{2,1,0:T(8,128)(2,1)S(1)}, bf16[16,16,128]{2,1,0:T(8,128)(2,1)S(1)}, u32[]{:S(2)}, u32[]{:S(2)}) collective-permute-start(bf16[16,16,128]{2,1,0:T(8,128)(2,1)S(1)} %get-tuple-element.36), channel_id=1, source_target_pairs={{0,12},{1,13},{2,14},{3,15},{4,8},{5,9},{6,10},{7,11},{8,4},{9,5},... | collective-permute-start | bytes 196616 | tf_op jit(solution)/shard_map/ppermute | solution.py:492
  19.0 0.0 copy-done
  19.0 1.8 %near_roots.1 = (bf16[1,32,64,256]{3,2,1,0:T(8,128)(2,1)S(1)}, bf16[4,32,128]{2,1,0:T(8,128)(2,1)S(1)}, bf16[256,128]{1,0:T(8,128)(2,1)S(1)}) custom-call(bf16[128,64,256]{2,1,0:T(8,128)(2,1)} %refs_8_.1, s32[128]{0:T(128)S(1)} %copy-done, bf16[16,32,128]{2,1,0:T(8,128)(2,1)S(1)} %get-tuple-element.24.after.state_ref), custom_call_target="tpu_custom_call" | custom-call | flops 16 | bytes 8388 | tf_op jit(solution)/shard_map/near_roots/pallas_call | solution.py:357
  20.8 2.1 %collective-permute-start.5 = (bf16[16,16,128]{2,1,0:T(8,128)(2,1)S(1)}, bf16[16,16,128]{2,1,0:T(8,128)(2,1)S(1)}, u32[]{:S(2)}, u32[]{:S(2)}) collective-permute-start(bf16[16,16,128]{2,1,0:T(8,128)(2,1)S(1)} %late_columns.1), channel_id=1, source_target_pairs={{0,12},{1,13},{2,14},{3,15},{4,8},{5,9},{6,10},{7,11},{8,4},{9,5},... | collective-permute-start | bytes 196616 | tf_op jit(solution)/shard_map/ppermute | solution.py:492
  22.9 0.0 collective-permute-done.3.partner_ref
  22.9 0.5 %last_own.1 = (bf16[256,128]{1,0:T(8,128)(2,1)S(1)}, bf16[256,128]{1,0:T(8,128)(2,1)S(1)}) custom-call(bf16[256,128]{1,0:T(8,128)(2,1)S(1)} %get-tuple-element.26.after.refs_1_.refs_2_, bf16[16,32,128]{2,1,0:T(8,128)(2,1)S(1)} %level1_0.1.own_ref, bf16[16,32,128]{2,1,0:T(8,128)(2,1)S(1)} %collective-permute-done.3.partner_ref, ...), custom_call_target="tpu_custom_call" | custom-call | flops 33554 | bytes 393 | tf_op jit(solution)/shard_map/last_own/pallas_call | solution.py:314
  23.4 1.6 %collective-permute-start.7 = (bf16[256,128]{1,0:T(8,128)(2,1)S(1)}, bf16[256,128]{1,0:T(8,128)(2,1)S(1)}, u32[]{:S(2)}, u32[]{:S(2)}) collective-permute-start(bf16[256,128]{1,0:T(8,128)(2,1)S(1)} %get-tuple-element.33), channel_id=1, source_target_pairs={{0,16},{8,24},{16,0},{24,8},{1,17},{9,25},{17,1},{25,9},{2,18},{10... | collective-permute-start | bytes 196616 | tf_op jit(solution)/shard_map/ppermute | solution.py:485
  24.9 0.0 collective-permute-done.8.partner_ref
  24.9 0.0 collective-permute-done.4.own_ref
  25.0 0.0 collective-permute-done.6.cross_ref
  25.0 0.4 %last_early.1 = bf16[256,128]{1,0:T(8,128)(2,1)S(1)} custom-call(bf16[256,128]{1,0:T(8,128)(2,1)S(1)} %get-tuple-element.26.after.refs_1_.refs_2_, bf16[16,32,128]{2,1,0:T(8,128)(2,1)S(1)} %collective-permute-done.4.own_ref, bf16[16,16,128]{2,1,0:T(8,128)(2,1)S(1)} %collective-permute-done.8.partner_ref, ...), custom_call_target="tpu_custom_call" | custom-call | flops 16777 | bytes 196 | tf_op jit(solution)/shard_map/last_early/pallas_call | solution.py:314
  25.3 0.5 %collective-permute-start.9 = (bf16[256,128]{1,0:T(8,128)(2,1)S(1)}, bf16[256,128]{1,0:T(8,128)(2,1)S(1)}, u32[]{:S(2)}, u32[]{:S(2)}) collective-permute-start(bf16[256,128]{1,0:T(8,128)(2,1)S(1)} %last_early.1), channel_id=1, source_target_pairs={{0,16},{8,24},{16,0},{24,8},{1,17},{9,25},{17,1},{25,9},{2,18},{10... | collective-permute-start | bytes 196616 | tf_op jit(solution)/shard_map/ppermute | solution.py:485
  25.9 1.1 %collective-permute-done.5.partner_ref = bf16[16,16,128]{2,1,0:T(8,128)(2,1)S(1)} collective-permute-done((bf16[16,16,128]{2,1,0:T(8,128)(2,1)S(1)}, bf16[16,16,128]{2,1,0:T(8,128)(2,1)S(1)}, u32[]{:S(2)}, u32[]{:S(2)}) %collective-permute-start.5) | collective-permute-done | bytes 65568 | tf_op jit(solution)/shard_map/ppermute | solution.py:492
  27.0 0.4 %last_late.1.refs_6_ = bf16[256,128]{1,0:T(8,128)(2,1)S(1)} custom-call(bf16[256,128]{1,0:T(8,128)(2,1)S(1)} %get-tuple-element.26.after.refs_1_.refs_2_, bf16[16,32,128]{2,1,0:T(8,128)(2,1)S(1)} %collective-permute-done.4.own_ref, bf16[16,16,128]{2,1,0:T(8,128)(2,1)S(1)} %collective-permute-done.5.partner_ref, ...), custom_call_target="tpu_custom_call" | custom-call | flops 16777 | bytes 196 | tf_op jit(solution)/shard_map/last_late/pallas_call | solution.py:314
  27.3 0.4 %collective-permute-done.7.refs_7_ = bf16[256,128]{1,0:T(8,128)(2,1)S(1)} collective-permute-done((bf16[256,128]{1,0:T(8,128)(2,1)S(1)}, bf16[256,128]{1,0:T(8,128)(2,1)S(1)}, u32[]{:S(2)}, u32[]{:S(2)}) %collective-permute-start.7) | collective-permute-done | bytes 65568 | tf_op jit(solution)/shard_map/ppermute | solution.py:485
  27.7 1.8 %root.2 = (bf16[8,2,256,128]{3,2,1,0:T(8,128)(2,1)S(1)}, bf16[1,32,64,256]{3,2,1,0:T(8,128)(2,1)S(1)}) custom-call(bf16[4,32,128]{2,1,0:T(8,128)(2,1)S(1)} %get-tuple-element.25.refs_0_.refs_1_, bf16[256,128]{1,0:T(8,128)(2,1)S(1)} %get-tuple-element.26.after.refs_1_.refs_2_, bf16[32,64,256]{2,1,0:T(8,128)(2,1)S(1)} %get-tuple-element.27.refs_2_, ...), custom_call_target="tpu_custom_call" | custom-call | flops 50331 | bytes 3145 | tf_op jit(solution)/shard_map/root/pallas_call | solution.py:460
  29.5 0.2 collective-permute-done.9.refs_4_
  29.6 1.6 %root.3 = bf16[8,2,256,128]{3,2,1,0:T(8,128)(2,1)} custom-call(bf16[8,2,256,128]{3,2,1,0:T(8,128)(2,1)S(1)} %get-tuple-element.34.refs_0_, bf16[4,32,128]{2,1,0:T(8,128)(2,1)S(1)} %get-tuple-element.25.refs_0_.refs_1_, bf16[256,128]{1,0:T(8,128)(2,1)S(1)} %get-tuple-element.26.after.refs_1_.refs_2_, bf16[1,32,64,256]{3,2,1,0:T(8,128)(2,1)S(1)} %get-tuple-element.35.refs_3_, ...), custom_call_target="tpu_custom_call" | custom-call | flops 16777 | bytes 1048 | tf_op jit(solution)/shard_map/root/pallas_call | solution.py:460
  (1 shorter events, 0.0 us)
Async XLA Ops:
  1.9 2.0 %collective-permute-start = (bf16[16,2,32,128]{3,2,1,0:T(8,128)(2,1)S(1)}, bf16[16,2,32,128]{3,2,1,0:T(8,128)(2,1)S(1)}, u32[]{:S(2)}, u32[]{:S(2)}) collective-permute-start(bf16[16,2,32,128]{3,2,1,0:T(8,128)(2,1)S(1)} %get-tuple-element.21.after.state_ref), channel_id=1, source_target_pairs={{0,1},{1,0},{2,3},{3,2},{4,5},{5,4},{6,7},{7,6},{8,9},{9,8},{10,11... | collective-permute-start | bytes 786440 | tf_op jit(solution)/shard_map/ppermute | solution.py:485
  4.4 7.2 %collective-permute-start.2 = (bf16[16,32,128]{2,1,0:T(8,128)(2,1)S(1)}, bf16[16,32,128]{2,1,0:T(8,128)(2,1)S(1)}, u32[]{:S(2)}, u32[]{:S(2)}) collective-permute-start(bf16[16,32,128]{2,1,0:T(8,128)(2,1)S(1)} %level0_0.1.state_ref), channel_id=1, source_target_pairs={{0,2},{1,3},{2,0},{3,1},{4,6},{5,7},{6,4},{7,5},{8,10},{9,11},{10,... | collective-permute-start | bytes 393224 | tf_op jit(solution)/shard_map/ppermute | solution.py:485
  7.5 11.5 %copy-start = (s32[128]{0:T(128)S(1)}, s32[128]{0:T(128)}, u32[]{:S(2)}) copy-start(s32[128]{0:T(128)} %order_ref.1) | copy-start | bytes 1540
  7.5 7.3 %collective-permute-start.1 = (bf16[16,32,128]{2,1,0:T(8,128)(2,1)S(1)}, bf16[16,32,128]{2,1,0:T(8,128)(2,1)S(1)}, u32[]{:S(2)}, u32[]{:S(2)}) collective-permute-start(bf16[16,32,128]{2,1,0:T(8,128)(2,1)S(1)} %level0_1.1.after.state_ref), channel_id=1, source_target_pairs={{0,2},{1,3},{2,0},{3,1},{4,6},{5,7},{6,4},{7,5},{8,10},{9,11},{10,... | collective-permute-start | bytes 393224 | tf_op jit(solution)/shard_map/ppermute | solution.py:485
  9.5 15.4 %collective-permute-start.6 = (bf16[16,64,128]{2,1,0:T(8,128)(2,1)S(1)}, bf16[16,64,128]{2,1,0:T(8,128)(2,1)S(1)}, u32[]{:S(2)}, u32[]{:S(2)}) collective-permute-start(bf16[16,64,128]{2,1,0:T(8,128)(2,1)S(1)} %get-tuple-element.30.cross_ref), channel_id=1, source_target_pairs={{0,8},{8,0},{16,24},{24,16},{1,9},{9,1},{17,25},{25,17},{2,10},{10... | collective-permute-start | bytes 786440 | tf_op jit(solution)/shard_map/ppermute | solution.py:485
  11.9 10.9 %collective-permute-start.3 = (bf16[16,32,128]{2,1,0:T(8,128)(2,1)S(1)}, bf16[16,32,128]{2,1,0:T(8,128)(2,1)S(1)}, u32[]{:S(2)}, u32[]{:S(2)}) collective-permute-start(bf16[16,32,128]{2,1,0:T(8,128)(2,1)S(1)} %level1_0.1.own_ref), channel_id=1, source_target_pairs={{0,4},{1,5},{2,6},{3,7},{4,0},{5,1},{6,2},{7,3},{8,12},{9,13},{10,... | collective-permute-start | bytes 393224 | tf_op jit(solution)/shard_map/ppermute | solution.py:485
  15.7 9.3 %collective-permute-start.4 = (bf16[16,32,128]{2,1,0:T(8,128)(2,1)S(1)}, bf16[16,32,128]{2,1,0:T(8,128)(2,1)S(1)}, u32[]{:S(2)}, u32[]{:S(2)}) collective-permute-start(bf16[16,32,128]{2,1,0:T(8,128)(2,1)S(1)} %get-tuple-element.32), channel_id=1, source_target_pairs={{0,8},{8,0},{16,24},{24,16},{1,9},{9,1},{17,25},{25,17},{2,10},{10... | collective-permute-start | bytes 393224 | tf_op jit(solution)/shard_map/ppermute | solution.py:485
  17.2 7.8 %collective-permute-start.8 = (bf16[16,16,128]{2,1,0:T(8,128)(2,1)S(1)}, bf16[16,16,128]{2,1,0:T(8,128)(2,1)S(1)}, u32[]{:S(2)}, u32[]{:S(2)}) collective-permute-start(bf16[16,16,128]{2,1,0:T(8,128)(2,1)S(1)} %get-tuple-element.36), channel_id=1, source_target_pairs={{0,12},{1,13},{2,14},{3,15},{4,8},{5,9},{6,10},{7,11},{8,4},{9,5},... | collective-permute-start | bytes 196616 | tf_op jit(solution)/shard_map/ppermute | solution.py:492
  20.8 6.1 %collective-permute-start.5 = (bf16[16,16,128]{2,1,0:T(8,128)(2,1)S(1)}, bf16[16,16,128]{2,1,0:T(8,128)(2,1)S(1)}, u32[]{:S(2)}, u32[]{:S(2)}) collective-permute-start(bf16[16,16,128]{2,1,0:T(8,128)(2,1)S(1)} %late_columns.1), channel_id=1, source_target_pairs={{0,12},{1,13},{2,14},{3,15},{4,8},{5,9},{6,10},{7,11},{8,4},{9,5},... | collective-permute-start | bytes 196616 | tf_op jit(solution)/shard_map/ppermute | solution.py:492
  23.4 4.3 %collective-permute-start.7 = (bf16[256,128]{1,0:T(8,128)(2,1)S(1)}, bf16[256,128]{1,0:T(8,128)(2,1)S(1)}, u32[]{:S(2)}, u32[]{:S(2)}) collective-permute-start(bf16[256,128]{1,0:T(8,128)(2,1)S(1)} %get-tuple-element.33), channel_id=1, source_target_pairs={{0,16},{8,24},{16,0},{24,8},{1,17},{9,25},{17,1},{25,9},{2,18},{10... | collective-permute-start | bytes 196616 | tf_op jit(solution)/shard_map/ppermute | solution.py:485
  25.3 4.3 %collective-permute-start.9 = (bf16[256,128]{1,0:T(8,128)(2,1)S(1)}, bf16[256,128]{1,0:T(8,128)(2,1)S(1)}, u32[]{:S(2)}, u32[]{:S(2)}) collective-permute-start(bf16[256,128]{1,0:T(8,128)(2,1)S(1)} %last_early.1), channel_id=1, source_target_pairs={{0,16},{8,24},{16,0},{24,8},{1,17},{9,25},{17,1},{25,9},{2,18},{10... | collective-permute-start | bytes 196616 | tf_op jit(solution)/shard_map/ppermute | solution.py:485
where the time goes:
time: 31.5 us; the launch traced here: 31.3 us
  starting transfers between devices  15.7 us (50%)
  Pallas kernels  13.9 us (44%)
  waiting for transfers between devices  1.6 us (5%)
    ppermute x8, starting transfers between devices, swap(): lax.ppermute(array, axis, [(i, i ^ bits) for i in range(lax.axis_size(axi...  11.8 us
    ppermute x2, starting transfers between devices, swap_both(): return lax.ppermute(array, ('order', 'lat'), pairs)  3.89 us
    pallas_call x2, Pallas kernels, spectra_of(): call(functools.partial(root_kernel, group, first, last), 'root', out, in_...  3.4 us
    pallas_call x2, Pallas kernels, level_weights(): call(functools.partial(factor_kernel, levels, pieces, root_basis is not N...  3.36 us
    pallas_call x4, Pallas kernels, next_states(): call(functools.partial(level_kernel, side, 'order'), name, [jax.ShapeDtyp...  2.14 us
    pallas_call x1, Pallas kernels, leaf_states(): call(functools.partial(leaf_kernel, pieces, group), 'leaf', [jax.ShapeDty...  1.92 us
    pallas_call x1, Pallas kernels, near_roots(): call(functools.partial(near_kernel, group), 'near_roots', [jax.ShapeDtype...  1.78 us
    pallas_call x3, Pallas kernels, last_states(): call(functools.partial(last_level_kernel, turn, begin, 'order'), name, [j...  1.23 us
  transfers between devices with their start and end apart: 10, of which 3 were waited for; matrix products, arithmetic and copies ran while one was open for 0% of the time, Pallas kernels for 32%

commit v1 on v0

--- a/solution.py
+++ b/solution.py
@@ -120,7 +120,8 @@
     fetches = []
     if roots:
         root_hbm, root_ref = weight_refs.pop(0), weight_refs.pop()
-        fetches.append(fetch_roots(1, root_hbm, root_ref, sems.at[len(levels) * pieces + 1]))
+        for i in range(root_ref.shape[0]):
+            fetches.append(fetch_roots(1 + i, root_hbm, root_ref.at[i], sems.at[len(levels) * pieces + 1 + i]))
     present_copy = pltpu.make_async_copy(present_hbm, present_ref, sems.at[len(levels) * pieces])
     present_copy.start()
     _, slots, _, rank, _ = factor_ref.shape
@@ -156,14 +157,15 @@
         fetch.wait()
 
 
-def level_weights(level_factors, present, levels, after, root_basis=None):
+def level_weights(level_factors, present, levels, after, root_basis=None, root_pieces=0):
     slots, last, _, _, rank, _ = level_factors.shape
     count, pieces = len(levels), 2
     roots = []
-    if root_basis is not None:
-        roots = [jax.ShapeDtypeStruct((root_basis.shape[0] // lax.axis_size("order"), *root_basis.shape[1:]), BF16)]
+    if root_pieces:
+        here = root_basis.shape[0] // lax.axis_size("order")
+        roots = [jax.ShapeDtypeStruct((root_pieces, here, *root_basis.shape[1:]), BF16)]
     return call(
-        functools.partial(factor_kernel, levels, pieces, root_basis is not None),
+        functools.partial(factor_kernel, levels, pieces, root_pieces),
         "factors",
         [
             jax.ShapeDtypeStruct((slots // 2, *((rank, 2 * rank) if level == last - 1 else (2 * rank, 4 * rank))), BF16)
@@ -177,7 +179,7 @@
         [
             pltpu.VMEM((count, slots, 2, rank, rank), BF16),
             pltpu.SMEM(present.shape, jnp.int32),
-            pltpu.SemaphoreType.DMA((count * pieces + 1 + len(roots),)),
+            pltpu.SemaphoreType.DMA((count * pieces + 1 + root_pieces,)),
         ],
         mib=24,
     )(level_factors, present, after, *([root_basis] if roots else []))
@@ -327,16 +329,11 @@
     return [part.reshape(rows, lanes) for part in parts]
 
 
-def near_kernel(group, root_hbm, order_ref, after, root_ref, place_ref, alive_ref, rows_ref, sems):
+def place_kernel(group, order_ref, after, place_ref, alive_ref, rows_ref):
     del after
-    early = root_ref.shape[0]
     owners, here, slots = place_ref.shape
     degrees = alive_ref.shape[0]
     me = lax.axis_index("order")
-    copies = []
-    for k in range(early):
-        copies.append(fetch_roots(2 + k, root_hbm, root_ref.at[k], sems.at[k]))
-        copies[-1].start()
     lane = lax.broadcasted_iota(jnp.int32, (1, slots), 1)
     for k in range(owners):
         for slot in range(here):
@@ -347,26 +344,20 @@
     degree = lax.axis_index("lat") * degrees + lax.broadcasted_iota(jnp.int32, (degrees, slots), 0)
     window = DEGREES // slots * lax.broadcasted_iota(jnp.int32, (degrees, slots), 1)
     alive_ref[...] = (degree >= window).astype(F32).astype(BF16)
-    for copy in copies:
-        copy.wait()
-
-
-def near_roots(root_basis, order_of_slot, owners, early, group, after):
-    slots, rank, degrees = root_basis.shape
+
+
+def places_of(order_of_slot, degrees, owners, group, after):
+    slots = order_of_slot.shape[0]
     here = slots // owners
     return call(
-        functools.partial(near_kernel, group),
-        "near_roots",
-        [
-            jax.ShapeDtypeStruct((early, here, rank, degrees), BF16),
-            jax.ShapeDtypeStruct((owners, here, slots), BF16),
-            jax.ShapeDtypeStruct((degrees, slots), BF16),
-        ],
-        [IN_HBM, IN_SMEM, ANYWHERE],
+        functools.partial(place_kernel, group),
+        "places",
+        [jax.ShapeDtypeStruct((owners, here, slots), BF16), jax.ShapeDtypeStruct((degrees, slots), BF16)],
+        [IN_SMEM, ANYWHERE],
         slots * slots,
-        4 * slots * rank * degrees,
-        [pltpu.VMEM((here, slots), F32), pltpu.SemaphoreType.DMA((early,))],
-    )(root_basis, order_of_slot, after)
+        8 * slots * slots,
+        [pltpu.VMEM((here, slots), F32)],
+    )(order_of_slot, after)
 
 
 def root_kernel(group, first, last, *refs):
@@ -375,12 +366,11 @@
     place_ref, alive_ref = refs.pop(0), refs.pop(0)
     count = place_ref.shape[0] - first if last else first
     first = first if last else 0
-    root_refs = refs[:count]
     if last:
         root_refs = [refs[0].at[i] for i in range(count)]
-    elif count > 2:
-        root_refs = refs[:2] + [refs[2].at[i] for i in range(count - 2)]
-    refs = refs[1:] if last else refs[3:]
+    else:
+        root_refs = refs[:1] + [refs[1].at[i] for i in range(count - 1)]
+    refs = refs[1:] if last else refs[2:]
     state_refs, refs = refs[:count], refs[count:]
     copies = []
     if last:
@@ -491,14 +481,14 @@
         ]
         return lax.ppermute(array, ("order", "lat"), pairs)
 
+    early_pieces = 3 * owners // 4
     state, root_0 = leaf_states(fourier, quad_weights, leaf_basis, root_basis, owners)
     partner = swap(state, "lat", 1)
     weights = level_weights(level_factors, present, (0,), state)
     states = [next_states(f"level0_{c}", state, partner, weights[0], c) for c in range(2)]
-    weights += level_weights(level_factors, present, tuple(range(1, levels)), states[1], root_basis)
-    own_factors, cross_factors, root_1 = weights[-3:]
+    weights += level_weights(level_factors, present, tuple(range(1, levels)), states[1], root_basis, early_pieces - 1)
+    own_factors, cross_factors, early_roots = weights[-3:]
     other_cross = swap(cross_factors, "order", 1)
-    early_pieces = 3 * owners // 4
     high = owners // 2
     own_columns = columns // owners
     for level in range(1, levels - 1):
@@ -513,14 +503,14 @@
     mine_partner = swap(mine, "lat", top)
     early_partner = swap_both(early, 1, top)
     other_own = swap(term, "order", 1)
-    roots, places, alive = near_roots(root_basis, order_of_slot, owners, early_pieces - 2, group, other)
+    places, alive = places_of(order_of_slot, root_basis.shape[2], owners, group, other)
     late_partner = swap_both(late_columns(alive, other, own_columns), 1, top)
     even = last_states("last_own", alive, mine, mine_partner, (cross_factors, own_factors), high, True)
     begin = columns // 2 - own_columns
     odd = last_states("last_early", alive, other_own, early_partner, (other_cross,), high - 1, False)
     odd = [*last_states("last_late", alive, other_own, late_partner, (other_cross,), 1, False, begin), *odd]
     arrived = [swap((odd if k % 2 else even)[k // 2], "order", k // 2 * 2) if k > 1 else (even, odd)[k][0] for k in range(owners)]
-    roots = [root_0, root_1, roots, root_basis]
+    roots = [root_0, early_roots, root_basis]
     spectra, later_roots = spectra_of(arrived[:early_pieces], roots, places, alive, None, early_pieces, group)
     return spectra_of(arrived[early_pieces:], [later_roots], places, alive, spectra, early_pieces, group)
 

time: 31.5 us -> 31.8 us (level)
  Pallas kernels: 13.9 us -> 13.1 us
  starting transfers between devices: 15.7 us -> 16.4 us
  waiting for transfers between devices: 1.6 us -> 2.02 us
    pallas_call x3, Pallas kernels: 5.15 us -> 4.36 us  [the longest x2 3.69 us: level_weights(): call(functools.partial(factor_kernel, levels, pieces, root_pieces), 'fact...]
    ppermute x8, starting transfers between devices: 11.8 us -> 12.5 us  [swap(): lax.ppermute(array, axis, [(i, i ^ bits) for i in range(lax.axis_size(axi...]
    ppermute x8, waiting for transfers between devices: 0.53 us -> 1.23 us  [swap(): lax.ppermute(array, axis, [(i, i ^ bits) for i in range(lax.axis_size(axi...]
  transfers between devices with their start and end apart: 10 -> 10, of which waited for: 3 -> 3; matrix products, arithmetic and copies ran while one was open for 0% -> 0% of each run, Pallas kernels for 32% -> 29%
where the time goes in v1:
time: 31.8 us; the launch traced here: 31.6 us
  starting transfers between devices  16.4 us (52%)
  Pallas kernels  13.1 us (41%)
  waiting for transfers between devices  2.02 us (6%)
    ppermute x8, starting transfers between devices, swap(): lax.ppermute(array, axis, [(i, i ^ bits) for i in range(lax.axis_size(axi...  12.5 us
    ppermute x2, starting transfers between devices, swap_both(): return lax.ppermute(array, ('order', 'lat'), pairs)  3.89 us
    pallas_call x2, Pallas kernels, level_weights(): call(functools.partial(factor_kernel, levels, pieces, root_pieces), 'fact...  3.69 us
    pallas_call x2, Pallas kernels, spectra_of(): call(functools.partial(root_kernel, group, first, last), 'root', out, in_...  3.43 us
    pallas_call x4, Pallas kernels, next_states(): call(functools.partial(level_kernel, side, 'order'), name, [jax.ShapeDtyp...  2.14 us
    pallas_call x1, Pallas kernels, leaf_states(): call(functools.partial(leaf_kernel, pieces, group), 'leaf', [jax.ShapeDty...  1.92 us
    pallas_call x3, Pallas kernels, last_states(): call(functools.partial(last_level_kernel, turn, begin, 'order'), name, [j...  1.23 us
    ppermute x8, waiting for transfers between devices, swap(): lax.ppermute(array, axis, [(i, i ^ bits) for i in range(lax.axis_size(axi...  1.23 us
  transfers between devices with their start and end apart: 10, of which 3 were waited for; matrix products, arithmetic and copies ran while one was open for 0% of the time, Pallas kernels for 29%

profile of v1, /device:TPU:0, one launch (start us, length us, event | category | flops | bytes accessed | tf_op | source)
XLA Modules:
  0.0 31.6 jit_solution(14183661693565782070)
XLA Ops:
  0.0 1.9 %leaf.1 = (bf16[16,2,32,128]{3,2,1,0:T(8,128)(2,1)S(1)}, bf16[32,64,256]{2,1,0:T(8,128)(2,1)S(1)}) custom-call(bf16[32,64,256]{2,1,0:T(8,128)(2,1)} %fourier_hbm.1, f32[1,256]{1,0:T(1,128)} %bitcast.4, bf16[32,64,256]{2,1,0:T(8,128)(2,1)} %leaf_hbm.1, bf16[128,64,256]{2,1,0:T(8,128)(2,1)} %refs_7_.1), custom_call_target="tpu_custom_call" | custom-call | flops 67108 | bytes 2097 | tf_op jit(solution)/shard_map/leaf/pallas_call | solution.py:92
  1.9 0.5 %collective-permute-start = (bf16[16,2,32,128]{3,2,1,0:T(8,128)(2,1)S(1)}, bf16[16,2,32,128]{3,2,1,0:T(8,128)(2,1)S(1)}, u32[]{:S(2)}, u32[]{:S(2)}) collective-permute-start(bf16[16,2,32,128]{3,2,1,0:T(8,128)(2,1)S(1)} %get-tuple-element.20.after.state_ref), channel_id=1, source_target_pairs={{0,1},{1,0},{2,3},{3,2},{4,5},{5,4},{6,7},{7,6},{8,9},{9,8},{10,11... | collective-permute-start | bytes 786440 | tf_op jit(solution)/shard_map/ppermute | solution.py:475
  2.5 1.4 %factors.2.weight_ref = bf16[16,128,256]{2,1,0:T(8,128)(2,1)S(1)} custom-call(bf16[32,3,2,1,64,64]{5,4,3,2,1,0:T(8,128)(2,1)} %factor_hbm.3, s32[3,1,32]{2,1,0:T(1,128)} %bitcast.2, bf16[16,2,32,128]{3,2,1,0:T(8,128)(2,1)S(1)} %get-tuple-element.20.after.state_ref), custom_call_target="tpu_custom_call" | custom-call | flops 524 | bytes 2097 | tf_op jit(solution)/shard_map/factors/pallas_call | solution.py:167
  3.9 0.0 collective-permute-done.partner_ref
  3.9 0.4 %level0_0.1.state_ref = bf16[16,32,128]{2,1,0:T(8,128)(2,1)S(1)} custom-call(bf16[16,2,32,128]{3,2,1,0:T(8,128)(2,1)S(1)} %get-tuple-element.20.after.state_ref, bf16[16,2,32,128]{3,2,1,0:T(8,128)(2,1)S(1)} %collective-permute-done.partner_ref, bf16[16,128,256]{2,1,0:T(8,128)(2,1)S(1)} %factors.2.weight_ref), custom_call_target="tpu_custom_call" | custom-call | flops 33554 | bytes 393 | tf_op jit(solution)/shard_map/level0_0/pallas_call | solution.py:218
  4.4 2.7 %collective-permute-start.2 = (bf16[16,32,128]{2,1,0:T(8,128)(2,1)S(1)}, bf16[16,32,128]{2,1,0:T(8,128)(2,1)S(1)}, u32[]{:S(2)}, u32[]{:S(2)}) collective-permute-start(bf16[16,32,128]{2,1,0:T(8,128)(2,1)S(1)} %level0_0.1.state_ref), channel_id=1, source_target_pairs={{0,2},{1,3},{2,0},{3,1},{4,6},{5,7},{6,4},{7,5},{8,10},{9,11},{10,... | collective-permute-start | bytes 393224 | tf_op jit(solution)/shard_map/ppermute | solution.py:475
  7.0 0.4 %level0_1.1.after.state_ref = bf16[16,32,128]{2,1,0:T(8,128)(2,1)S(1)} custom-call(bf16[16,2,32,128]{3,2,1,0:T(8,128)(2,1)S(1)} %get-tuple-element.20.after.state_ref, bf16[16,2,32,128]{3,2,1,0:T(8,128)(2,1)S(1)} %collective-permute-done.partner_ref, bf16[16,128,256]{2,1,0:T(8,128)(2,1)S(1)} %factors.2.weight_ref), custom_call_target="tpu_custom_call" | custom-call | flops 33554 | bytes 393 | tf_op jit(solution)/shard_map/level0_1/pallas_call | solution.py:218
  7.5 0.0 copy-start
  7.5 0.1 collective-permute-start.1
  7.6 2.3 %factors.3 = (bf16[16,128,256]{2,1,0:T(8,128)(2,1)S(1)}, bf16[16,64,128]{2,1,0:T(8,128)(2,1)S(1)}, bf16[16,64,128]{2,1,0:T(8,128)(2,1)S(1)}, bf16[2,32,64,256]{3,2,1,0:T(8,128)(2,1)S(1)}) custom-call(bf16[32,3,2,1,64,64]{5,4,3,2,1,0:T(8,128)(2,1)} %factor_hbm.3, s32[3,1,32]{2,1,0:T(1,128)} %bitcast.3, bf16[16,32,128]{2,1,0:T(8,128)(2,1)S(1)} %level0_1.1.after.state_ref, ...), custom_call_target="tpu_custom_call" | custom-call | flops 1048 | bytes 4194 | tf_op jit(solution)/shard_map/factors/pallas_call | solution.py:167
  9.8 2.0 %collective-permute-start.6 = (bf16[16,64,128]{2,1,0:T(8,128)(2,1)S(1)}, bf16[16,64,128]{2,1,0:T(8,128)(2,1)S(1)}, u32[]{:S(2)}, u32[]{:S(2)}) collective-permute-start(bf16[16,64,128]{2,1,0:T(8,128)(2,1)S(1)} %get-tuple-element.28.cross_ref), channel_id=1, source_target_pairs={{0,8},{8,0},{16,24},{24,16},{1,9},{9,1},{17,25},{25,17},{2,10},{10... | collective-permute-start | bytes 786440 | tf_op jit(solution)/shard_map/ppermute | solution.py:475
  11.8 0.0 collective-permute-done.2.partner_ref
  11.8 0.4 %level1_0.1.own_ref = bf16[16,32,128]{2,1,0:T(8,128)(2,1)S(1)} custom-call(bf16[16,32,128]{2,1,0:T(8,128)(2,1)S(1)} %level0_0.1.state_ref, bf16[16,32,128]{2,1,0:T(8,128)(2,1)S(1)} %collective-permute-done.2.partner_ref, bf16[16,128,256]{2,1,0:T(8,128)(2,1)S(1)} %get-tuple-element.21.weight_ref), custom_call_target="tpu_custom_call" | custom-call | flops 33554 | bytes 393 | tf_op jit(solution)/shard_map/level1_0/pallas_call | solution.py:218
  12.3 2.6 %collective-permute-start.3 = (bf16[16,32,128]{2,1,0:T(8,128)(2,1)S(1)}, bf16[16,32,128]{2,1,0:T(8,128)(2,1)S(1)}, u32[]{:S(2)}, u32[]{:S(2)}) collective-permute-start(bf16[16,32,128]{2,1,0:T(8,128)(2,1)S(1)} %level1_0.1.own_ref), channel_id=1, source_target_pairs={{0,4},{1,5},{2,6},{3,7},{4,0},{5,1},{6,2},{7,3},{8,12},{9,13},{10,... | collective-permute-start | bytes 393224 | tf_op jit(solution)/shard_map/ppermute | solution.py:475
  14.9 0.0 collective-permute-done.1.partner_ref
  14.9 0.8 %level1_1.1 = (bf16[16,32,128]{2,1,0:T(8,128)(2,1)S(1)}, bf16[16,16,128]{2,1,0:T(8,128)(2,1)S(1)}, bf16[16,32,128]{2,1,0:T(8,128)(2,1)S(1)}) custom-call(bf16[16,32,128]{2,1,0:T(8,128)(2,1)S(1)} %level0_1.1.after.state_ref, bf16[16,32,128]{2,1,0:T(8,128)(2,1)S(1)} %collective-permute-done.1.partner_ref, ...), custom_call_target="tpu_custom_call" | custom-call | flops 33554 | bytes 393 | tf_op jit(solution)/shard_map/level1_1/pallas_call | solution.py:218
  15.7 1.4 %collective-permute-start.4 = (bf16[16,32,128]{2,1,0:T(8,128)(2,1)S(1)}, bf16[16,32,128]{2,1,0:T(8,128)(2,1)S(1)}, u32[]{:S(2)}, u32[]{:S(2)}) collective-permute-start(bf16[16,32,128]{2,1,0:T(8,128)(2,1)S(1)} %get-tuple-element.30), channel_id=1, source_target_pairs={{0,8},{8,0},{16,24},{24,16},{1,9},{9,1},{17,25},{25,17},{2,10},{10... | collective-permute-start | bytes 393224 | tf_op jit(solution)/shard_map/ppermute | solution.py:475
  17.2 1.8 %collective-permute-start.8 = (bf16[16,16,128]{2,1,0:T(8,128)(2,1)S(1)}, bf16[16,16,128]{2,1,0:T(8,128)(2,1)S(1)}, u32[]{:S(2)}, u32[]{:S(2)}) collective-permute-start(bf16[16,16,128]{2,1,0:T(8,128)(2,1)S(1)} %get-tuple-element.34), channel_id=1, source_target_pairs={{0,12},{1,13},{2,14},{3,15},{4,8},{5,9},{6,10},{7,11},{8,4},{9,5},... | collective-permute-start | bytes 196616 | tf_op jit(solution)/shard_map/ppermute | solution.py:482
  19.0 0.0 copy-done
  19.0 0.7 %places.1 = (bf16[4,32,128]{2,1,0:T(8,128)(2,1)S(1)}, bf16[256,128]{1,0:T(8,128)(2,1)S(1)}) custom-call(s32[128]{0:T(128)S(1)} %copy-done, bf16[16,32,128]{2,1,0:T(8,128)(2,1)S(1)} %get-tuple-element.23.after.state_ref), custom_call_target="tpu_custom_call" | custom-call | flops 16 | bytes 131 | tf_op jit(solution)/shard_map/places/pallas_call | solution.py:352
  19.7 2.1 %collective-permute-start.5 = (bf16[16,16,128]{2,1,0:T(8,128)(2,1)S(1)}, bf16[16,16,128]{2,1,0:T(8,128)(2,1)S(1)}, u32[]{:S(2)}, u32[]{:S(2)}) collective-permute-start(bf16[16,16,128]{2,1,0:T(8,128)(2,1)S(1)} %late_columns.1), channel_id=1, source_target_pairs={{0,12},{1,13},{2,14},{3,15},{4,8},{5,9},{6,10},{7,11},{8,4},{9,5},... | collective-permute-start | bytes 196616 | tf_op jit(solution)/shard_map/ppermute | solution.py:482
  21.8 0.7 %collective-permute-done.3.partner_ref = bf16[16,32,128]{2,1,0:T(8,128)(2,1)S(1)} collective-permute-done((bf16[16,32,128]{2,1,0:T(8,128)(2,1)S(1)}, bf16[16,32,128]{2,1,0:T(8,128)(2,1)S(1)}, u32[]{:S(2)}, u32[]{:S(2)}) %collective-permute-start.3) | collective-permute-done | bytes 131104 | tf_op jit(solution)/shard_map/ppermute | solution.py:475
  22.4 0.5 %last_own.1 = (bf16[256,128]{1,0:T(8,128)(2,1)S(1)}, bf16[256,128]{1,0:T(8,128)(2,1)S(1)}) custom-call(bf16[256,128]{1,0:T(8,128)(2,1)S(1)} %get-tuple-element.25.after.refs_1_.refs_2_, bf16[16,32,128]{2,1,0:T(8,128)(2,1)S(1)} %level1_0.1.own_ref, bf16[16,32,128]{2,1,0:T(8,128)(2,1)S(1)} %collective-permute-done.3.partner_ref, ...), custom_call_target="tpu_custom_call" | custom-call | flops 33554 | bytes 393 | tf_op jit(solution)/shard_map/last_own/pallas_call | solution.py:316
  22.9 1.6 %collective-permute-start.7 = (bf16[256,128]{1,0:T(8,128)(2,1)S(1)}, bf16[256,128]{1,0:T(8,128)(2,1)S(1)}, u32[]{:S(2)}, u32[]{:S(2)}) collective-permute-start(bf16[256,128]{1,0:T(8,128)(2,1)S(1)} %get-tuple-element.31), channel_id=1, source_target_pairs={{0,16},{8,24},{16,0},{24,8},{1,17},{9,25},{17,1},{25,9},{2,18},{10... | collective-permute-start | bytes 196616 | tf_op jit(solution)/shard_map/ppermute | solution.py:475
  24.5 0.8 %collective-permute-done.8.partner_ref = bf16[16,16,128]{2,1,0:T(8,128)(2,1)S(1)} collective-permute-done((bf16[16,16,128]{2,1,0:T(8,128)(2,1)S(1)}, bf16[16,16,128]{2,1,0:T(8,128)(2,1)S(1)}, u32[]{:S(2)}, u32[]{:S(2)}) %collective-permute-start.8) | collective-permute-done | bytes 65568 | tf_op jit(solution)/shard_map/ppermute | solution.py:482
  25.3 0.0 collective-permute-done.4.own_ref
  25.3 0.0 collective-permute-done.6.cross_ref
  25.3 0.4 %last_early.1 = bf16[256,128]{1,0:T(8,128)(2,1)S(1)} custom-call(bf16[256,128]{1,0:T(8,128)(2,1)S(1)} %get-tuple-element.25.after.refs_1_.refs_2_, bf16[16,32,128]{2,1,0:T(8,128)(2,1)S(1)} %collective-permute-done.4.own_ref, bf16[16,16,128]{2,1,0:T(8,128)(2,1)S(1)} %collective-permute-done.8.partner_ref, ...), custom_call_target="tpu_custom_call" | custom-call | flops 16777 | bytes 196 | tf_op jit(solution)/shard_map/last_early/pallas_call | solution.py:316
  25.7 1.6 %collective-permute-start.9 = (bf16[256,128]{1,0:T(8,128)(2,1)S(1)}, bf16[256,128]{1,0:T(8,128)(2,1)S(1)}, u32[]{:S(2)}, u32[]{:S(2)}) collective-permute-start(bf16[256,128]{1,0:T(8,128)(2,1)S(1)} %last_early.1), channel_id=1, source_target_pairs={{0,16},{8,24},{16,0},{24,8},{1,17},{9,25},{17,1},{25,9},{2,18},{10... | collective-permute-start | bytes 196616 | tf_op jit(solution)/shard_map/ppermute | solution.py:475
  27.3 0.0 collective-permute-done.5.partner_ref
  27.3 0.4 %last_late.1.refs_5_ = bf16[256,128]{1,0:T(8,128)(2,1)S(1)} custom-call(bf16[256,128]{1,0:T(8,128)(2,1)S(1)} %get-tuple-element.25.after.refs_1_.refs_2_, bf16[16,32,128]{2,1,0:T(8,128)(2,1)S(1)} %collective-permute-done.4.own_ref, bf16[16,16,128]{2,1,0:T(8,128)(2,1)S(1)} %collective-permute-done.5.partner_ref, ...), custom_call_target="tpu_custom_call" | custom-call | flops 16777 | bytes 196 | tf_op jit(solution)/shard_map/last_late/pallas_call | solution.py:316
  27.6 0.0 collective-permute-done.7.refs_6_
  27.6 1.8 %root.2 = (bf16[8,2,256,128]{3,2,1,0:T(8,128)(2,1)S(1)}, bf16[1,32,64,256]{3,2,1,0:T(8,128)(2,1)S(1)}) custom-call(bf16[4,32,128]{2,1,0:T(8,128)(2,1)S(1)} %get-tuple-element.24.refs_0_.refs_1_, bf16[256,128]{1,0:T(8,128)(2,1)S(1)} %get-tuple-element.25.after.refs_1_.refs_2_, bf16[32,64,256]{2,1,0:T(8,128)(2,1)S(1)} %get-tuple-element.26.refs_2_, ...), custom_call_target="tpu_custom_call" | custom-call | flops 50331 | bytes 3145 | tf_op jit(solution)/shard_map/root/pallas_call | solution.py:450
  29.5 0.5 %collective-permute-done.9.refs_4_ = bf16[256,128]{1,0:T(8,128)(2,1)S(1)} collective-permute-done((bf16[256,128]{1,0:T(8,128)(2,1)S(1)}, bf16[256,128]{1,0:T(8,128)(2,1)S(1)}, u32[]{:S(2)}, u32[]{:S(2)}) %collective-permute-start.9) | collective-permute-done | bytes 65568 | tf_op jit(solution)/shard_map/ppermute | solution.py:475
  30.0 1.6 %root.3 = bf16[8,2,256,128]{3,2,1,0:T(8,128)(2,1)} custom-call(bf16[8,2,256,128]{3,2,1,0:T(8,128)(2,1)S(1)} %get-tuple-element.32.refs_0_, bf16[4,32,128]{2,1,0:T(8,128)(2,1)S(1)} %get-tuple-element.24.refs_0_.refs_1_, bf16[256,128]{1,0:T(8,128)(2,1)S(1)} %get-tuple-element.25.after.refs_1_.refs_2_, bf16[1,32,64,256]{3,2,1,0:T(8,128)(2,1)S(1)} %get-tuple-element.33.refs_3_, ...), custom_call_target="tpu_custom_call" | custom-call | flops 16777 | bytes 1048 | tf_op jit(solution)/shard_map/root/pallas_call | solution.py:450
  (1 shorter events, 0.0 us)
Async XLA Ops:
  1.9 2.0 %collective-permute-start = (bf16[16,2,32,128]{3,2,1,0:T(8,128)(2,1)S(1)}, bf16[16,2,32,128]{3,2,1,0:T(8,128)(2,1)S(1)}, u32[]{:S(2)}, u32[]{:S(2)}) collective-permute-start(bf16[16,2,32,128]{3,2,1,0:T(8,128)(2,1)S(1)} %get-tuple-element.20.after.state_ref), channel_id=1, source_target_pairs={{0,1},{1,0},{2,3},{3,2},{4,5},{5,4},{6,7},{7,6},{8,9},{9,8},{10,11... | collective-permute-start | bytes 786440 | tf_op jit(solution)/shard_map/ppermute | solution.py:475
  4.4 7.5 %collective-permute-start.2 = (bf16[16,32,128]{2,1,0:T(8,128)(2,1)S(1)}, bf16[16,32,128]{2,1,0:T(8,128)(2,1)S(1)}, u32[]{:S(2)}, u32[]{:S(2)}) collective-permute-start(bf16[16,32,128]{2,1,0:T(8,128)(2,1)S(1)} %level0_0.1.state_ref), channel_id=1, source_target_pairs={{0,2},{1,3},{2,0},{3,1},{4,6},{5,7},{6,4},{7,5},{8,10},{9,11},{10,... | collective-permute-start | bytes 393224 | tf_op jit(solution)/shard_map/ppermute | solution.py:475
  7.5 11.5 %copy-start = (s32[128]{0:T(128)S(1)}, s32[128]{0:T(128)}, u32[]{:S(2)}) copy-start(s32[128]{0:T(128)} %order_ref.1) | copy-start | bytes 1540
  7.5 7.4 %collective-permute-start.1 = (bf16[16,32,128]{2,1,0:T(8,128)(2,1)S(1)}, bf16[16,32,128]{2,1,0:T(8,128)(2,1)S(1)}, u32[]{:S(2)}, u32[]{:S(2)}) collective-permute-start(bf16[16,32,128]{2,1,0:T(8,128)(2,1)S(1)} %level0_1.1.after.state_ref), channel_id=1, source_target_pairs={{0,2},{1,3},{2,0},{3,1},{4,6},{5,7},{6,4},{7,5},{8,10},{9,11},{10,... | collective-permute-start | bytes 393224 | tf_op jit(solution)/shard_map/ppermute | solution.py:475
  9.8 15.5 %collective-permute-start.6 = (bf16[16,64,128]{2,1,0:T(8,128)(2,1)S(1)}, bf16[16,64,128]{2,1,0:T(8,128)(2,1)S(1)}, u32[]{:S(2)}, u32[]{:S(2)}) collective-permute-start(bf16[16,64,128]{2,1,0:T(8,128)(2,1)S(1)} %get-tuple-element.28.cross_ref), channel_id=1, source_target_pairs={{0,8},{8,0},{16,24},{24,16},{1,9},{9,1},{17,25},{25,17},{2,10},{10... | collective-permute-start | bytes 786440 | tf_op jit(solution)/shard_map/ppermute | solution.py:475
  12.3 10.2 %collective-permute-start.3 = (bf16[16,32,128]{2,1,0:T(8,128)(2,1)S(1)}, bf16[16,32,128]{2,1,0:T(8,128)(2,1)S(1)}, u32[]{:S(2)}, u32[]{:S(2)}) collective-permute-start(bf16[16,32,128]{2,1,0:T(8,128)(2,1)S(1)} %level1_0.1.own_ref), channel_id=1, source_target_pairs={{0,4},{1,5},{2,6},{3,7},{4,0},{5,1},{6,2},{7,3},{8,12},{9,13},{10,... | collective-permute-start | bytes 393224 | tf_op jit(solution)/shard_map/ppermute | solution.py:475
  15.7 9.6 %collective-permute-start.4 = (bf16[16,32,128]{2,1,0:T(8,128)(2,1)S(1)}, bf16[16,32,128]{2,1,0:T(8,128)(2,1)S(1)}, u32[]{:S(2)}, u32[]{:S(2)}) collective-permute-start(bf16[16,32,128]{2,1,0:T(8,128)(2,1)S(1)} %get-tuple-element.30), channel_id=1, source_target_pairs={{0,8},{8,0},{16,24},{24,16},{1,9},{9,1},{17,25},{25,17},{2,10},{10... | collective-permute-start | bytes 393224 | tf_op jit(solution)/shard_map/ppermute | solution.py:475
  17.2 8.1 %collective-permute-start.8 = (bf16[16,16,128]{2,1,0:T(8,128)(2,1)S(1)}, bf16[16,16,128]{2,1,0:T(8,128)(2,1)S(1)}, u32[]{:S(2)}, u32[]{:S(2)}) collective-permute-start(bf16[16,16,128]{2,1,0:T(8,128)(2,1)S(1)} %get-tuple-element.34), channel_id=1, source_target_pairs={{0,12},{1,13},{2,14},{3,15},{4,8},{5,9},{6,10},{7,11},{8,4},{9,5},... | collective-permute-start | bytes 196616 | tf_op jit(solution)/shard_map/ppermute | solution.py:482
  19.7 7.5 %collective-permute-start.5 = (bf16[16,16,128]{2,1,0:T(8,128)(2,1)S(1)}, bf16[16,16,128]{2,1,0:T(8,128)(2,1)S(1)}, u32[]{:S(2)}, u32[]{:S(2)}) collective-permute-start(bf16[16,16,128]{2,1,0:T(8,128)(2,1)S(1)} %late_columns.1), channel_id=1, source_target_pairs={{0,12},{1,13},{2,14},{3,15},{4,8},{5,9},{6,10},{7,11},{8,4},{9,5},... | collective-permute-start | bytes 196616 | tf_op jit(solution)/shard_map/ppermute | solution.py:482
  22.9 4.7 %collective-permute-start.7 = (bf16[256,128]{1,0:T(8,128)(2,1)S(1)}, bf16[256,128]{1,0:T(8,128)(2,1)S(1)}, u32[]{:S(2)}, u32[]{:S(2)}) collective-permute-start(bf16[256,128]{1,0:T(8,128)(2,1)S(1)} %get-tuple-element.31), channel_id=1, source_target_pairs={{0,16},{8,24},{16,0},{24,8},{1,17},{9,25},{17,1},{25,9},{2,18},{10... | collective-permute-start | bytes 196616 | tf_op jit(solution)/shard_map/ppermute | solution.py:475
  25.7 4.3 %collective-permute-start.9 = (bf16[256,128]{1,0:T(8,128)(2,1)S(1)}, bf16[256,128]{1,0:T(8,128)(2,1)S(1)}, u32[]{:S(2)}, u32[]{:S(2)}) collective-permute-start(bf16[256,128]{1,0:T(8,128)(2,1)S(1)} %last_early.1), channel_id=1, source_target_pairs={{0,16},{8,24},{16,0},{24,8},{1,17},{9,25},{17,1},{25,9},{2,18},{10... | collective-permute-start | bytes 196616 | tf_op jit(solution)/shard_map/ppermute | solution.py:475

commit v2 on v1

--- a/solution.py
+++ b/solution.py
@@ -329,11 +329,15 @@
     return [part.reshape(rows, lanes) for part in parts]
 
 
-def place_kernel(group, order_ref, after, place_ref, alive_ref, rows_ref):
+def place_kernel(group, order_ref, after, root_hbm, place_ref, alive_ref, later_ref, rows_ref, sems):
     del after
     owners, here, slots = place_ref.shape
     degrees = alive_ref.shape[0]
     me = lax.axis_index("order")
+    later = later_ref.shape[0]
+    fetches = [fetch_roots(owners - later + i, root_hbm, later_ref.at[i], sems.at[i]) for i in range(later)]
+    for fetch in fetches:
+        fetch.start()
     lane = lax.broadcasted_iota(jnp.int32, (1, slots), 1)
     for k in range(owners):
         for slot in range(here):
@@ -344,20 +348,26 @@
     degree = lax.axis_index("lat") * degrees + lax.broadcasted_iota(jnp.int32, (degrees, slots), 0)
     window = DEGREES // slots * lax.broadcasted_iota(jnp.int32, (degrees, slots), 1)
     alive_ref[...] = (degree >= window).astype(F32).astype(BF16)
-
-
-def places_of(order_of_slot, degrees, owners, group, after):
-    slots = order_of_slot.shape[0]
+    for fetch in fetches:
+        fetch.wait()
+
+
+def places_of(order_of_slot, root_basis, owners, later, group, after):
+    slots, rank, degrees = root_basis.shape
     here = slots // owners
     return call(
         functools.partial(place_kernel, group),
         "places",
-        [jax.ShapeDtypeStruct((owners, here, slots), BF16), jax.ShapeDtypeStruct((degrees, slots), BF16)],
-        [IN_SMEM, ANYWHERE],
+        [
+            jax.ShapeDtypeStruct((owners, here, slots), BF16),
+            jax.ShapeDtypeStruct((degrees, slots), BF16),
+            jax.ShapeDtypeStruct((later, here, rank, degrees), BF16),
+        ],
+        [IN_SMEM, ANYWHERE, IN_HBM],
         slots * slots,
         8 * slots * slots,
-        [pltpu.VMEM((here, slots), F32)],
-    )(order_of_slot, after)
+        [pltpu.VMEM((here, slots), F32), pltpu.SemaphoreType.DMA((later,))],
+    )(order_of_slot, after, root_basis)
 
 
 def root_kernel(group, first, last, *refs):
@@ -376,11 +386,8 @@
     if last:
         out_ref, rows_ref, natural_ref, sems = refs
     else:
-        root_hbm, out_ref, later_ref, rows_ref, sems = refs
+        out_ref, rows_ref = refs
         natural_ref = out_ref
-        for i in range(later_ref.shape[0]):
-            copies.append(fetch_roots(count + i, root_hbm, later_ref.at[i], sems.at[i]))
-            copies[-1].start()
     fields, parts, degrees, slots = out_ref.shape
     columns = fields * parts
     rank = root_refs[0].shape[1]
@@ -432,8 +439,7 @@
     columns = state_rows * 2 // here
     last = so_far is not None
     out = jax.ShapeDtypeStruct((columns // 2, 2, degrees, slots), BF16)
-    root_basis = roots[-1]
-    inputs = [places, alive, *(roots if so_far is not None else roots[:-1]), *states]
+    inputs = [places, alive, *roots, *states]
     in_specs = whole_blocks(len(inputs))
     scratch = [pltpu.VMEM((degrees // 128, count * here * columns, 128), F32)]
     more = {}
@@ -442,11 +448,6 @@
         in_specs = whole_blocks(len(inputs))
         scratch += [pltpu.VMEM(out.shape, BF16), pltpu.SemaphoreType.DMA((columns // 2,))]
         more["out_specs"] = IN_HBM
-    else:
-        inputs.append(root_basis)
-        in_specs.append(IN_HBM)
-        out = [out, jax.ShapeDtypeStruct((owners - count, here, rank, degrees), BF16)]
-        scratch.append(pltpu.SemaphoreType.DMA((owners - count,)))
     return call(
         functools.partial(root_kernel, group, first, last),
         "root",
@@ -503,15 +504,17 @@
     mine_partner = swap(mine, "lat", top)
     early_partner = swap_both(early, 1, top)
     other_own = swap(term, "order", 1)
-    places, alive = places_of(order_of_slot, root_basis.shape[2], owners, group, other)
+    places, alive, later_roots = places_of(
+        order_of_slot, root_basis, owners, owners - early_pieces, group, other
+    )
     late_partner = swap_both(late_columns(alive, other, own_columns), 1, top)
     even = last_states("last_own", alive, mine, mine_partner, (cross_factors, own_factors), high, True)
     begin = columns // 2 - own_columns
     odd = last_states("last_early", alive, other_own, early_partner, (other_cross,), high - 1, False)
     odd = [*last_states("last_late", alive, other_own, late_partner, (other_cross,), 1, False, begin), *odd]
     arrived = [swap((odd if k % 2 else even)[k // 2], "order", k // 2 * 2) if k > 1 else (even, odd)[k][0] for k in range(owners)]
-    roots = [root_0, early_roots, root_basis]
-    spectra, later_roots = spectra_of(arrived[:early_pieces], roots, places, alive, None, early_pieces, group)
+    roots = [root_0, early_roots]
+    spectra = spectra_of(arrived[:early_pieces], roots, places, alive, None, early_pieces, group)
     return spectra_of(arrived[early_pieces:], [later_roots], places, alive, spectra, early_pieces, group)
 
 

time: 31.8 us -> 31.5 us (level)
  starting transfers between devices: 16.4 us -> 15.4 us
  Pallas kernels: 13.1 us -> 13.8 us
    pallas_call x1, Pallas kernels: 0.67 us -> 1.78 us  [places_of(): call(functools.partial(place_kernel, group), 'places', [jax.ShapeDtypeStr...]
    ppermute x8, starting transfers between devices: 12.5 us -> 11.5 us  [swap(): lax.ppermute(array, axis, [(i, i ^ bits) for i in range(lax.axis_size(axi...]
    pallas_call x2, Pallas kernels: 3.43 us -> 3.06 us  [spectra_of(): call(functools.partial(root_kernel, group, first, last), 'root', out, in_...]
    ppermute x8, waiting for transfers between devices: 1.23 us -> 0.87 us  [swap(): lax.ppermute(array, axis, [(i, i ^ bits) for i in range(lax.axis_size(axi...]
  transfers between devices with their start and end apart: 10 -> 10, of which waited for: 3 -> 3; matrix products, arithmetic and copies ran while one was open for 0% -> 0% of each run, Pallas kernels for 29% -> 31%
where the time goes in v2:
time: 31.5 us; the launch traced here: 31.3 us
  starting transfers between devices  15.4 us (49%)
  Pallas kernels  13.8 us (44%)
  waiting for transfers between devices  1.95 us (6%)
    ppermute x8, starting transfers between devices, swap(): lax.ppermute(array, axis, [(i, i ^ bits) for i in range(lax.axis_size(axi...  11.5 us
    ppermute x2, starting transfers between devices, swap_both(): return lax.ppermute(array, ('order', 'lat'), pairs)  3.89 us
    pallas_call x2, Pallas kernels, level_weights(): call(functools.partial(factor_kernel, levels, pieces, root_pieces), 'fact...  3.69 us
    pallas_call x2, Pallas kernels, spectra_of(): call(functools.partial(root_kernel, group, first, last), 'root', out, in_...  3.06 us
    pallas_call x4, Pallas kernels, next_states(): call(functools.partial(level_kernel, side, 'order'), name, [jax.ShapeDtyp...  2.14 us
    pallas_call x1, Pallas kernels, leaf_states(): call(functools.partial(leaf_kernel, pieces, group), 'leaf', [jax.ShapeDty...  1.92 us
    pallas_call x1, Pallas kernels, places_of(): call(functools.partial(place_kernel, group), 'places', [jax.ShapeDtypeStr...  1.78 us
    pallas_call x3, Pallas kernels, last_states(): call(functools.partial(last_level_kernel, turn, begin, 'order'), name, [j...  1.23 us
  transfers between devices with their start and end apart: 10, of which 3 were waited for; matrix products, arithmetic and copies ran while one was open for 0% of the time, Pallas kernels for 31%

profile of v2, /device:TPU:0, one launch (start us, length us, event | category | flops | bytes accessed | tf_op | source)
XLA Modules:
  0.0 31.3 jit_solution(10351113868243369598)
XLA Ops:
  0.0 1.9 %leaf.1 = (bf16[16,2,32,128]{3,2,1,0:T(8,128)(2,1)S(1)}, bf16[32,64,256]{2,1,0:T(8,128)(2,1)S(1)}) custom-call(bf16[32,64,256]{2,1,0:T(8,128)(2,1)} %fourier_hbm.1, f32[1,256]{1,0:T(1,128)} %bitcast.4, bf16[32,64,256]{2,1,0:T(8,128)(2,1)} %leaf_hbm.1, bf16[128,64,256]{2,1,0:T(8,128)(2,1)} %root_hbm.3), custom_call_target="tpu_custom_call" | custom-call | flops 67108 | bytes 2097 | tf_op jit(solution)/shard_map/leaf/pallas_call | solution.py:92
  1.9 0.5 %collective-permute-start = (bf16[16,2,32,128]{3,2,1,0:T(8,128)(2,1)S(1)}, bf16[16,2,32,128]{3,2,1,0:T(8,128)(2,1)S(1)}, u32[]{:S(2)}, u32[]{:S(2)}) collective-permute-start(bf16[16,2,32,128]{3,2,1,0:T(8,128)(2,1)S(1)} %get-tuple-element.19.after.state_ref), channel_id=1, source_target_pairs={{0,1},{1,0},{2,3},{3,2},{4,5},{5,4},{6,7},{7,6},{8,9},{9,8},{10,11... | collective-permute-start | bytes 786440 | tf_op jit(solution)/shard_map/ppermute | solution.py:476
  2.5 1.4 %factors.2.weight_ref = bf16[16,128,256]{2,1,0:T(8,128)(2,1)S(1)} custom-call(bf16[32,3,2,1,64,64]{5,4,3,2,1,0:T(8,128)(2,1)} %factor_hbm.3, s32[3,1,32]{2,1,0:T(1,128)} %bitcast.2, bf16[16,2,32,128]{3,2,1,0:T(8,128)(2,1)S(1)} %get-tuple-element.19.after.state_ref), custom_call_target="tpu_custom_call" | custom-call | flops 524 | bytes 2097 | tf_op jit(solution)/shard_map/factors/pallas_call | solution.py:167
  3.9 0.0 collective-permute-done.partner_ref
  3.9 0.4 %level0_0.1.state_ref = bf16[16,32,128]{2,1,0:T(8,128)(2,1)S(1)} custom-call(bf16[16,2,32,128]{3,2,1,0:T(8,128)(2,1)S(1)} %get-tuple-element.19.after.state_ref, bf16[16,2,32,128]{3,2,1,0:T(8,128)(2,1)S(1)} %collective-permute-done.partner_ref, bf16[16,128,256]{2,1,0:T(8,128)(2,1)S(1)} %factors.2.weight_ref), custom_call_target="tpu_custom_call" | custom-call | flops 33554 | bytes 393 | tf_op jit(solution)/shard_map/level0_0/pallas_call | solution.py:218
  4.4 2.7 %collective-permute-start.2 = (bf16[16,32,128]{2,1,0:T(8,128)(2,1)S(1)}, bf16[16,32,128]{2,1,0:T(8,128)(2,1)S(1)}, u32[]{:S(2)}, u32[]{:S(2)}) collective-permute-start(bf16[16,32,128]{2,1,0:T(8,128)(2,1)S(1)} %level0_0.1.state_ref), channel_id=1, source_target_pairs={{0,2},{1,3},{2,0},{3,1},{4,6},{5,7},{6,4},{7,5},{8,10},{9,11},{10,... | collective-permute-start | bytes 393224 | tf_op jit(solution)/shard_map/ppermute | solution.py:476
  7.0 0.4 %level0_1.1.after.state_ref = bf16[16,32,128]{2,1,0:T(8,128)(2,1)S(1)} custom-call(bf16[16,2,32,128]{3,2,1,0:T(8,128)(2,1)S(1)} %get-tuple-element.19.after.state_ref, bf16[16,2,32,128]{3,2,1,0:T(8,128)(2,1)S(1)} %collective-permute-done.partner_ref, bf16[16,128,256]{2,1,0:T(8,128)(2,1)S(1)} %factors.2.weight_ref), custom_call_target="tpu_custom_call" | custom-call | flops 33554 | bytes 393 | tf_op jit(solution)/shard_map/level0_1/pallas_call | solution.py:218
  7.5 0.0 copy-start
  7.5 0.1 collective-permute-start.1
  7.6 2.3 %factors.3 = (bf16[16,128,256]{2,1,0:T(8,128)(2,1)S(1)}, bf16[16,64,128]{2,1,0:T(8,128)(2,1)S(1)}, bf16[16,64,128]{2,1,0:T(8,128)(2,1)S(1)}, bf16[2,32,64,256]{3,2,1,0:T(8,128)(2,1)S(1)}) custom-call(bf16[32,3,2,1,64,64]{5,4,3,2,1,0:T(8,128)(2,1)} %factor_hbm.3, s32[3,1,32]{2,1,0:T(1,128)} %bitcast.3, bf16[16,32,128]{2,1,0:T(8,128)(2,1)S(1)} %level0_1.1.after.state_ref, ...), custom_call_target="tpu_custom_call" | custom-call | flops 1048 | bytes 4194 | tf_op jit(solution)/shard_map/factors/pallas_call | solution.py:167
  9.8 2.0 %collective-permute-start.6 = (bf16[16,64,128]{2,1,0:T(8,128)(2,1)S(1)}, bf16[16,64,128]{2,1,0:T(8,128)(2,1)S(1)}, u32[]{:S(2)}, u32[]{:S(2)}) collective-permute-start(bf16[16,64,128]{2,1,0:T(8,128)(2,1)S(1)} %get-tuple-element.27.cross_ref), channel_id=1, source_target_pairs={{0,8},{8,0},{16,24},{24,16},{1,9},{9,1},{17,25},{25,17},{2,10},{10... | collective-permute-start | bytes 786440 | tf_op jit(solution)/shard_map/ppermute | solution.py:476
  11.8 0.0 collective-permute-done.2.partner_ref
  11.8 0.4 %level1_0.1.own_ref = bf16[16,32,128]{2,1,0:T(8,128)(2,1)S(1)} custom-call(bf16[16,32,128]{2,1,0:T(8,128)(2,1)S(1)} %level0_0.1.state_ref, bf16[16,32,128]{2,1,0:T(8,128)(2,1)S(1)} %collective-permute-done.2.partner_ref, bf16[16,128,256]{2,1,0:T(8,128)(2,1)S(1)} %get-tuple-element.20.weight_ref), custom_call_target="tpu_custom_call" | custom-call | flops 33554 | bytes 393 | tf_op jit(solution)/shard_map/level1_0/pallas_call | solution.py:218
  12.3 2.6 %collective-permute-start.3 = (bf16[16,32,128]{2,1,0:T(8,128)(2,1)S(1)}, bf16[16,32,128]{2,1,0:T(8,128)(2,1)S(1)}, u32[]{:S(2)}, u32[]{:S(2)}) collective-permute-start(bf16[16,32,128]{2,1,0:T(8,128)(2,1)S(1)} %level1_0.1.own_ref), channel_id=1, source_target_pairs={{0,4},{1,5},{2,6},{3,7},{4,0},{5,1},{6,2},{7,3},{8,12},{9,13},{10,... | collective-permute-start | bytes 393224 | tf_op jit(solution)/shard_map/ppermute | solution.py:476
  14.9 0.0 collective-permute-done.1.partner_ref
  14.9 0.8 %level1_1.1 = (bf16[16,32,128]{2,1,0:T(8,128)(2,1)S(1)}, bf16[16,16,128]{2,1,0:T(8,128)(2,1)S(1)}, bf16[16,32,128]{2,1,0:T(8,128)(2,1)S(1)}) custom-call(bf16[16,32,128]{2,1,0:T(8,128)(2,1)S(1)} %level0_1.1.after.state_ref, bf16[16,32,128]{2,1,0:T(8,128)(2,1)S(1)} %collective-permute-done.1.partner_ref, ...), custom_call_target="tpu_custom_call" | custom-call | flops 33554 | bytes 393 | tf_op jit(solution)/shard_map/level1_1/pallas_call | solution.py:218
  15.7 1.4 %collective-permute-start.4 = (bf16[16,32,128]{2,1,0:T(8,128)(2,1)S(1)}, bf16[16,32,128]{2,1,0:T(8,128)(2,1)S(1)}, u32[]{:S(2)}, u32[]{:S(2)}) collective-permute-start(bf16[16,32,128]{2,1,0:T(8,128)(2,1)S(1)} %get-tuple-element.29), channel_id=1, source_target_pairs={{0,8},{8,0},{16,24},{24,16},{1,9},{9,1},{17,25},{25,17},{2,10},{10... | collective-permute-start | bytes 393224 | tf_op jit(solution)/shard_map/ppermute | solution.py:476
  17.2 1.8 %collective-permute-start.8 = (bf16[16,16,128]{2,1,0:T(8,128)(2,1)S(1)}, bf16[16,16,128]{2,1,0:T(8,128)(2,1)S(1)}, u32[]{:S(2)}, u32[]{:S(2)}) collective-permute-start(bf16[16,16,128]{2,1,0:T(8,128)(2,1)S(1)} %get-tuple-element.32), channel_id=1, source_target_pairs={{0,12},{1,13},{2,14},{3,15},{4,8},{5,9},{6,10},{7,11},{8,4},{9,5},... | collective-permute-start | bytes 196616 | tf_op jit(solution)/shard_map/ppermute | solution.py:483
  19.0 0.0 copy-done
  19.0 1.8 %places.1 = (bf16[4,32,128]{2,1,0:T(8,128)(2,1)S(1)}, bf16[256,128]{1,0:T(8,128)(2,1)S(1)}, bf16[1,32,64,256]{3,2,1,0:T(8,128)(2,1)S(1)}) custom-call(s32[128]{0:T(128)S(1)} %copy-done, bf16[16,32,128]{2,1,0:T(8,128)(2,1)S(1)} %get-tuple-element.22.after.state_ref, bf16[128,64,256]{2,1,0:T(8,128)(2,1)} %root_hbm.3), custom_call_target="tpu_custom_call" | custom-call | flops 16 | bytes 131 | tf_op jit(solution)/shard_map/places/pallas_call | solution.py:358
  20.8 2.1 %collective-permute-start.5 = (bf16[16,16,128]{2,1,0:T(8,128)(2,1)S(1)}, bf16[16,16,128]{2,1,0:T(8,128)(2,1)S(1)}, u32[]{:S(2)}, u32[]{:S(2)}) collective-permute-start(bf16[16,16,128]{2,1,0:T(8,128)(2,1)S(1)} %late_columns.1), channel_id=1, source_target_pairs={{0,12},{1,13},{2,14},{3,15},{4,8},{5,9},{6,10},{7,11},{8,4},{9,5},... | collective-permute-start | bytes 196616 | tf_op jit(solution)/shard_map/ppermute | solution.py:483
  22.9 0.0 collective-permute-done.3.partner_ref
  22.9 0.5 %last_own.1 = (bf16[256,128]{1,0:T(8,128)(2,1)S(1)}, bf16[256,128]{1,0:T(8,128)(2,1)S(1)}) custom-call(bf16[256,128]{1,0:T(8,128)(2,1)S(1)} %get-tuple-element.24.after.refs_1_.refs_2_, bf16[16,32,128]{2,1,0:T(8,128)(2,1)S(1)} %level1_0.1.own_ref, bf16[16,32,128]{2,1,0:T(8,128)(2,1)S(1)} %collective-permute-done.3.partner_ref, ...), custom_call_target="tpu_custom_call" | custom-call | flops 33554 | bytes 393 | tf_op jit(solution)/shard_map/last_own/pallas_call | solution.py:316
  23.4 1.6 %collective-permute-start.7 = (bf16[256,128]{1,0:T(8,128)(2,1)S(1)}, bf16[256,128]{1,0:T(8,128)(2,1)S(1)}, u32[]{:S(2)}, u32[]{:S(2)}) collective-permute-start(bf16[256,128]{1,0:T(8,128)(2,1)S(1)} %get-tuple-element.30), channel_id=1, source_target_pairs={{0,16},{8,24},{16,0},{24,8},{1,17},{9,25},{17,1},{25,9},{2,18},{10... | collective-permute-start | bytes 196616 | tf_op jit(solution)/shard_map/ppermute | solution.py:476
  24.9 0.0 collective-permute-done.8.partner_ref
  24.9 0.0 collective-permute-done.4.own_ref
  25.0 0.0 collective-permute-done.6.cross_ref
  25.0 0.4 %last_early.1 = bf16[256,128]{1,0:T(8,128)(2,1)S(1)} custom-call(bf16[256,128]{1,0:T(8,128)(2,1)S(1)} %get-tuple-element.24.after.refs_1_.refs_2_, bf16[16,32,128]{2,1,0:T(8,128)(2,1)S(1)} %collective-permute-done.4.own_ref, bf16[16,16,128]{2,1,0:T(8,128)(2,1)S(1)} %collective-permute-done.8.partner_ref, ...), custom_call_target="tpu_custom_call" | custom-call | flops 16777 | bytes 196 | tf_op jit(solution)/shard_map/last_early/pallas_call | solution.py:316
  25.3 0.5 %collective-permute-start.9 = (bf16[256,128]{1,0:T(8,128)(2,1)S(1)}, bf16[256,128]{1,0:T(8,128)(2,1)S(1)}, u32[]{:S(2)}, u32[]{:S(2)}) collective-permute-start(bf16[256,128]{1,0:T(8,128)(2,1)S(1)} %last_early.1), channel_id=1, source_target_pairs={{0,16},{8,24},{16,0},{24,8},{1,17},{9,25},{17,1},{25,9},{2,18},{10... | collective-permute-start | bytes 196616 | tf_op jit(solution)/shard_map/ppermute | solution.py:476
  25.9 1.1 %collective-permute-done.5.partner_ref = bf16[16,16,128]{2,1,0:T(8,128)(2,1)S(1)} collective-permute-done((bf16[16,16,128]{2,1,0:T(8,128)(2,1)S(1)}, bf16[16,16,128]{2,1,0:T(8,128)(2,1)S(1)}, u32[]{:S(2)}, u32[]{:S(2)}) %collective-permute-start.5) | collective-permute-done | bytes 65568 | tf_op jit(solution)/shard_map/ppermute | solution.py:483
  27.0 0.4 %last_late.1.refs_5_ = bf16[256,128]{1,0:T(8,128)(2,1)S(1)} custom-call(bf16[256,128]{1,0:T(8,128)(2,1)S(1)} %get-tuple-element.24.after.refs_1_.refs_2_, bf16[16,32,128]{2,1,0:T(8,128)(2,1)S(1)} %collective-permute-done.4.own_ref, bf16[16,16,128]{2,1,0:T(8,128)(2,1)S(1)} %collective-permute-done.5.partner_ref, ...), custom_call_target="tpu_custom_call" | custom-call | flops 16777 | bytes 196 | tf_op jit(solution)/shard_map/last_late/pallas_call | solution.py:316
  27.3 0.4 %collective-permute-done.7.refs_6_ = bf16[256,128]{1,0:T(8,128)(2,1)S(1)} collective-permute-done((bf16[256,128]{1,0:T(8,128)(2,1)S(1)}, bf16[256,128]{1,0:T(8,128)(2,1)S(1)}, u32[]{:S(2)}, u32[]{:S(2)}) %collective-permute-start.7) | collective-permute-done | bytes 65568 | tf_op jit(solution)/shard_map/ppermute | solution.py:476
  27.7 1.4 %root.2.refs_0_ = bf16[8,2,256,128]{3,2,1,0:T(8,128)(2,1)S(1)} custom-call(bf16[4,32,128]{2,1,0:T(8,128)(2,1)S(1)} %get-tuple-element.23.refs_0_.refs_1_, bf16[256,128]{1,0:T(8,128)(2,1)S(1)} %get-tuple-element.24.after.refs_1_.refs_2_, bf16[32,64,256]{2,1,0:T(8,128)(2,1)S(1)} %get-tuple-element.25.refs_2_, ...), custom_call_target="tpu_custom_call" | custom-call | flops 50331 | bytes 3145 | tf_op jit(solution)/shard_map/root/pallas_call | solution.py:451
  29.1 0.5 %collective-permute-done.9.refs_4_ = bf16[256,128]{1,0:T(8,128)(2,1)S(1)} collective-permute-done((bf16[256,128]{1,0:T(8,128)(2,1)S(1)}, bf16[256,128]{1,0:T(8,128)(2,1)S(1)}, u32[]{:S(2)}, u32[]{:S(2)}) %collective-permute-start.9) | collective-permute-done | bytes 65568 | tf_op jit(solution)/shard_map/ppermute | solution.py:476
  29.6 1.6 %root.3 = bf16[8,2,256,128]{3,2,1,0:T(8,128)(2,1)} custom-call(bf16[8,2,256,128]{3,2,1,0:T(8,128)(2,1)S(1)} %root.2.refs_0_, bf16[4,32,128]{2,1,0:T(8,128)(2,1)S(1)} %get-tuple-element.23.refs_0_.refs_1_, bf16[256,128]{1,0:T(8,128)(2,1)S(1)} %get-tuple-element.24.after.refs_1_.refs_2_, bf16[1,32,64,256]{3,2,1,0:T(8,128)(2,1)S(1)} %get-tuple-element.31.refs_3_, ...), custom_call_target="tpu_custom_call" | custom-call | flops 16777 | bytes 1048 | tf_op jit(solution)/shard_map/root/pallas_call | solution.py:451
  (1 shorter events, 0.0 us)
Async XLA Ops:
  1.9 2.0 %collective-permute-start = (bf16[16,2,32,128]{3,2,1,0:T(8,128)(2,1)S(1)}, bf16[16,2,32,128]{3,2,1,0:T(8,128)(2,1)S(1)}, u32[]{:S(2)}, u32[]{:S(2)}) collective-permute-start(bf16[16,2,32,128]{3,2,1,0:T(8,128)(2,1)S(1)} %get-tuple-element.19.after.state_ref), channel_id=1, source_target_pairs={{0,1},{1,0},{2,3},{3,2},{4,5},{5,4},{6,7},{7,6},{8,9},{9,8},{10,11... | collective-permute-start | bytes 786440 | tf_op jit(solution)/shard_map/ppermute | solution.py:476
  4.4 7.5 %collective-permute-start.2 = (bf16[16,32,128]{2,1,0:T(8,128)(2,1)S(1)}, bf16[16,32,128]{2,1,0:T(8,128)(2,1)S(1)}, u32[]{:S(2)}, u32[]{:S(2)}) collective-permute-start(bf16[16,32,128]{2,1,0:T(8,128)(2,1)S(1)} %level0_0.1.state_ref), channel_id=1, source_target_pairs={{0,2},{1,3},{2,0},{3,1},{4,6},{5,7},{6,4},{7,5},{8,10},{9,11},{10,... | collective-permute-start | bytes 393224 | tf_op jit(solution)/shard_map/ppermute | solution.py:476
  7.5 11.5 %copy-start = (s32[128]{0:T(128)S(1)}, s32[128]{0:T(128)}, u32[]{:S(2)}) copy-start(s32[128]{0:T(128)} %order_ref.1) | copy-start | bytes 1540
  7.5 7.4 %collective-permute-start.1 = (bf16[16,32,128]{2,1,0:T(8,128)(2,1)S(1)}, bf16[16,32,128]{2,1,0:T(8,128)(2,1)S(1)}, u32[]{:S(2)}, u32[]{:S(2)}) collective-permute-start(bf16[16,32,128]{2,1,0:T(8,128)(2,1)S(1)} %level0_1.1.after.state_ref), channel_id=1, source_target_pairs={{0,2},{1,3},{2,0},{3,1},{4,6},{5,7},{6,4},{7,5},{8,10},{9,11},{10,... | collective-permute-start | bytes 393224 | tf_op jit(solution)/shard_map/ppermute | solution.py:476
  9.8 15.1 %collective-permute-start.6 = (bf16[16,64,128]{2,1,0:T(8,128)(2,1)S(1)}, bf16[16,64,128]{2,1,0:T(8,128)(2,1)S(1)}, u32[]{:S(2)}, u32[]{:S(2)}) collective-permute-start(bf16[16,64,128]{2,1,0:T(8,128)(2,1)S(1)} %get-tuple-element.27.cross_ref), channel_id=1, source_target_pairs={{0,8},{8,0},{16,24},{24,16},{1,9},{9,1},{17,25},{25,17},{2,10},{10... | collective-permute-start | bytes 786440 | tf_op jit(solution)/shard_map/ppermute | solution.py:476
  12.3 10.6 %collective-permute-start.3 = (bf16[16,32,128]{2,1,0:T(8,128)(2,1)S(1)}, bf16[16,32,128]{2,1,0:T(8,128)(2,1)S(1)}, u32[]{:S(2)}, u32[]{:S(2)}) collective-permute-start(bf16[16,32,128]{2,1,0:T(8,128)(2,1)S(1)} %level1_0.1.own_ref), channel_id=1, source_target_pairs={{0,4},{1,5},{2,6},{3,7},{4,0},{5,1},{6,2},{7,3},{8,12},{9,13},{10,... | collective-permute-start | bytes 393224 | tf_op jit(solution)/shard_map/ppermute | solution.py:476
  15.7 9.2 %collective-permute-start.4 = (bf16[16,32,128]{2,1,0:T(8,128)(2,1)S(1)}, bf16[16,32,128]{2,1,0:T(8,128)(2,1)S(1)}, u32[]{:S(2)}, u32[]{:S(2)}) collective-permute-start(bf16[16,32,128]{2,1,0:T(8,128)(2,1)S(1)} %get-tuple-element.29), channel_id=1, source_target_pairs={{0,8},{8,0},{16,24},{24,16},{1,9},{9,1},{17,25},{25,17},{2,10},{10... | collective-permute-start | bytes 393224 | tf_op jit(solution)/shard_map/ppermute | solution.py:476
  17.2 7.8 %collective-permute-start.8 = (bf16[16,16,128]{2,1,0:T(8,128)(2,1)S(1)}, bf16[16,16,128]{2,1,0:T(8,128)(2,1)S(1)}, u32[]{:S(2)}, u32[]{:S(2)}) collective-permute-start(bf16[16,16,128]{2,1,0:T(8,128)(2,1)S(1)} %get-tuple-element.32), channel_id=1, source_target_pairs={{0,12},{1,13},{2,14},{3,15},{4,8},{5,9},{6,10},{7,11},{8,4},{9,5},... | collective-permute-start | bytes 196616 | tf_op jit(solution)/shard_map/ppermute | solution.py:483
  20.8 6.1 %collective-permute-start.5 = (bf16[16,16,128]{2,1,0:T(8,128)(2,1)S(1)}, bf16[16,16,128]{2,1,0:T(8,128)(2,1)S(1)}, u32[]{:S(2)}, u32[]{:S(2)}) collective-permute-start(bf16[16,16,128]{2,1,0:T(8,128)(2,1)S(1)} %late_columns.1), channel_id=1, source_target_pairs={{0,12},{1,13},{2,14},{3,15},{4,8},{5,9},{6,10},{7,11},{8,4},{9,5},... | collective-permute-start | bytes 196616 | tf_op jit(solution)/shard_map/ppermute | solution.py:483
  23.4 4.3 %collective-permute-start.7 = (bf16[256,128]{1,0:T(8,128)(2,1)S(1)}, bf16[256,128]{1,0:T(8,128)(2,1)S(1)}, u32[]{:S(2)}, u32[]{:S(2)}) collective-permute-start(bf16[256,128]{1,0:T(8,128)(2,1)S(1)} %get-tuple-element.30), channel_id=1, source_target_pairs={{0,16},{8,24},{16,0},{24,8},{1,17},{9,25},{17,1},{25,9},{2,18},{10... | collective-permute-start | bytes 196616 | tf_op jit(solution)/shard_map/ppermute | solution.py:476
  25.3 4.3 %collective-permute-start.9 = (bf16[256,128]{1,0:T(8,128)(2,1)S(1)}, bf16[256,128]{1,0:T(8,128)(2,1)S(1)}, u32[]{:S(2)}, u32[]{:S(2)}) collective-permute-start(bf16[256,128]{1,0:T(8,128)(2,1)S(1)} %last_early.1), channel_id=1, source_target_pairs={{0,16},{8,24},{16,0},{24,8},{1,17},{9,25},{17,1},{25,9},{2,18},{10... | collective-permute-start | bytes 196616 | tf_op jit(solution)/shard_map/ppermute | solution.py:476

commit v3 on v2

--- a/solution.py
+++ b/solution.py
@@ -413,15 +413,15 @@
     place = place_ref[pl.ds(first, count)].reshape(count * here, slots)
     per = max(1, fields // 4)
     for column in range(columns):
-        for tile in range(degrees // 128):
-            span = slice(tile * 128, (tile + 1) * 128)
-            one = rows_ref[tile, pl.ds(column, count * here, stride=columns), :].astype(BF16)
-            natural = contract(one.T, place, ((1,), (0,))).astype(BF16)
-            where = (column // 2, column % 2, span)
-            if last:
-                natural = natural + so_far_ref[where]
-                natural = jnp.where(alive_ref[span] != 0, natural, jnp.zeros((), BF16))
-            natural_ref[where] = natural
+        tiles = [
+            rows_ref[tile, pl.ds(column, count * here, stride=columns), :].astype(BF16) for tile in range(degrees // 128)
+        ]
+        natural = contract(jnp.concatenate(tiles, axis=1).T, place, ((1,), (0,))).astype(BF16)
+        where = (column // 2, column % 2)
+        if last:
+            natural = natural + so_far_ref[where]
+            natural = jnp.where(alive_ref[...] != 0, natural, jnp.zeros((), BF16))
+        natural_ref[where] = natural
         if last and (column + 1) % (2 * per) == 0:
             done = column // (2 * per)
             where = pl.ds(done * per, per)

time: 31.5 us -> 31.5 us (level)
  no operation moved by 1% of the time
where the time goes in v3:
time: 31.5 us; the launch traced here: 31.3 us
  starting transfers between devices  15.4 us (49%)
  Pallas kernels  13.7 us (43%)
  waiting for transfers between devices  2.08 us (7%)
    ppermute x8, starting transfers between devices, swap(): lax.ppermute(array, axis, [(i, i ^ bits) for i in range(lax.axis_size(axi...  11.5 us
    ppermute x2, starting transfers between devices, swap_both(): return lax.ppermute(array, ('order', 'lat'), pairs)  3.89 us
    pallas_call x2, Pallas kernels, level_weights(): call(functools.partial(factor_kernel, levels, pieces, root_pieces), 'fact...  3.69 us
    pallas_call x2, Pallas kernels, spectra_of(): call(functools.partial(root_kernel, group, first, last), 'root', out, in_...  2.94 us
    pallas_call x4, Pallas kernels, next_states(): call(functools.partial(level_kernel, side, 'order'), name, [jax.ShapeDtyp...  2.14 us
    pallas_call x1, Pallas kernels, leaf_states(): call(functools.partial(leaf_kernel, pieces, group), 'leaf', [jax.ShapeDty...  1.92 us
    pallas_call x1, Pallas kernels, places_of(): call(functools.partial(place_kernel, group), 'places', [jax.ShapeDtypeStr...  1.78 us
    pallas_call x3, Pallas kernels, last_states(): call(functools.partial(last_level_kernel, turn, begin, 'order'), name, [j...  1.23 us
  transfers between devices with their start and end apart: 10, of which 3 were waited for; matrix products, arithmetic and copies ran while one was open for 0% of the time, Pallas kernels for 31%

profile of v3, /device:TPU:0, one launch (start us, length us, event | category | flops | bytes accessed | tf_op | source)
XLA Modules:
  0.0 31.3 jit_solution(15609322402410555321)
XLA Ops:
  0.0 1.9 %leaf.1 = (bf16[16,2,32,128]{3,2,1,0:T(8,128)(2,1)S(1)}, bf16[32,64,256]{2,1,0:T(8,128)(2,1)S(1)}) custom-call(bf16[32,64,256]{2,1,0:T(8,128)(2,1)} %fourier_hbm.1, f32[1,256]{1,0:T(1,128)} %bitcast.4, bf16[32,64,256]{2,1,0:T(8,128)(2,1)} %leaf_hbm.1, bf16[128,64,256]{2,1,0:T(8,128)(2,1)} %root_hbm.3), custom_call_target="tpu_custom_call" | custom-call | flops 67108 | bytes 2097 | tf_op jit(solution)/shard_map/leaf/pallas_call | solution.py:92
  1.9 0.5 %collective-permute-start = (bf16[16,2,32,128]{3,2,1,0:T(8,128)(2,1)S(1)}, bf16[16,2,32,128]{3,2,1,0:T(8,128)(2,1)S(1)}, u32[]{:S(2)}, u32[]{:S(2)}) collective-permute-start(bf16[16,2,32,128]{3,2,1,0:T(8,128)(2,1)S(1)} %get-tuple-element.19.after.state_ref), channel_id=1, source_target_pairs={{0,1},{1,0},{2,3},{3,2},{4,5},{5,4},{6,7},{7,6},{8,9},{9,8},{10,11... | collective-permute-start | bytes 786440 | tf_op jit(solution)/shard_map/ppermute | solution.py:476
  2.5 1.4 %factors.2.weight_ref = bf16[16,128,256]{2,1,0:T(8,128)(2,1)S(1)} custom-call(bf16[32,3,2,1,64,64]{5,4,3,2,1,0:T(8,128)(2,1)} %factor_hbm.3, s32[3,1,32]{2,1,0:T(1,128)} %bitcast.2, bf16[16,2,32,128]{3,2,1,0:T(8,128)(2,1)S(1)} %get-tuple-element.19.after.state_ref), custom_call_target="tpu_custom_call" | custom-call | flops 524 | bytes 2097 | tf_op jit(solution)/shard_map/factors/pallas_call | solution.py:167
  3.9 0.0 collective-permute-done.partner_ref
  3.9 0.4 %level0_0.1.state_ref = bf16[16,32,128]{2,1,0:T(8,128)(2,1)S(1)} custom-call(bf16[16,2,32,128]{3,2,1,0:T(8,128)(2,1)S(1)} %get-tuple-element.19.after.state_ref, bf16[16,2,32,128]{3,2,1,0:T(8,128)(2,1)S(1)} %collective-permute-done.partner_ref, bf16[16,128,256]{2,1,0:T(8,128)(2,1)S(1)} %factors.2.weight_ref), custom_call_target="tpu_custom_call" | custom-call | flops 33554 | bytes 393 | tf_op jit(solution)/shard_map/level0_0/pallas_call | solution.py:218
  4.4 2.7 %collective-permute-start.2 = (bf16[16,32,128]{2,1,0:T(8,128)(2,1)S(1)}, bf16[16,32,128]{2,1,0:T(8,128)(2,1)S(1)}, u32[]{:S(2)}, u32[]{:S(2)}) collective-permute-start(bf16[16,32,128]{2,1,0:T(8,128)(2,1)S(1)} %level0_0.1.state_ref), channel_id=1, source_target_pairs={{0,2},{1,3},{2,0},{3,1},{4,6},{5,7},{6,4},{7,5},{8,10},{9,11},{10,... | collective-permute-start | bytes 393224 | tf_op jit(solution)/shard_map/ppermute | solution.py:476
  7.0 0.4 %level0_1.1.after.state_ref = bf16[16,32,128]{2,1,0:T(8,128)(2,1)S(1)} custom-call(bf16[16,2,32,128]{3,2,1,0:T(8,128)(2,1)S(1)} %get-tuple-element.19.after.state_ref, bf16[16,2,32,128]{3,2,1,0:T(8,128)(2,1)S(1)} %collective-permute-done.partner_ref, bf16[16,128,256]{2,1,0:T(8,128)(2,1)S(1)} %factors.2.weight_ref), custom_call_target="tpu_custom_call" | custom-call | flops 33554 | bytes 393 | tf_op jit(solution)/shard_map/level0_1/pallas_call | solution.py:218
  7.5 0.0 copy-start
  7.5 0.1 collective-permute-start.1
  7.6 2.3 %factors.3 = (bf16[16,128,256]{2,1,0:T(8,128)(2,1)S(1)}, bf16[16,64,128]{2,1,0:T(8,128)(2,1)S(1)}, bf16[16,64,128]{2,1,0:T(8,128)(2,1)S(1)}, bf16[2,32,64,256]{3,2,1,0:T(8,128)(2,1)S(1)}) custom-call(bf16[32,3,2,1,64,64]{5,4,3,2,1,0:T(8,128)(2,1)} %factor_hbm.3, s32[3,1,32]{2,1,0:T(1,128)} %bitcast.3, bf16[16,32,128]{2,1,0:T(8,128)(2,1)S(1)} %level0_1.1.after.state_ref, ...), custom_call_target="tpu_custom_call" | custom-call | flops 1048 | bytes 4194 | tf_op jit(solution)/shard_map/factors/pallas_call | solution.py:167
  9.8 2.0 %collective-permute-start.6 = (bf16[16,64,128]{2,1,0:T(8,128)(2,1)S(1)}, bf16[16,64,128]{2,1,0:T(8,128)(2,1)S(1)}, u32[]{:S(2)}, u32[]{:S(2)}) collective-permute-start(bf16[16,64,128]{2,1,0:T(8,128)(2,1)S(1)} %get-tuple-element.27.cross_ref), channel_id=1, source_target_pairs={{0,8},{8,0},{16,24},{24,16},{1,9},{9,1},{17,25},{25,17},{2,10},{10... | collective-permute-start | bytes 786440 | tf_op jit(solution)/shard_map/ppermute | solution.py:476
  11.8 0.0 collective-permute-done.2.partner_ref
  11.8 0.4 %level1_0.1.own_ref = bf16[16,32,128]{2,1,0:T(8,128)(2,1)S(1)} custom-call(bf16[16,32,128]{2,1,0:T(8,128)(2,1)S(1)} %level0_0.1.state_ref, bf16[16,32,128]{2,1,0:T(8,128)(2,1)S(1)} %collective-permute-done.2.partner_ref, bf16[16,128,256]{2,1,0:T(8,128)(2,1)S(1)} %get-tuple-element.20.weight_ref), custom_call_target="tpu_custom_call" | custom-call | flops 33554 | bytes 393 | tf_op jit(solution)/shard_map/level1_0/pallas_call | solution.py:218
  12.3 2.6 %collective-permute-start.3 = (bf16[16,32,128]{2,1,0:T(8,128)(2,1)S(1)}, bf16[16,32,128]{2,1,0:T(8,128)(2,1)S(1)}, u32[]{:S(2)}, u32[]{:S(2)}) collective-permute-start(bf16[16,32,128]{2,1,0:T(8,128)(2,1)S(1)} %level1_0.1.own_ref), channel_id=1, source_target_pairs={{0,4},{1,5},{2,6},{3,7},{4,0},{5,1},{6,2},{7,3},{8,12},{9,13},{10,... | collective-permute-start | bytes 393224 | tf_op jit(solution)/shard_map/ppermute | solution.py:476
  14.9 0.0 collective-permute-done.1.partner_ref
  14.9 0.8 %level1_1.1 = (bf16[16,32,128]{2,1,0:T(8,128)(2,1)S(1)}, bf16[16,16,128]{2,1,0:T(8,128)(2,1)S(1)}, bf16[16,32,128]{2,1,0:T(8,128)(2,1)S(1)}) custom-call(bf16[16,32,128]{2,1,0:T(8,128)(2,1)S(1)} %level0_1.1.after.state_ref, bf16[16,32,128]{2,1,0:T(8,128)(2,1)S(1)} %collective-permute-done.1.partner_ref, ...), custom_call_target="tpu_custom_call" | custom-call | flops 33554 | bytes 393 | tf_op jit(solution)/shard_map/level1_1/pallas_call | solution.py:218
  15.7 1.4 %collective-permute-start.4 = (bf16[16,32,128]{2,1,0:T(8,128)(2,1)S(1)}, bf16[16,32,128]{2,1,0:T(8,128)(2,1)S(1)}, u32[]{:S(2)}, u32[]{:S(2)}) collective-permute-start(bf16[16,32,128]{2,1,0:T(8,128)(2,1)S(1)} %get-tuple-element.29), channel_id=1, source_target_pairs={{0,8},{8,0},{16,24},{24,16},{1,9},{9,1},{17,25},{25,17},{2,10},{10... | collective-permute-start | bytes 393224 | tf_op jit(solution)/shard_map/ppermute | solution.py:476
  17.2 1.8 %collective-permute-start.8 = (bf16[16,16,128]{2,1,0:T(8,128)(2,1)S(1)}, bf16[16,16,128]{2,1,0:T(8,128)(2,1)S(1)}, u32[]{:S(2)}, u32[]{:S(2)}) collective-permute-start(bf16[16,16,128]{2,1,0:T(8,128)(2,1)S(1)} %get-tuple-element.32), channel_id=1, source_target_pairs={{0,12},{1,13},{2,14},{3,15},{4,8},{5,9},{6,10},{7,11},{8,4},{9,5},... | collective-permute-start | bytes 196616 | tf_op jit(solution)/shard_map/ppermute | solution.py:483
  19.0 0.0 copy-done
  19.0 1.8 %places.1 = (bf16[4,32,128]{2,1,0:T(8,128)(2,1)S(1)}, bf16[256,128]{1,0:T(8,128)(2,1)S(1)}, bf16[1,32,64,256]{3,2,1,0:T(8,128)(2,1)S(1)}) custom-call(s32[128]{0:T(128)S(1)} %copy-done, bf16[16,32,128]{2,1,0:T(8,128)(2,1)S(1)} %get-tuple-element.22.after.state_ref, bf16[128,64,256]{2,1,0:T(8,128)(2,1)} %root_hbm.3), custom_call_target="tpu_custom_call" | custom-call | flops 16 | bytes 131 | tf_op jit(solution)/shard_map/places/pallas_call | solution.py:358
  20.8 2.1 %collective-permute-start.5 = (bf16[16,16,128]{2,1,0:T(8,128)(2,1)S(1)}, bf16[16,16,128]{2,1,0:T(8,128)(2,1)S(1)}, u32[]{:S(2)}, u32[]{:S(2)}) collective-permute-start(bf16[16,16,128]{2,1,0:T(8,128)(2,1)S(1)} %late_columns.1), channel_id=1, source_target_pairs={{0,12},{1,13},{2,14},{3,15},{4,8},{5,9},{6,10},{7,11},{8,4},{9,5},... | collective-permute-start | bytes 196616 | tf_op jit(solution)/shard_map/ppermute | solution.py:483
  22.9 0.0 collective-permute-done.3.partner_ref
  22.9 0.5 %last_own.1 = (bf16[256,128]{1,0:T(8,128)(2,1)S(1)}, bf16[256,128]{1,0:T(8,128)(2,1)S(1)}) custom-call(bf16[256,128]{1,0:T(8,128)(2,1)S(1)} %get-tuple-element.24.after.refs_1_.refs_2_, bf16[16,32,128]{2,1,0:T(8,128)(2,1)S(1)} %level1_0.1.own_ref, bf16[16,32,128]{2,1,0:T(8,128)(2,1)S(1)} %collective-permute-done.3.partner_ref, ...), custom_call_target="tpu_custom_call" | custom-call | flops 33554 | bytes 393 | tf_op jit(solution)/shard_map/last_own/pallas_call | solution.py:316
  23.4 1.6 %collective-permute-start.7 = (bf16[256,128]{1,0:T(8,128)(2,1)S(1)}, bf16[256,128]{1,0:T(8,128)(2,1)S(1)}, u32[]{:S(2)}, u32[]{:S(2)}) collective-permute-start(bf16[256,128]{1,0:T(8,128)(2,1)S(1)} %get-tuple-element.30), channel_id=1, source_target_pairs={{0,16},{8,24},{16,0},{24,8},{1,17},{9,25},{17,1},{25,9},{2,18},{10... | collective-permute-start | bytes 196616 | tf_op jit(solution)/shard_map/ppermute | solution.py:476
  24.9 0.0 collective-permute-done.8.partner_ref
  24.9 0.0 collective-permute-done.4.own_ref
  25.0 0.0 collective-permute-done.6.cross_ref
  25.0 0.4 %last_early.1 = bf16[256,128]{1,0:T(8,128)(2,1)S(1)} custom-call(bf16[256,128]{1,0:T(8,128)(2,1)S(1)} %get-tuple-element.24.after.refs_1_.refs_2_, bf16[16,32,128]{2,1,0:T(8,128)(2,1)S(1)} %collective-permute-done.4.own_ref, bf16[16,16,128]{2,1,0:T(8,128)(2,1)S(1)} %collective-permute-done.8.partner_ref, ...), custom_call_target="tpu_custom_call" | custom-call | flops 16777 | bytes 196 | tf_op jit(solution)/shard_map/last_early/pallas_call | solution.py:316
  25.3 0.5 %collective-permute-start.9 = (bf16[256,128]{1,0:T(8,128)(2,1)S(1)}, bf16[256,128]{1,0:T(8,128)(2,1)S(1)}, u32[]{:S(2)}, u32[]{:S(2)}) collective-permute-start(bf16[256,128]{1,0:T(8,128)(2,1)S(1)} %last_early.1), channel_id=1, source_target_pairs={{0,16},{8,24},{16,0},{24,8},{1,17},{9,25},{17,1},{25,9},{2,18},{10... | collective-permute-start | bytes 196616 | tf_op jit(solution)/shard_map/ppermute | solution.py:476
  25.9 1.1 %collective-permute-done.5.partner_ref = bf16[16,16,128]{2,1,0:T(8,128)(2,1)S(1)} collective-permute-done((bf16[16,16,128]{2,1,0:T(8,128)(2,1)S(1)}, bf16[16,16,128]{2,1,0:T(8,128)(2,1)S(1)}, u32[]{:S(2)}, u32[]{:S(2)}) %collective-permute-start.5) | collective-permute-done | bytes 65568 | tf_op jit(solution)/shard_map/ppermute | solution.py:483
  27.0 0.4 %last_late.1.refs_5_ = bf16[256,128]{1,0:T(8,128)(2,1)S(1)} custom-call(bf16[256,128]{1,0:T(8,128)(2,1)S(1)} %get-tuple-element.24.after.refs_1_.refs_2_, bf16[16,32,128]{2,1,0:T(8,128)(2,1)S(1)} %collective-permute-done.4.own_ref, bf16[16,16,128]{2,1,0:T(8,128)(2,1)S(1)} %collective-permute-done.5.partner_ref, ...), custom_call_target="tpu_custom_call" | custom-call | flops 16777 | bytes 196 | tf_op jit(solution)/shard_map/last_late/pallas_call | solution.py:316
  27.3 0.4 %collective-permute-done.7.refs_6_ = bf16[256,128]{1,0:T(8,128)(2,1)S(1)} collective-permute-done((bf16[256,128]{1,0:T(8,128)(2,1)S(1)}, bf16[256,128]{1,0:T(8,128)(2,1)S(1)}, u32[]{:S(2)}, u32[]{:S(2)}) %collective-permute-start.7) | collective-permute-done | bytes 65568 | tf_op jit(solution)/shard_map/ppermute | solution.py:476
  27.7 1.3 %root.2.refs_0_ = bf16[8,2,256,128]{3,2,1,0:T(8,128)(2,1)S(1)} custom-call(bf16[4,32,128]{2,1,0:T(8,128)(2,1)S(1)} %get-tuple-element.23.refs_0_.refs_1_, bf16[256,128]{1,0:T(8,128)(2,1)S(1)} %get-tuple-element.24.after.refs_1_.refs_2_, bf16[32,64,256]{2,1,0:T(8,128)(2,1)S(1)} %get-tuple-element.25.refs_2_, ...), custom_call_target="tpu_custom_call" | custom-call | flops 50331 | bytes 3145 | tf_op jit(solution)/shard_map/root/pallas_call | solution.py:451
  29.0 0.6 %collective-permute-done.9.refs_4_ = bf16[256,128]{1,0:T(8,128)(2,1)S(1)} collective-permute-done((bf16[256,128]{1,0:T(8,128)(2,1)S(1)}, bf16[256,128]{1,0:T(8,128)(2,1)S(1)}, u32[]{:S(2)}, u32[]{:S(2)}) %collective-permute-start.9) | collective-permute-done | bytes 65568 | tf_op jit(solution)/shard_map/ppermute | solution.py:476
  29.6 1.6 %root.3 = bf16[8,2,256,128]{3,2,1,0:T(8,128)(2,1)} custom-call(bf16[8,2,256,128]{3,2,1,0:T(8,128)(2,1)S(1)} %root.2.refs_0_, bf16[4,32,128]{2,1,0:T(8,128)(2,1)S(1)} %get-tuple-element.23.refs_0_.refs_1_, bf16[256,128]{1,0:T(8,128)(2,1)S(1)} %get-tuple-element.24.after.refs_1_.refs_2_, bf16[1,32,64,256]{3,2,1,0:T(8,128)(2,1)S(1)} %get-tuple-element.31.refs_3_, ...), custom_call_target="tpu_custom_call" | custom-call | flops 16777 | bytes 1048 | tf_op jit(solution)/shard_map/root/pallas_call | solution.py:451
  (1 shorter events, 0.0 us)
Async XLA Ops:
  1.9 2.0 %collective-permute-start = (bf16[16,2,32,128]{3,2,1,0:T(8,128)(2,1)S(1)}, bf16[16,2,32,128]{3,2,1,0:T(8,128)(2,1)S(1)}, u32[]{:S(2)}, u32[]{:S(2)}) collective-permute-start(bf16[16,2,32,128]{3,2,1,0:T(8,128)(2,1)S(1)} %get-tuple-element.19.after.state_ref), channel_id=1, source_target_pairs={{0,1},{1,0},{2,3},{3,2},{4,5},{5,4},{6,7},{7,6},{8,9},{9,8},{10,11... | collective-permute-start | bytes 786440 | tf_op jit(solution)/shard_map/ppermute | solution.py:476
  4.4 7.5 %collective-permute-start.2 = (bf16[16,32,128]{2,1,0:T(8,128)(2,1)S(1)}, bf16[16,32,128]{2,1,0:T(8,128)(2,1)S(1)}, u32[]{:S(2)}, u32[]{:S(2)}) collective-permute-start(bf16[16,32,128]{2,1,0:T(8,128)(2,1)S(1)} %level0_0.1.state_ref), channel_id=1, source_target_pairs={{0,2},{1,3},{2,0},{3,1},{4,6},{5,7},{6,4},{7,5},{8,10},{9,11},{10,... | collective-permute-start | bytes 393224 | tf_op jit(solution)/shard_map/ppermute | solution.py:476
  7.5 11.5 %copy-start = (s32[128]{0:T(128)S(1)}, s32[128]{0:T(128)}, u32[]{:S(2)}) copy-start(s32[128]{0:T(128)} %order_ref.1) | copy-start | bytes 1540
  7.5 7.4 %collective-permute-start.1 = (bf16[16,32,128]{2,1,0:T(8,128)(2,1)S(1)}, bf16[16,32,128]{2,1,0:T(8,128)(2,1)S(1)}, u32[]{:S(2)}, u32[]{:S(2)}) collective-permute-start(bf16[16,32,128]{2,1,0:T(8,128)(2,1)S(1)} %level0_1.1.after.state_ref), channel_id=1, source_target_pairs={{0,2},{1,3},{2,0},{3,1},{4,6},{5,7},{6,4},{7,5},{8,10},{9,11},{10,... | collective-permute-start | bytes 393224 | tf_op jit(solution)/shard_map/ppermute | solution.py:476
  9.8 15.1 %collective-permute-start.6 = (bf16[16,64,128]{2,1,0:T(8,128)(2,1)S(1)}, bf16[16,64,128]{2,1,0:T(8,128)(2,1)S(1)}, u32[]{:S(2)}, u32[]{:S(2)}) collective-permute-start(bf16[16,64,128]{2,1,0:T(8,128)(2,1)S(1)} %get-tuple-element.27.cross_ref), channel_id=1, source_target_pairs={{0,8},{8,0},{16,24},{24,16},{1,9},{9,1},{17,25},{25,17},{2,10},{10... | collective-permute-start | bytes 786440 | tf_op jit(solution)/shard_map/ppermute | solution.py:476
  12.3 10.6 %collective-permute-start.3 = (bf16[16,32,128]{2,1,0:T(8,128)(2,1)S(1)}, bf16[16,32,128]{2,1,0:T(8,128)(2,1)S(1)}, u32[]{:S(2)}, u32[]{:S(2)}) collective-permute-start(bf16[16,32,128]{2,1,0:T(8,128)(2,1)S(1)} %level1_0.1.own_ref), channel_id=1, source_target_pairs={{0,4},{1,5},{2,6},{3,7},{4,0},{5,1},{6,2},{7,3},{8,12},{9,13},{10,... | collective-permute-start | bytes 393224 | tf_op jit(solution)/shard_map/ppermute | solution.py:476
  15.7 9.2 %collective-permute-start.4 = (bf16[16,32,128]{2,1,0:T(8,128)(2,1)S(1)}, bf16[16,32,128]{2,1,0:T(8,128)(2,1)S(1)}, u32[]{:S(2)}, u32[]{:S(2)}) collective-permute-start(bf16[16,32,128]{2,1,0:T(8,128)(2,1)S(1)} %get-tuple-element.29), channel_id=1, source_target_pairs={{0,8},{8,0},{16,24},{24,16},{1,9},{9,1},{17,25},{25,17},{2,10},{10... | collective-permute-start | bytes 393224 | tf_op jit(solution)/shard_map/ppermute | solution.py:476
  17.2 7.8 %collective-permute-start.8 = (bf16[16,16,128]{2,1,0:T(8,128)(2,1)S(1)}, bf16[16,16,128]{2,1,0:T(8,128)(2,1)S(1)}, u32[]{:S(2)}, u32[]{:S(2)}) collective-permute-start(bf16[16,16,128]{2,1,0:T(8,128)(2,1)S(1)} %get-tuple-element.32), channel_id=1, source_target_pairs={{0,12},{1,13},{2,14},{3,15},{4,8},{5,9},{6,10},{7,11},{8,4},{9,5},... | collective-permute-start | bytes 196616 | tf_op jit(solution)/shard_map/ppermute | solution.py:483
  20.8 6.1 %collective-permute-start.5 = (bf16[16,16,128]{2,1,0:T(8,128)(2,1)S(1)}, bf16[16,16,128]{2,1,0:T(8,128)(2,1)S(1)}, u32[]{:S(2)}, u32[]{:S(2)}) collective-permute-start(bf16[16,16,128]{2,1,0:T(8,128)(2,1)S(1)} %late_columns.1), channel_id=1, source_target_pairs={{0,12},{1,13},{2,14},{3,15},{4,8},{5,9},{6,10},{7,11},{8,4},{9,5},... | collective-permute-start | bytes 196616 | tf_op jit(solution)/shard_map/ppermute | solution.py:483
  23.4 4.3 %collective-permute-start.7 = (bf16[256,128]{1,0:T(8,128)(2,1)S(1)}, bf16[256,128]{1,0:T(8,128)(2,1)S(1)}, u32[]{:S(2)}, u32[]{:S(2)}) collective-permute-start(bf16[256,128]{1,0:T(8,128)(2,1)S(1)} %get-tuple-element.30), channel_id=1, source_target_pairs={{0,16},{8,24},{16,0},{24,8},{1,17},{9,25},{17,1},{25,9},{2,18},{10... | collective-permute-start | bytes 196616 | tf_op jit(solution)/shard_map/ppermute | solution.py:476
  25.3 4.3 %collective-permute-start.9 = (bf16[256,128]{1,0:T(8,128)(2,1)S(1)}, bf16[256,128]{1,0:T(8,128)(2,1)S(1)}, u32[]{:S(2)}, u32[]{:S(2)}) collective-permute-start(bf16[256,128]{1,0:T(8,128)(2,1)S(1)} %last_early.1), channel_id=1, source_target_pairs={{0,16},{8,24},{16,0},{24,8},{1,17},{9,25},{17,1},{25,9},{2,18},{10... | collective-permute-start | bytes 196616 | tf_op jit(solution)/shard_map/ppermute | solution.py:476

commit v4 on v3

--- a/solution.py
+++ b/solution.py
@@ -183,6 +183,27 @@
         ],
         mib=24,
     )(level_factors, present, after, *([root_basis] if roots else []))
+
+
+def first_level_kernel(state_ref, partner_ref, weight_ref, *out_refs):
+    pairs, sides, rows, lanes = state_ref.shape
+    for pair in range(pairs):
+        both = [ref[pair].reshape(sides * rows, lanes) for ref in (state_ref, partner_ref)]
+        result = contract(jnp.concatenate(both, axis=1), weight_ref[pair], ((1,), (1,))).astype(BF16)
+        for side, out_ref in enumerate(out_refs):
+            out_ref[pair] = result[side * rows : (side + 1) * rows]
+
+
+def first_states(state, partner, weights):
+    pairs, sides, rows, lanes = state.shape
+    return call(
+        first_level_kernel,
+        "level0",
+        [jax.ShapeDtypeStruct((pairs, rows, lanes), BF16)] * sides,
+        whole_blocks(3),
+        4 * pairs * sides * rows * lanes * lanes,
+        6 * pairs * sides * rows * lanes,
+    )(state, partner, weights)
 
 
 def level_kernel(side, axis, state_ref, partner_ref, weight_ref, *refs):
@@ -486,7 +507,7 @@
     state, root_0 = leaf_states(fourier, quad_weights, leaf_basis, root_basis, owners)
     partner = swap(state, "lat", 1)
     weights = level_weights(level_factors, present, (0,), state)
-    states = [next_states(f"level0_{c}", state, partner, weights[0], c) for c in range(2)]
+    states = first_states(state, partner, weights[0])
     weights += level_weights(level_factors, present, tuple(range(1, levels)), states[1], root_basis, early_pieces - 1)
     own_factors, cross_factors, early_roots = weights[-3:]
     other_cross = swap(cross_factors, "order", 1)

time: 31.5 us -> 31.5 us (level)
  starting transfers between devices: 15.4 us -> 15.8 us
  Pallas kernels: 13.7 us -> 13.3 us
    pallas_call x4 -> x2, Pallas kernels: 2.14 us -> 1.26 us  [next_states(): call(functools.partial(level_kernel, side, 'order'), name, [jax.ShapeDtyp...]
    pallas_call x0 -> x1, Pallas kernels: none -> 0.48 us  [first_states(): call(first_level_kernel, 'level0', [jax.ShapeDtypeStruct((pairs, rows, la...]
    ppermute x8, starting transfers between devices: 11.5 us -> 11.9 us  [swap(): lax.ppermute(array, axis, [(i, i ^ bits) for i in range(lax.axis_size(axi...]
  transfers between devices with their start and end apart: 10 -> 10, of which waited for: 3 -> 4; matrix products, arithmetic and copies ran while one was open for 0% -> 0% of each run, Pallas kernels for 31% -> 30%
where the time goes in v4:
time: 31.5 us; the launch traced here: 31.3 us
  starting transfers between devices  15.8 us (50%)
  Pallas kernels  13.3 us (42%)
  waiting for transfers between devices  2.17 us (7%)
    ppermute x8, starting transfers between devices, swap(): lax.ppermute(array, axis, [(i, i ^ bits) for i in range(lax.axis_size(axi...  11.9 us
    ppermute x2, starting transfers between devices, swap_both(): return lax.ppermute(array, ('order', 'lat'), pairs)  3.89 us
    pallas_call x2, Pallas kernels, level_weights(): call(functools.partial(factor_kernel, levels, pieces, root_pieces), 'fact...  3.68 us
    pallas_call x2, Pallas kernels, spectra_of(): call(functools.partial(root_kernel, group, first, last), 'root', out, in_...  2.94 us
    pallas_call x1, Pallas kernels, leaf_states(): call(functools.partial(leaf_kernel, pieces, group), 'leaf', [jax.ShapeDty...  1.92 us
    pallas_call x1, Pallas kernels, places_of(): call(functools.partial(place_kernel, group), 'places', [jax.ShapeDtypeStr...  1.78 us
    pallas_call x2, Pallas kernels, next_states(): call(functools.partial(level_kernel, side, 'order'), name, [jax.ShapeDtyp...  1.26 us
    pallas_call x3, Pallas kernels, last_states(): call(functools.partial(last_level_kernel, turn, begin, 'order'), name, [j...  1.23 us
  transfers between devices with their start and end apart: 10, of which 4 were waited for; matrix products, arithmetic and copies ran while one was open for 0% of the time, Pallas kernels for 30%

profile of v4, /device:TPU:0, one launch (start us, length us, event | category | flops | bytes accessed | tf_op | source)
XLA Modules:
  0.0 31.3 jit_solution(14453412266786772155)
XLA Ops:
  0.0 1.9 %leaf.1 = (bf16[16,2,32,128]{3,2,1,0:T(8,128)(2,1)S(1)}, bf16[32,64,256]{2,1,0:T(8,128)(2,1)S(1)}) custom-call(bf16[32,64,256]{2,1,0:T(8,128)(2,1)} %fourier_hbm.1, f32[1,256]{1,0:T(1,128)} %bitcast.4, bf16[32,64,256]{2,1,0:T(8,128)(2,1)} %leaf_hbm.1, bf16[128,64,256]{2,1,0:T(8,128)(2,1)} %root_hbm.3), custom_call_target="tpu_custom_call" | custom-call | flops 67108 | bytes 2097 | tf_op jit(solution)/shard_map/leaf/pallas_call | solution.py:92
  1.9 0.5 %collective-permute-start = (bf16[16,2,32,128]{3,2,1,0:T(8,128)(2,1)S(1)}, bf16[16,2,32,128]{3,2,1,0:T(8,128)(2,1)S(1)}, u32[]{:S(2)}, u32[]{:S(2)}) collective-permute-start(bf16[16,2,32,128]{3,2,1,0:T(8,128)(2,1)S(1)} %get-tuple-element.21.after.state_ref), channel_id=1, source_target_pairs={{0,1},{1,0},{2,3},{3,2},{4,5},{5,4},{6,7},{7,6},{8,9},{9,8},{10,11... | collective-permute-start | bytes 786440 | tf_op jit(solution)/shard_map/ppermute | solution.py:497
  2.5 1.4 %factors.2.weight_ref = bf16[16,128,256]{2,1,0:T(8,128)(2,1)S(1)} custom-call(bf16[32,3,2,1,64,64]{5,4,3,2,1,0:T(8,128)(2,1)} %factor_hbm.3, s32[3,1,32]{2,1,0:T(1,128)} %bitcast.2, bf16[16,2,32,128]{3,2,1,0:T(8,128)(2,1)S(1)} %get-tuple-element.21.after.state_ref), custom_call_target="tpu_custom_call" | custom-call | flops 524 | bytes 2097 | tf_op jit(solution)/shard_map/factors/pallas_call | solution.py:167
  3.9 0.0 collective-permute-done.partner_ref
  3.9 0.5 %level0.1 = (bf16[16,32,128]{2,1,0:T(8,128)(2,1)S(1)}, bf16[16,32,128]{2,1,0:T(8,128)(2,1)S(1)}) custom-call(bf16[16,2,32,128]{3,2,1,0:T(8,128)(2,1)S(1)} %get-tuple-element.21.after.state_ref, bf16[16,2,32,128]{3,2,1,0:T(8,128)(2,1)S(1)} %collective-permute-done.partner_ref, bf16[16,128,256]{2,1,0:T(8,128)(2,1)S(1)} %factors.2.weight_ref), custom_call_target="tpu_custom_call" | custom-call | flops 67108 | bytes 786 | tf_op jit(solution)/shard_map/level0/pallas_call | solution.py:199
  4.4 2.7 %collective-permute-start.2 = (bf16[16,32,128]{2,1,0:T(8,128)(2,1)S(1)}, bf16[16,32,128]{2,1,0:T(8,128)(2,1)S(1)}, u32[]{:S(2)}, u32[]{:S(2)}) collective-permute-start(bf16[16,32,128]{2,1,0:T(8,128)(2,1)S(1)} %get-tuple-element.30.state_ref), channel_id=1, source_target_pairs={{0,2},{1,3},{2,0},{3,1},{4,6},{5,7},{6,4},{7,5},{8,10},{9,11},{10,... | collective-permute-start | bytes 393224 | tf_op jit(solution)/shard_map/ppermute | solution.py:497
  7.1 0.0 copy-start
  7.1 0.1 collective-permute-start.1
  7.2 2.2 %factors.3 = (bf16[16,128,256]{2,1,0:T(8,128)(2,1)S(1)}, bf16[16,64,128]{2,1,0:T(8,128)(2,1)S(1)}, bf16[16,64,128]{2,1,0:T(8,128)(2,1)S(1)}, bf16[2,32,64,256]{3,2,1,0:T(8,128)(2,1)S(1)}) custom-call(bf16[32,3,2,1,64,64]{5,4,3,2,1,0:T(8,128)(2,1)} %factor_hbm.3, s32[3,1,32]{2,1,0:T(1,128)} %bitcast.3, ...), custom_call_target="tpu_custom_call" | custom-call | flops 1048 | bytes 4194 | tf_op jit(solution)/shard_map/factors/pallas_call | solution.py:167
  9.4 1.9 %collective-permute-start.6 = (bf16[16,64,128]{2,1,0:T(8,128)(2,1)S(1)}, bf16[16,64,128]{2,1,0:T(8,128)(2,1)S(1)}, u32[]{:S(2)}, u32[]{:S(2)}) collective-permute-start(bf16[16,64,128]{2,1,0:T(8,128)(2,1)S(1)} %get-tuple-element.31.cross_ref), channel_id=1, source_target_pairs={{0,8},{8,0},{16,24},{24,16},{1,9},{9,1},{17,25},{25,17},{2,10},{10... | collective-permute-start | bytes 786440 | tf_op jit(solution)/shard_map/ppermute | solution.py:497
  11.4 0.1 collective-permute-done.2.partner_ref
  11.5 0.4 %level1_0.1.own_ref = bf16[16,32,128]{2,1,0:T(8,128)(2,1)S(1)} custom-call(bf16[16,32,128]{2,1,0:T(8,128)(2,1)S(1)} %get-tuple-element.30.state_ref, bf16[16,32,128]{2,1,0:T(8,128)(2,1)S(1)} %collective-permute-done.2.partner_ref, bf16[16,128,256]{2,1,0:T(8,128)(2,1)S(1)} %get-tuple-element.23.weight_ref), custom_call_target="tpu_custom_call" | custom-call | flops 33554 | bytes 393 | tf_op jit(solution)/shard_map/level1_0/pallas_call | solution.py:239
  11.9 3.0 %collective-permute-start.3 = (bf16[16,32,128]{2,1,0:T(8,128)(2,1)S(1)}, bf16[16,32,128]{2,1,0:T(8,128)(2,1)S(1)}, u32[]{:S(2)}, u32[]{:S(2)}) collective-permute-start(bf16[16,32,128]{2,1,0:T(8,128)(2,1)S(1)} %level1_0.1.own_ref), channel_id=1, source_target_pairs={{0,4},{1,5},{2,6},{3,7},{4,0},{5,1},{6,2},{7,3},{8,12},{9,13},{10,... | collective-permute-start | bytes 393224 | tf_op jit(solution)/shard_map/ppermute | solution.py:497
  14.9 0.0 collective-permute-done.1.partner_ref
  14.9 0.8 %level1_1.1 = (bf16[16,32,128]{2,1,0:T(8,128)(2,1)S(1)}, bf16[16,16,128]{2,1,0:T(8,128)(2,1)S(1)}, bf16[16,32,128]{2,1,0:T(8,128)(2,1)S(1)}) custom-call(bf16[16,32,128]{2,1,0:T(8,128)(2,1)S(1)} %get-tuple-element.22.after.state_ref, bf16[16,32,128]{2,1,0:T(8,128)(2,1)S(1)} %collective-permute-done.1.partner_ref, ...), custom_call_target="tpu_custom_call" | custom-call | flops 33554 | bytes 393 | tf_op jit(solution)/shard_map/level1_1/pallas_call | solution.py:239
  15.7 1.5 %collective-permute-start.4 = (bf16[16,32,128]{2,1,0:T(8,128)(2,1)S(1)}, bf16[16,32,128]{2,1,0:T(8,128)(2,1)S(1)}, u32[]{:S(2)}, u32[]{:S(2)}) collective-permute-start(bf16[16,32,128]{2,1,0:T(8,128)(2,1)S(1)} %get-tuple-element.33), channel_id=1, source_target_pairs={{0,8},{8,0},{16,24},{24,16},{1,9},{9,1},{17,25},{25,17},{2,10},{10... | collective-permute-start | bytes 393224 | tf_op jit(solution)/shard_map/ppermute | solution.py:497
  17.2 1.9 %collective-permute-start.8 = (bf16[16,16,128]{2,1,0:T(8,128)(2,1)S(1)}, bf16[16,16,128]{2,1,0:T(8,128)(2,1)S(1)}, u32[]{:S(2)}, u32[]{:S(2)}) collective-permute-start(bf16[16,16,128]{2,1,0:T(8,128)(2,1)S(1)} %get-tuple-element.36), channel_id=1, source_target_pairs={{0,12},{1,13},{2,14},{3,15},{4,8},{5,9},{6,10},{7,11},{8,4},{9,5},... | collective-permute-start | bytes 196616 | tf_op jit(solution)/shard_map/ppermute | solution.py:504
  19.2 0.0 copy-done
  19.2 1.8 %places.1 = (bf16[4,32,128]{2,1,0:T(8,128)(2,1)S(1)}, bf16[256,128]{1,0:T(8,128)(2,1)S(1)}, bf16[1,32,64,256]{3,2,1,0:T(8,128)(2,1)S(1)}) custom-call(s32[128]{0:T(128)S(1)} %copy-done, bf16[16,32,128]{2,1,0:T(8,128)(2,1)S(1)} %get-tuple-element.25.after.state_ref, bf16[128,64,256]{2,1,0:T(8,128)(2,1)} %root_hbm.3), custom_call_target="tpu_custom_call" | custom-call | flops 16 | bytes 131 | tf_op jit(solution)/shard_map/places/pallas_call | solution.py:379
  21.0 1.9 %collective-permute-start.5 = (bf16[16,16,128]{2,1,0:T(8,128)(2,1)S(1)}, bf16[16,16,128]{2,1,0:T(8,128)(2,1)S(1)}, u32[]{:S(2)}, u32[]{:S(2)}) collective-permute-start(bf16[16,16,128]{2,1,0:T(8,128)(2,1)S(1)} %late_columns.1), channel_id=1, source_target_pairs={{0,12},{1,13},{2,14},{3,15},{4,8},{5,9},{6,10},{7,11},{8,4},{9,5},... | collective-permute-start | bytes 196616 | tf_op jit(solution)/shard_map/ppermute | solution.py:504
  22.9 0.0 collective-permute-done.3.partner_ref
  22.9 0.5 %last_own.1 = (bf16[256,128]{1,0:T(8,128)(2,1)S(1)}, bf16[256,128]{1,0:T(8,128)(2,1)S(1)}) custom-call(bf16[256,128]{1,0:T(8,128)(2,1)S(1)} %get-tuple-element.27.after.refs_1_.refs_2_, bf16[16,32,128]{2,1,0:T(8,128)(2,1)S(1)} %level1_0.1.own_ref, bf16[16,32,128]{2,1,0:T(8,128)(2,1)S(1)} %collective-permute-done.3.partner_ref, ...), custom_call_target="tpu_custom_call" | custom-call | flops 33554 | bytes 393 | tf_op jit(solution)/shard_map/last_own/pallas_call | solution.py:337
  23.4 1.6 %collective-permute-start.7 = (bf16[256,128]{1,0:T(8,128)(2,1)S(1)}, bf16[256,128]{1,0:T(8,128)(2,1)S(1)}, u32[]{:S(2)}, u32[]{:S(2)}) collective-permute-start(bf16[256,128]{1,0:T(8,128)(2,1)S(1)} %get-tuple-element.34), channel_id=1, source_target_pairs={{0,16},{8,24},{16,0},{24,8},{1,17},{9,25},{17,1},{25,9},{2,18},{10... | collective-permute-start | bytes 196616 | tf_op jit(solution)/shard_map/ppermute | solution.py:497
  25.0 0.0 collective-permute-done.8.partner_ref
  25.0 0.0 collective-permute-done.4.own_ref
  25.0 0.0 collective-permute-done.6.cross_ref
  25.0 0.4 %last_early.1 = bf16[256,128]{1,0:T(8,128)(2,1)S(1)} custom-call(bf16[256,128]{1,0:T(8,128)(2,1)S(1)} %get-tuple-element.27.after.refs_1_.refs_2_, bf16[16,32,128]{2,1,0:T(8,128)(2,1)S(1)} %collective-permute-done.4.own_ref, bf16[16,16,128]{2,1,0:T(8,128)(2,1)S(1)} %collective-permute-done.8.partner_ref, ...), custom_call_target="tpu_custom_call" | custom-call | flops 16777 | bytes 196 | tf_op jit(solution)/shard_map/last_early/pallas_call | solution.py:337
  25.4 0.6 %collective-permute-start.9 = (bf16[256,128]{1,0:T(8,128)(2,1)S(1)}, bf16[256,128]{1,0:T(8,128)(2,1)S(1)}, u32[]{:S(2)}, u32[]{:S(2)}) collective-permute-start(bf16[256,128]{1,0:T(8,128)(2,1)S(1)} %last_early.1), channel_id=1, source_target_pairs={{0,16},{8,24},{16,0},{24,8},{1,17},{9,25},{17,1},{25,9},{2,18},{10... | collective-permute-start | bytes 196616 | tf_op jit(solution)/shard_map/ppermute | solution.py:497
  25.9 1.2 %collective-permute-done.5.partner_ref = bf16[16,16,128]{2,1,0:T(8,128)(2,1)S(1)} collective-permute-done((bf16[16,16,128]{2,1,0:T(8,128)(2,1)S(1)}, bf16[16,16,128]{2,1,0:T(8,128)(2,1)S(1)}, u32[]{:S(2)}, u32[]{:S(2)}) %collective-permute-start.5) | collective-permute-done | bytes 65568 | tf_op jit(solution)/shard_map/ppermute | solution.py:504
  27.1 0.4 %last_late.1.refs_5_ = bf16[256,128]{1,0:T(8,128)(2,1)S(1)} custom-call(bf16[256,128]{1,0:T(8,128)(2,1)S(1)} %get-tuple-element.27.after.refs_1_.refs_2_, bf16[16,32,128]{2,1,0:T(8,128)(2,1)S(1)} %collective-permute-done.4.own_ref, bf16[16,16,128]{2,1,0:T(8,128)(2,1)S(1)} %collective-permute-done.5.partner_ref, ...), custom_call_target="tpu_custom_call" | custom-call | flops 16777 | bytes 196 | tf_op jit(solution)/shard_map/last_late/pallas_call | solution.py:337
  27.5 0.2 collective-permute-done.7.refs_6_
  27.8 1.3 %root.2.refs_0_ = bf16[8,2,256,128]{3,2,1,0:T(8,128)(2,1)S(1)} custom-call(bf16[4,32,128]{2,1,0:T(8,128)(2,1)S(1)} %get-tuple-element.26.refs_0_.refs_1_, bf16[256,128]{1,0:T(8,128)(2,1)S(1)} %get-tuple-element.27.after.refs_1_.refs_2_, bf16[32,64,256]{2,1,0:T(8,128)(2,1)S(1)} %get-tuple-element.28.refs_2_, ...), custom_call_target="tpu_custom_call" | custom-call | flops 50331 | bytes 3145 | tf_op jit(solution)/shard_map/root/pallas_call | solution.py:472
  29.1 0.6 %collective-permute-done.9.refs_4_ = bf16[256,128]{1,0:T(8,128)(2,1)S(1)} collective-permute-done((bf16[256,128]{1,0:T(8,128)(2,1)S(1)}, bf16[256,128]{1,0:T(8,128)(2,1)S(1)}, u32[]{:S(2)}, u32[]{:S(2)}) %collective-permute-start.9) | collective-permute-done | bytes 65568 | tf_op jit(solution)/shard_map/ppermute | solution.py:497
  29.7 1.6 %root.3 = bf16[8,2,256,128]{3,2,1,0:T(8,128)(2,1)} custom-call(bf16[8,2,256,128]{3,2,1,0:T(8,128)(2,1)S(1)} %root.2.refs_0_, bf16[4,32,128]{2,1,0:T(8,128)(2,1)S(1)} %get-tuple-element.26.refs_0_.refs_1_, bf16[256,128]{1,0:T(8,128)(2,1)S(1)} %get-tuple-element.27.after.refs_1_.refs_2_, bf16[1,32,64,256]{3,2,1,0:T(8,128)(2,1)S(1)} %get-tuple-element.35.refs_3_, ...), custom_call_target="tpu_custom_call" | custom-call | flops 16777 | bytes 1048 | tf_op jit(solution)/shard_map/root/pallas_call | solution.py:472
  (1 shorter events, 0.0 us)
Async XLA Ops:
  1.9 2.0 %collective-permute-start = (bf16[16,2,32,128]{3,2,1,0:T(8,128)(2,1)S(1)}, bf16[16,2,32,128]{3,2,1,0:T(8,128)(2,1)S(1)}, u32[]{:S(2)}, u32[]{:S(2)}) collective-permute-start(bf16[16,2,32,128]{3,2,1,0:T(8,128)(2,1)S(1)} %get-tuple-element.21.after.state_ref), channel_id=1, source_target_pairs={{0,1},{1,0},{2,3},{3,2},{4,5},{5,4},{6,7},{7,6},{8,9},{9,8},{10,11... | collective-permute-start | bytes 786440 | tf_op jit(solution)/shard_map/ppermute | solution.py:497
  4.4 7.1 %collective-permute-start.2 = (bf16[16,32,128]{2,1,0:T(8,128)(2,1)S(1)}, bf16[16,32,128]{2,1,0:T(8,128)(2,1)S(1)}, u32[]{:S(2)}, u32[]{:S(2)}) collective-permute-start(bf16[16,32,128]{2,1,0:T(8,128)(2,1)S(1)} %get-tuple-element.30.state_ref), channel_id=1, source_target_pairs={{0,2},{1,3},{2,0},{3,1},{4,6},{5,7},{6,4},{7,5},{8,10},{9,11},{10,... | collective-permute-start | bytes 393224 | tf_op jit(solution)/shard_map/ppermute | solution.py:497
  7.1 12.1 %copy-start = (s32[128]{0:T(128)S(1)}, s32[128]{0:T(128)}, u32[]{:S(2)}) copy-start(s32[128]{0:T(128)} %order_ref.1) | copy-start | bytes 1540
  7.1 7.8 %collective-permute-start.1 = (bf16[16,32,128]{2,1,0:T(8,128)(2,1)S(1)}, bf16[16,32,128]{2,1,0:T(8,128)(2,1)S(1)}, u32[]{:S(2)}, u32[]{:S(2)}) collective-permute-start(bf16[16,32,128]{2,1,0:T(8,128)(2,1)S(1)} %get-tuple-element.22.after.state_ref), channel_id=1, source_target_pairs={{0,2},{1,3},{2,0},{3,1},{4,6},{5,7},{6,4},{7,5},{8,10},{9,11},{10,... | collective-permute-start | bytes 393224 | tf_op jit(solution)/shard_map/ppermute | solution.py:497
  9.4 15.6 %collective-permute-start.6 = (bf16[16,64,128]{2,1,0:T(8,128)(2,1)S(1)}, bf16[16,64,128]{2,1,0:T(8,128)(2,1)S(1)}, u32[]{:S(2)}, u32[]{:S(2)}) collective-permute-start(bf16[16,64,128]{2,1,0:T(8,128)(2,1)S(1)} %get-tuple-element.31.cross_ref), channel_id=1, source_target_pairs={{0,8},{8,0},{16,24},{24,16},{1,9},{9,1},{17,25},{25,17},{2,10},{10... | collective-permute-start | bytes 786440 | tf_op jit(solution)/shard_map/ppermute | solution.py:497
  11.9 11.0 %collective-permute-start.3 = (bf16[16,32,128]{2,1,0:T(8,128)(2,1)S(1)}, bf16[16,32,128]{2,1,0:T(8,128)(2,1)S(1)}, u32[]{:S(2)}, u32[]{:S(2)}) collective-permute-start(bf16[16,32,128]{2,1,0:T(8,128)(2,1)S(1)} %level1_0.1.own_ref), channel_id=1, source_target_pairs={{0,4},{1,5},{2,6},{3,7},{4,0},{5,1},{6,2},{7,3},{8,12},{9,13},{10,... | collective-permute-start | bytes 393224 | tf_op jit(solution)/shard_map/ppermute | solution.py:497
  15.7 9.3 %collective-permute-start.4 = (bf16[16,32,128]{2,1,0:T(8,128)(2,1)S(1)}, bf16[16,32,128]{2,1,0:T(8,128)(2,1)S(1)}, u32[]{:S(2)}, u32[]{:S(2)}) collective-permute-start(bf16[16,32,128]{2,1,0:T(8,128)(2,1)S(1)} %get-tuple-element.33), channel_id=1, source_target_pairs={{0,8},{8,0},{16,24},{24,16},{1,9},{9,1},{17,25},{25,17},{2,10},{10... | collective-permute-start | bytes 393224 | tf_op jit(solution)/shard_map/ppermute | solution.py:497
  17.2 7.8 %collective-permute-start.8 = (bf16[16,16,128]{2,1,0:T(8,128)(2,1)S(1)}, bf16[16,16,128]{2,1,0:T(8,128)(2,1)S(1)}, u32[]{:S(2)}, u32[]{:S(2)}) collective-permute-start(bf16[16,16,128]{2,1,0:T(8,128)(2,1)S(1)} %get-tuple-element.36), channel_id=1, source_target_pairs={{0,12},{1,13},{2,14},{3,15},{4,8},{5,9},{6,10},{7,11},{8,4},{9,5},... | collective-permute-start | bytes 196616 | tf_op jit(solution)/shard_map/ppermute | solution.py:504
  21.0 6.1 %collective-permute-start.5 = (bf16[16,16,128]{2,1,0:T(8,128)(2,1)S(1)}, bf16[16,16,128]{2,1,0:T(8,128)(2,1)S(1)}, u32[]{:S(2)}, u32[]{:S(2)}) collective-permute-start(bf16[16,16,128]{2,1,0:T(8,128)(2,1)S(1)} %late_columns.1), channel_id=1, source_target_pairs={{0,12},{1,13},{2,14},{3,15},{4,8},{5,9},{6,10},{7,11},{8,4},{9,5},... | collective-permute-start | bytes 196616 | tf_op jit(solution)/shard_map/ppermute | solution.py:504
  23.4 4.3 %collective-permute-start.7 = (bf16[256,128]{1,0:T(8,128)(2,1)S(1)}, bf16[256,128]{1,0:T(8,128)(2,1)S(1)}, u32[]{:S(2)}, u32[]{:S(2)}) collective-permute-start(bf16[256,128]{1,0:T(8,128)(2,1)S(1)} %get-tuple-element.34), channel_id=1, source_target_pairs={{0,16},{8,24},{16,0},{24,8},{1,17},{9,25},{17,1},{25,9},{2,18},{10... | collective-permute-start | bytes 196616 | tf_op jit(solution)/shard_map/ppermute | solution.py:497
  25.4 4.3 %collective-permute-start.9 = (bf16[256,128]{1,0:T(8,128)(2,1)S(1)}, bf16[256,128]{1,0:T(8,128)(2,1)S(1)}, u32[]{:S(2)}, u32[]{:S(2)}) collective-permute-start(bf16[256,128]{1,0:T(8,128)(2,1)S(1)} %last_early.1), channel_id=1, source_target_pairs={{0,16},{8,24},{16,0},{24,8},{1,17},{9,25},{17,1},{25,9},{2,18},{10... | collective-permute-start | bytes 196616 | tf_op jit(solution)/shard_map/ppermute | solution.py:497

commit v5 on v4

--- a/solution.py
+++ b/solution.py
@@ -40,10 +40,11 @@
     return [pl.BlockSpec()] * count
 
 
-def fetch_roots(k, root_hbm, root_ref, sem):
-    here = root_ref.shape[0]
+def fetch_roots(k, root_hbm, root_ref, sem, here=None, begin=0):
+    size = root_ref.shape[0]
+    here = here or size
     me = lax.axis_index("order")
-    return pltpu.make_async_copy(root_hbm.at[pl.ds((me ^ k) * here, here)], root_ref, sem)
+    return pltpu.make_async_copy(root_hbm.at[pl.ds((me ^ k) * here + begin, size)], root_ref, sem)
 
 
 def leaf_kernel(
@@ -356,7 +357,7 @@
     degrees = alive_ref.shape[0]
     me = lax.axis_index("order")
     later = later_ref.shape[0]
-    fetches = [fetch_roots(owners - later + i, root_hbm, later_ref.at[i], sems.at[i]) for i in range(later)]
+    fetches = [fetch_roots(owners - later + i, root_hbm, later_ref.at[i], sems.at[i], here) for i in range(later)]
     for fetch in fetches:
         fetch.start()
     lane = lax.broadcasted_iota(jnp.int32, (1, slots), 1)
@@ -382,7 +383,7 @@
         [
             jax.ShapeDtypeStruct((owners, here, slots), BF16),
             jax.ShapeDtypeStruct((degrees, slots), BF16),
-            jax.ShapeDtypeStruct((later, here, rank, degrees), BF16),
+            jax.ShapeDtypeStruct((later, here // 2, rank, degrees), BF16),
         ],
         [IN_SMEM, ANYWHERE, IN_HBM],
         slots * slots,
@@ -398,20 +399,24 @@
     count = place_ref.shape[0] - first if last else first
     first = first if last else 0
     if last:
-        root_refs = [refs[0].at[i] for i in range(count)]
+        root_refs = [(refs[0].at[i], refs[1].at[i]) for i in range(count)]
     else:
-        root_refs = refs[:1] + [refs[1].at[i] for i in range(count - 1)]
-    refs = refs[1:] if last else refs[2:]
+        root_refs = [(ref,) for ref in refs[:1] + [refs[1].at[i] for i in range(count - 1)]]
+    refs = refs[2:]
     state_refs, refs = refs[:count], refs[count:]
     copies = []
     if last:
         out_ref, rows_ref, natural_ref, sems = refs
     else:
-        out_ref, rows_ref = refs
+        root_hbm, out_ref, later_ref, rows_ref, sems = refs
         natural_ref = out_ref
+        half = later_ref.shape[1]
+        for i in range(later_ref.shape[0]):
+            copies.append(fetch_roots(count + i, root_hbm, later_ref.at[i], sems.at[i], 2 * half, half))
+            copies[-1].start()
     fields, parts, degrees, slots = out_ref.shape
     columns = fields * parts
-    rank = root_refs[0].shape[1]
+    rank = root_refs[0][0].shape[1]
     group_rows = group * columns
     here = place_ref.shape[1]
     steps = state_refs[0].shape[0] // group_rows
@@ -426,7 +431,9 @@
             left = jnp.concatenate(
                 [jnp.concatenate([jnp.where(m, state, empty) for m in line], axis=1) for line in masks], axis=0
             )
-            right = root_refs[i][pl.ds(step * group * 2, group * 2)].reshape(group * 2 * rank, degrees)
+            halves = len(root_refs[i])
+            part, at = divmod(step, steps // halves)
+            right = root_refs[i][part][pl.ds(at * group * 2, group * 2)].reshape(group * 2 * rank, degrees)
             product = contract(left, right, ((1,), (0,)))
             begin = (i * steps + step) * 2 * group_rows
             for tile in range(degrees // 128):
@@ -452,7 +459,7 @@
         copy.wait()
 
 
-def spectra_of(states, roots, places, alive, so_far, first, group):
+def spectra_of(states, roots, places, alive, so_far, first, group, root_basis=None):
     state_rows = states[0].shape[0]
     rank, degrees = roots[0].shape[-2:]
     owners, here, slots = places.shape
@@ -469,6 +476,11 @@
         in_specs = whole_blocks(len(inputs))
         scratch += [pltpu.VMEM(out.shape, BF16), pltpu.SemaphoreType.DMA((columns // 2,))]
         more["out_specs"] = IN_HBM
+    else:
+        inputs.append(root_basis)
+        in_specs.append(IN_HBM)
+        out = [out, jax.ShapeDtypeStruct((owners - count, here // 2, rank, degrees), BF16)]
+        scratch.append(pltpu.SemaphoreType.DMA((owners - count,)))
     return call(
         functools.partial(root_kernel, group, first, last),
         "root",
@@ -535,8 +547,8 @@
     odd = [*last_states("last_late", alive, other_own, late_partner, (other_cross,), 1, False, begin), *odd]
     arrived = [swap((odd if k % 2 else even)[k // 2], "order", k // 2 * 2) if k > 1 else (even, odd)[k][0] for k in range(owners)]
     roots = [root_0, early_roots]
-    spectra = spectra_of(arrived[:early_pieces], roots, places, alive, None, early_pieces, group)
-    return spectra_of(arrived[early_pieces:], [later_roots], places, alive, spectra, early_pieces, group)
+    spectra, more_roots = spectra_of(arrived[:early_pieces], roots, places, alive, None, early_pieces, group, root_basis)
+    return spectra_of(arrived[early_pieces:], [later_roots, more_roots], places, alive, spectra, early_pieces, group)
 
 
 def solution(mesh):

time: 31.5 us -> 31.4 us (level)
  no operation moved by 1% of the time
where the time goes in v5:
time: 31.4 us; the launch traced here: 31.2 us
  starting transfers between devices  15.8 us (50%)
  Pallas kernels  13.4 us (43%)
  waiting for transfers between devices  1.87 us (6%)
    ppermute x8, starting transfers between devices, swap(): lax.ppermute(array, axis, [(i, i ^ bits) for i in range(lax.axis_size(axi...  11.9 us
    ppermute x2, starting transfers between devices, swap_both(): return lax.ppermute(array, ('order', 'lat'), pairs)  3.89 us
    pallas_call x2, Pallas kernels, level_weights(): call(functools.partial(factor_kernel, levels, pieces, root_pieces), 'fact...  3.68 us
    pallas_call x2, Pallas kernels, spectra_of(): call(functools.partial(root_kernel, group, first, last), 'root', out, in_...  3.24 us
    pallas_call x1, Pallas kernels, leaf_states(): call(functools.partial(leaf_kernel, pieces, group), 'leaf', [jax.ShapeDty...  1.92 us
    pallas_call x1, Pallas kernels, places_of(): call(functools.partial(place_kernel, group), 'places', [jax.ShapeDtypeStr...  1.6 us
    pallas_call x2, Pallas kernels, next_states(): call(functools.partial(level_kernel, side, 'order'), name, [jax.ShapeDtyp...  1.26 us
    pallas_call x3, Pallas kernels, last_states(): call(functools.partial(last_level_kernel, turn, begin, 'order'), name, [j...  1.23 us
  transfers between devices with their start and end apart: 10, of which 4 were waited for; matrix products, arithmetic and copies ran while one was open for 0% of the time, Pallas kernels for 30%

profile of v5, /device:TPU:0, one launch (start us, length us, event | category | flops | bytes accessed | tf_op | source)
XLA Modules:
  0.0 31.2 jit_solution(5784098994797156854)
XLA Ops:
  0.0 1.9 %leaf.1 = (bf16[16,2,32,128]{3,2,1,0:T(8,128)(2,1)S(1)}, bf16[32,64,256]{2,1,0:T(8,128)(2,1)S(1)}) custom-call(bf16[32,64,256]{2,1,0:T(8,128)(2,1)} %fourier_hbm.1, f32[1,256]{1,0:T(1,128)} %bitcast.4, bf16[32,64,256]{2,1,0:T(8,128)(2,1)} %leaf_hbm.1, bf16[128,64,256]{2,1,0:T(8,128)(2,1)} %refs_7_.1), custom_call_target="tpu_custom_call" | custom-call | flops 67108 | bytes 2097 | tf_op jit(solution)/shard_map/leaf/pallas_call | solution.py:93
  1.9 0.5 %collective-permute-start = (bf16[16,2,32,128]{3,2,1,0:T(8,128)(2,1)S(1)}, bf16[16,2,32,128]{3,2,1,0:T(8,128)(2,1)S(1)}, u32[]{:S(2)}, u32[]{:S(2)}) collective-permute-start(bf16[16,2,32,128]{3,2,1,0:T(8,128)(2,1)S(1)} %get-tuple-element.23.after.state_ref), channel_id=1, source_target_pairs={{0,1},{1,0},{2,3},{3,2},{4,5},{5,4},{6,7},{7,6},{8,9},{9,8},{10,11... | collective-permute-start | bytes 786440 | tf_op jit(solution)/shard_map/ppermute | solution.py:509
  2.5 1.4 %factors.2.weight_ref = bf16[16,128,256]{2,1,0:T(8,128)(2,1)S(1)} custom-call(bf16[32,3,2,1,64,64]{5,4,3,2,1,0:T(8,128)(2,1)} %factor_hbm.3, s32[3,1,32]{2,1,0:T(1,128)} %bitcast.2, bf16[16,2,32,128]{3,2,1,0:T(8,128)(2,1)S(1)} %get-tuple-element.23.after.state_ref), custom_call_target="tpu_custom_call" | custom-call | flops 524 | bytes 2097 | tf_op jit(solution)/shard_map/factors/pallas_call | solution.py:168
  3.9 0.0 collective-permute-done.partner_ref
  3.9 0.5 %level0.1 = (bf16[16,32,128]{2,1,0:T(8,128)(2,1)S(1)}, bf16[16,32,128]{2,1,0:T(8,128)(2,1)S(1)}) custom-call(bf16[16,2,32,128]{3,2,1,0:T(8,128)(2,1)S(1)} %get-tuple-element.23.after.state_ref, bf16[16,2,32,128]{3,2,1,0:T(8,128)(2,1)S(1)} %collective-permute-done.partner_ref, bf16[16,128,256]{2,1,0:T(8,128)(2,1)S(1)} %factors.2.weight_ref), custom_call_target="tpu_custom_call" | custom-call | flops 67108 | bytes 786 | tf_op jit(solution)/shard_map/level0/pallas_call | solution.py:200
  4.4 2.7 %collective-permute-start.2 = (bf16[16,32,128]{2,1,0:T(8,128)(2,1)S(1)}, bf16[16,32,128]{2,1,0:T(8,128)(2,1)S(1)}, u32[]{:S(2)}, u32[]{:S(2)}) collective-permute-start(bf16[16,32,128]{2,1,0:T(8,128)(2,1)S(1)} %get-tuple-element.32.state_ref), channel_id=1, source_target_pairs={{0,2},{1,3},{2,0},{3,1},{4,6},{5,7},{6,4},{7,5},{8,10},{9,11},{10,... | collective-permute-start | bytes 393224 | tf_op jit(solution)/shard_map/ppermute | solution.py:509
  7.1 0.0 copy-start
  7.1 0.1 collective-permute-start.1
  7.2 2.2 %factors.3 = (bf16[16,128,256]{2,1,0:T(8,128)(2,1)S(1)}, bf16[16,64,128]{2,1,0:T(8,128)(2,1)S(1)}, bf16[16,64,128]{2,1,0:T(8,128)(2,1)S(1)}, bf16[2,32,64,256]{3,2,1,0:T(8,128)(2,1)S(1)}) custom-call(bf16[32,3,2,1,64,64]{5,4,3,2,1,0:T(8,128)(2,1)} %factor_hbm.3, s32[3,1,32]{2,1,0:T(1,128)} %bitcast.3, ...), custom_call_target="tpu_custom_call" | custom-call | flops 1048 | bytes 4194 | tf_op jit(solution)/shard_map/factors/pallas_call | solution.py:168
  9.4 1.9 %collective-permute-start.6 = (bf16[16,64,128]{2,1,0:T(8,128)(2,1)S(1)}, bf16[16,64,128]{2,1,0:T(8,128)(2,1)S(1)}, u32[]{:S(2)}, u32[]{:S(2)}) collective-permute-start(bf16[16,64,128]{2,1,0:T(8,128)(2,1)S(1)} %get-tuple-element.33.cross_ref), channel_id=1, source_target_pairs={{0,8},{8,0},{16,24},{24,16},{1,9},{9,1},{17,25},{25,17},{2,10},{10... | collective-permute-start | bytes 786440 | tf_op jit(solution)/shard_map/ppermute | solution.py:509
  11.4 0.1 collective-permute-done.2.partner_ref
  11.5 0.4 %level1_0.1.own_ref = bf16[16,32,128]{2,1,0:T(8,128)(2,1)S(1)} custom-call(bf16[16,32,128]{2,1,0:T(8,128)(2,1)S(1)} %get-tuple-element.32.state_ref, bf16[16,32,128]{2,1,0:T(8,128)(2,1)S(1)} %collective-permute-done.2.partner_ref, bf16[16,128,256]{2,1,0:T(8,128)(2,1)S(1)} %get-tuple-element.25.weight_ref), custom_call_target="tpu_custom_call" | custom-call | flops 33554 | bytes 393 | tf_op jit(solution)/shard_map/level1_0/pallas_call | solution.py:240
  11.9 3.0 %collective-permute-start.3 = (bf16[16,32,128]{2,1,0:T(8,128)(2,1)S(1)}, bf16[16,32,128]{2,1,0:T(8,128)(2,1)S(1)}, u32[]{:S(2)}, u32[]{:S(2)}) collective-permute-start(bf16[16,32,128]{2,1,0:T(8,128)(2,1)S(1)} %level1_0.1.own_ref), channel_id=1, source_target_pairs={{0,4},{1,5},{2,6},{3,7},{4,0},{5,1},{6,2},{7,3},{8,12},{9,13},{10,... | collective-permute-start | bytes 393224 | tf_op jit(solution)/shard_map/ppermute | solution.py:509
  14.9 0.0 collective-permute-done.1.partner_ref
  14.9 0.8 %level1_1.1 = (bf16[16,32,128]{2,1,0:T(8,128)(2,1)S(1)}, bf16[16,16,128]{2,1,0:T(8,128)(2,1)S(1)}, bf16[16,32,128]{2,1,0:T(8,128)(2,1)S(1)}) custom-call(bf16[16,32,128]{2,1,0:T(8,128)(2,1)S(1)} %get-tuple-element.24.after.state_ref, bf16[16,32,128]{2,1,0:T(8,128)(2,1)S(1)} %collective-permute-done.1.partner_ref, ...), custom_call_target="tpu_custom_call" | custom-call | flops 33554 | bytes 393 | tf_op jit(solution)/shard_map/level1_1/pallas_call | solution.py:240
  15.7 1.5 %collective-permute-start.4 = (bf16[16,32,128]{2,1,0:T(8,128)(2,1)S(1)}, bf16[16,32,128]{2,1,0:T(8,128)(2,1)S(1)}, u32[]{:S(2)}, u32[]{:S(2)}) collective-permute-start(bf16[16,32,128]{2,1,0:T(8,128)(2,1)S(1)} %get-tuple-element.35), channel_id=1, source_target_pairs={{0,8},{8,0},{16,24},{24,16},{1,9},{9,1},{17,25},{25,17},{2,10},{10... | collective-permute-start | bytes 393224 | tf_op jit(solution)/shard_map/ppermute | solution.py:509
  17.2 1.9 %collective-permute-start.8 = (bf16[16,16,128]{2,1,0:T(8,128)(2,1)S(1)}, bf16[16,16,128]{2,1,0:T(8,128)(2,1)S(1)}, u32[]{:S(2)}, u32[]{:S(2)}) collective-permute-start(bf16[16,16,128]{2,1,0:T(8,128)(2,1)S(1)} %get-tuple-element.40), channel_id=1, source_target_pairs={{0,12},{1,13},{2,14},{3,15},{4,8},{5,9},{6,10},{7,11},{8,4},{9,5},... | collective-permute-start | bytes 196616 | tf_op jit(solution)/shard_map/ppermute | solution.py:516
  19.2 0.0 copy-done
  19.2 1.6 %places.1 = (bf16[4,32,128]{2,1,0:T(8,128)(2,1)S(1)}, bf16[256,128]{1,0:T(8,128)(2,1)S(1)}, bf16[1,16,64,256]{3,2,1,0:T(8,128)(2,1)S(1)}) custom-call(s32[128]{0:T(128)S(1)} %copy-done, bf16[16,32,128]{2,1,0:T(8,128)(2,1)S(1)} %get-tuple-element.27.after.state_ref, bf16[128,64,256]{2,1,0:T(8,128)(2,1)} %refs_7_.1), custom_call_target="tpu_custom_call" | custom-call | flops 16 | bytes 131 | tf_op jit(solution)/shard_map/places/pallas_call | solution.py:380
  20.8 1.9 %collective-permute-start.5 = (bf16[16,16,128]{2,1,0:T(8,128)(2,1)S(1)}, bf16[16,16,128]{2,1,0:T(8,128)(2,1)S(1)}, u32[]{:S(2)}, u32[]{:S(2)}) collective-permute-start(bf16[16,16,128]{2,1,0:T(8,128)(2,1)S(1)} %late_columns.1), channel_id=1, source_target_pairs={{0,12},{1,13},{2,14},{3,15},{4,8},{5,9},{6,10},{7,11},{8,4},{9,5},... | collective-permute-start | bytes 196616 | tf_op jit(solution)/shard_map/ppermute | solution.py:516
  22.8 0.0 collective-permute-done.3.partner_ref
  22.8 0.5 %last_own.1 = (bf16[256,128]{1,0:T(8,128)(2,1)S(1)}, bf16[256,128]{1,0:T(8,128)(2,1)S(1)}) custom-call(bf16[256,128]{1,0:T(8,128)(2,1)S(1)} %get-tuple-element.29.after.refs_1_.refs_2_, bf16[16,32,128]{2,1,0:T(8,128)(2,1)S(1)} %level1_0.1.own_ref, bf16[16,32,128]{2,1,0:T(8,128)(2,1)S(1)} %collective-permute-done.3.partner_ref, ...), custom_call_target="tpu_custom_call" | custom-call | flops 33554 | bytes 393 | tf_op jit(solution)/shard_map/last_own/pallas_call | solution.py:338
  23.2 1.6 %collective-permute-start.7 = (bf16[256,128]{1,0:T(8,128)(2,1)S(1)}, bf16[256,128]{1,0:T(8,128)(2,1)S(1)}, u32[]{:S(2)}, u32[]{:S(2)}) collective-permute-start(bf16[256,128]{1,0:T(8,128)(2,1)S(1)} %get-tuple-element.36), channel_id=1, source_target_pairs={{0,16},{8,24},{16,0},{24,8},{1,17},{9,25},{17,1},{25,9},{2,18},{10... | collective-permute-start | bytes 196616 | tf_op jit(solution)/shard_map/ppermute | solution.py:509
  24.8 0.0 collective-permute-done.8.partner_ref
  24.8 0.0 collective-permute-done.4.own_ref
  24.8 0.0 collective-permute-done.6.cross_ref
  24.8 0.4 %last_early.1 = bf16[256,128]{1,0:T(8,128)(2,1)S(1)} custom-call(bf16[256,128]{1,0:T(8,128)(2,1)S(1)} %get-tuple-element.29.after.refs_1_.refs_2_, bf16[16,32,128]{2,1,0:T(8,128)(2,1)S(1)} %collective-permute-done.4.own_ref, bf16[16,16,128]{2,1,0:T(8,128)(2,1)S(1)} %collective-permute-done.8.partner_ref, ...), custom_call_target="tpu_custom_call" | custom-call | flops 16777 | bytes 196 | tf_op jit(solution)/shard_map/last_early/pallas_call | solution.py:338
  25.2 0.6 %collective-permute-start.9 = (bf16[256,128]{1,0:T(8,128)(2,1)S(1)}, bf16[256,128]{1,0:T(8,128)(2,1)S(1)}, u32[]{:S(2)}, u32[]{:S(2)}) collective-permute-start(bf16[256,128]{1,0:T(8,128)(2,1)S(1)} %last_early.1), channel_id=1, source_target_pairs={{0,16},{8,24},{16,0},{24,8},{1,17},{9,25},{17,1},{25,9},{2,18},{10... | collective-permute-start | bytes 196616 | tf_op jit(solution)/shard_map/ppermute | solution.py:509
  25.8 1.2 %collective-permute-done.5.partner_ref = bf16[16,16,128]{2,1,0:T(8,128)(2,1)S(1)} collective-permute-done((bf16[16,16,128]{2,1,0:T(8,128)(2,1)S(1)}, bf16[16,16,128]{2,1,0:T(8,128)(2,1)S(1)}, u32[]{:S(2)}, u32[]{:S(2)}) %collective-permute-start.5) | collective-permute-done | bytes 65568 | tf_op jit(solution)/shard_map/ppermute | solution.py:516
  26.9 0.4 %last_late.1.refs_5_ = bf16[256,128]{1,0:T(8,128)(2,1)S(1)} custom-call(bf16[256,128]{1,0:T(8,128)(2,1)S(1)} %get-tuple-element.29.after.refs_1_.refs_2_, bf16[16,32,128]{2,1,0:T(8,128)(2,1)S(1)} %collective-permute-done.4.own_ref, bf16[16,16,128]{2,1,0:T(8,128)(2,1)S(1)} %collective-permute-done.5.partner_ref, ...), custom_call_target="tpu_custom_call" | custom-call | flops 16777 | bytes 196 | tf_op jit(solution)/shard_map/last_late/pallas_call | solution.py:338
  27.3 0.2 collective-permute-done.7.refs_6_
  27.6 1.6 %root.2 = (bf16[8,2,256,128]{3,2,1,0:T(8,128)(2,1)S(1)}, bf16[1,16,64,256]{3,2,1,0:T(8,128)(2,1)S(1)}) custom-call(bf16[4,32,128]{2,1,0:T(8,128)(2,1)S(1)} %get-tuple-element.28.refs_0_.refs_1_, bf16[256,128]{1,0:T(8,128)(2,1)S(1)} %get-tuple-element.29.after.refs_1_.refs_2_, bf16[32,64,256]{2,1,0:T(8,128)(2,1)S(1)} %get-tuple-element.30.refs_2_, ...), custom_call_target="tpu_custom_call" | custom-call | flops 50331 | bytes 3145 | tf_op jit(solution)/shard_map/root/pallas_call | solution.py:484
  29.2 0.3 %collective-permute-done.9.refs_5_ = bf16[256,128]{1,0:T(8,128)(2,1)S(1)} collective-permute-done((bf16[256,128]{1,0:T(8,128)(2,1)S(1)}, bf16[256,128]{1,0:T(8,128)(2,1)S(1)}, u32[]{:S(2)}, u32[]{:S(2)}) %collective-permute-start.9) | collective-permute-done | bytes 65568 | tf_op jit(solution)/shard_map/ppermute | solution.py:509
  29.5 1.6 %root.3 = bf16[8,2,256,128]{3,2,1,0:T(8,128)(2,1)} custom-call(bf16[8,2,256,128]{3,2,1,0:T(8,128)(2,1)S(1)} %get-tuple-element.37.refs_0_, bf16[4,32,128]{2,1,0:T(8,128)(2,1)S(1)} %get-tuple-element.28.refs_0_.refs_1_, bf16[256,128]{1,0:T(8,128)(2,1)S(1)} %get-tuple-element.29.after.refs_1_.refs_2_, bf16[1,16,64,256]{3,2,1,0:T(8,128)(2,1)S(1)} %get-tuple-element.38.refs_3_, ...), custom_call_target="tpu_custom_call" | custom-call | flops 16777 | bytes 1048 | tf_op jit(solution)/shard_map/root/pallas_call | solution.py:484
  (1 shorter events, 0.0 us)
Async XLA Ops:
  1.9 2.0 %collective-permute-start = (bf16[16,2,32,128]{3,2,1,0:T(8,128)(2,1)S(1)}, bf16[16,2,32,128]{3,2,1,0:T(8,128)(2,1)S(1)}, u32[]{:S(2)}, u32[]{:S(2)}) collective-permute-start(bf16[16,2,32,128]{3,2,1,0:T(8,128)(2,1)S(1)} %get-tuple-element.23.after.state_ref), channel_id=1, source_target_pairs={{0,1},{1,0},{2,3},{3,2},{4,5},{5,4},{6,7},{7,6},{8,9},{9,8},{10,11... | collective-permute-start | bytes 786440 | tf_op jit(solution)/shard_map/ppermute | solution.py:509
  4.4 7.1 %collective-permute-start.2 = (bf16[16,32,128]{2,1,0:T(8,128)(2,1)S(1)}, bf16[16,32,128]{2,1,0:T(8,128)(2,1)S(1)}, u32[]{:S(2)}, u32[]{:S(2)}) collective-permute-start(bf16[16,32,128]{2,1,0:T(8,128)(2,1)S(1)} %get-tuple-element.32.state_ref), channel_id=1, source_target_pairs={{0,2},{1,3},{2,0},{3,1},{4,6},{5,7},{6,4},{7,5},{8,10},{9,11},{10,... | collective-permute-start | bytes 393224 | tf_op jit(solution)/shard_map/ppermute | solution.py:509
  7.1 12.1 %copy-start = (s32[128]{0:T(128)S(1)}, s32[128]{0:T(128)}, u32[]{:S(2)}) copy-start(s32[128]{0:T(128)} %order_ref.1) | copy-start | bytes 1540
  7.1 7.8 %collective-permute-start.1 = (bf16[16,32,128]{2,1,0:T(8,128)(2,1)S(1)}, bf16[16,32,128]{2,1,0:T(8,128)(2,1)S(1)}, u32[]{:S(2)}, u32[]{:S(2)}) collective-permute-start(bf16[16,32,128]{2,1,0:T(8,128)(2,1)S(1)} %get-tuple-element.24.after.state_ref), channel_id=1, source_target_pairs={{0,2},{1,3},{2,0},{3,1},{4,6},{5,7},{6,4},{7,5},{8,10},{9,11},{10,... | collective-permute-start | bytes 393224 | tf_op jit(solution)/shard_map/ppermute | solution.py:509
  9.4 15.4 %collective-permute-start.6 = (bf16[16,64,128]{2,1,0:T(8,128)(2,1)S(1)}, bf16[16,64,128]{2,1,0:T(8,128)(2,1)S(1)}, u32[]{:S(2)}, u32[]{:S(2)}) collective-permute-start(bf16[16,64,128]{2,1,0:T(8,128)(2,1)S(1)} %get-tuple-element.33.cross_ref), channel_id=1, source_target_pairs={{0,8},{8,0},{16,24},{24,16},{1,9},{9,1},{17,25},{25,17},{2,10},{10... | collective-permute-start | bytes 786440 | tf_op jit(solution)/shard_map/ppermute | solution.py:509
  11.9 10.9 %collective-permute-start.3 = (bf16[16,32,128]{2,1,0:T(8,128)(2,1)S(1)}, bf16[16,32,128]{2,1,0:T(8,128)(2,1)S(1)}, u32[]{:S(2)}, u32[]{:S(2)}) collective-permute-start(bf16[16,32,128]{2,1,0:T(8,128)(2,1)S(1)} %level1_0.1.own_ref), channel_id=1, source_target_pairs={{0,4},{1,5},{2,6},{3,7},{4,0},{5,1},{6,2},{7,3},{8,12},{9,13},{10,... | collective-permute-start | bytes 393224 | tf_op jit(solution)/shard_map/ppermute | solution.py:509
  15.7 9.1 %collective-permute-start.4 = (bf16[16,32,128]{2,1,0:T(8,128)(2,1)S(1)}, bf16[16,32,128]{2,1,0:T(8,128)(2,1)S(1)}, u32[]{:S(2)}, u32[]{:S(2)}) collective-permute-start(bf16[16,32,128]{2,1,0:T(8,128)(2,1)S(1)} %get-tuple-element.35), channel_id=1, source_target_pairs={{0,8},{8,0},{16,24},{24,16},{1,9},{9,1},{17,25},{25,17},{2,10},{10... | collective-permute-start | bytes 393224 | tf_op jit(solution)/shard_map/ppermute | solution.py:509
  17.2 7.6 %collective-permute-start.8 = (bf16[16,16,128]{2,1,0:T(8,128)(2,1)S(1)}, bf16[16,16,128]{2,1,0:T(8,128)(2,1)S(1)}, u32[]{:S(2)}, u32[]{:S(2)}) collective-permute-start(bf16[16,16,128]{2,1,0:T(8,128)(2,1)S(1)} %get-tuple-element.40), channel_id=1, source_target_pairs={{0,12},{1,13},{2,14},{3,15},{4,8},{5,9},{6,10},{7,11},{8,4},{9,5},... | collective-permute-start | bytes 196616 | tf_op jit(solution)/shard_map/ppermute | solution.py:516
  20.8 6.1 %collective-permute-start.5 = (bf16[16,16,128]{2,1,0:T(8,128)(2,1)S(1)}, bf16[16,16,128]{2,1,0:T(8,128)(2,1)S(1)}, u32[]{:S(2)}, u32[]{:S(2)}) collective-permute-start(bf16[16,16,128]{2,1,0:T(8,128)(2,1)S(1)} %late_columns.1), channel_id=1, source_target_pairs={{0,12},{1,13},{2,14},{3,15},{4,8},{5,9},{6,10},{7,11},{8,4},{9,5},... | collective-permute-start | bytes 196616 | tf_op jit(solution)/shard_map/ppermute | solution.py:516
  23.2 4.3 %collective-permute-start.7 = (bf16[256,128]{1,0:T(8,128)(2,1)S(1)}, bf16[256,128]{1,0:T(8,128)(2,1)S(1)}, u32[]{:S(2)}, u32[]{:S(2)}) collective-permute-start(bf16[256,128]{1,0:T(8,128)(2,1)S(1)} %get-tuple-element.36), channel_id=1, source_target_pairs={{0,16},{8,24},{16,0},{24,8},{1,17},{9,25},{17,1},{25,9},{2,18},{10... | collective-permute-start | bytes 196616 | tf_op jit(solution)/shard_map/ppermute | solution.py:509
  25.2 4.3 %collective-permute-start.9 = (bf16[256,128]{1,0:T(8,128)(2,1)S(1)}, bf16[256,128]{1,0:T(8,128)(2,1)S(1)}, u32[]{:S(2)}, u32[]{:S(2)}) collective-permute-start(bf16[256,128]{1,0:T(8,128)(2,1)S(1)} %last_early.1), channel_id=1, source_target_pairs={{0,16},{8,24},{16,0},{24,8},{1,17},{9,25},{17,1},{25,9},{2,18},{10... | collective-permute-start | bytes 196616 | tf_op jit(solution)/shard_map/ppermute | solution.py:509

commit v6 on v4

--- a/solution.py
+++ b/solution.py
@@ -432,7 +432,6 @@
             for tile in range(degrees // 128):
                 rows_ref[tile, pl.ds(begin, 2 * group_rows), :] = product[:, tile * 128 : (tile + 1) * 128]
     place = place_ref[pl.ds(first, count)].reshape(count * here, slots)
-    per = max(1, fields // 4)
     for column in range(columns):
         tiles = [
             rows_ref[tile, pl.ds(column, count * here, stride=columns), :].astype(BF16) for tile in range(degrees // 128)
@@ -443,10 +442,8 @@
             natural = natural + so_far_ref[where]
             natural = jnp.where(alive_ref[...] != 0, natural, jnp.zeros((), BF16))
         natural_ref[where] = natural
-        if last and (column + 1) % (2 * per) == 0:
-            done = column // (2 * per)
-            where = pl.ds(done * per, per)
-            copies.append(pltpu.make_async_copy(natural_ref.at[where], out_ref.at[where], sems.at[done]))
+        if last:
+            copies.append(pltpu.make_async_copy(natural_ref.at[where], out_ref.at[where], sems.at[column]))
             copies[-1].start()
     for copy in copies:
         copy.wait()
@@ -467,7 +464,7 @@
     if last:
         inputs = [so_far, *inputs]
         in_specs = whole_blocks(len(inputs))
-        scratch += [pltpu.VMEM(out.shape, BF16), pltpu.SemaphoreType.DMA((columns // 2,))]
+        scratch += [pltpu.VMEM(out.shape, BF16), pltpu.SemaphoreType.DMA((columns,))]
         more["out_specs"] = IN_HBM
     return call(
         functools.partial(root_kernel, group, first, last),

time: 31.5 us -> 31.6 us (level)
  transfers between devices with their start and end apart: 10 -> 10, of which waited for: 4 -> 4; matrix products, arithmetic and copies ran while one was open for 0% -> 0% of each run, Pallas kernels for 30% -> 29%
where the time goes in v6:
time: 31.6 us; the launch traced here: 31.4 us
  starting transfers between devices  15.8 us (50%)
  Pallas kernels  13.3 us (42%)
  waiting for transfers between devices  2.17 us (7%)
    ppermute x8, starting transfers between devices, swap(): lax.ppermute(array, axis, [(i, i ^ bits) for i in range(lax.axis_size(axi...  11.9 us
    ppermute x2, starting transfers between devices, swap_both(): return lax.ppermute(array, ('order', 'lat'), pairs)  3.89 us
    pallas_call x2, Pallas kernels, level_weights(): call(functools.partial(factor_kernel, levels, pieces, root_pieces), 'fact...  3.68 us
    pallas_call x2, Pallas kernels, spectra_of(): call(functools.partial(root_kernel, group, first, last), 'root', out, in_...  2.98 us
    pallas_call x1, Pallas kernels, leaf_states(): call(functools.partial(leaf_kernel, pieces, group), 'leaf', [jax.ShapeDty...  1.92 us
    pallas_call x1, Pallas kernels, places_of(): call(functools.partial(place_kernel, group), 'places', [jax.ShapeDtypeStr...  1.78 us
    pallas_call x2, Pallas kernels, next_states(): call(functools.partial(level_kernel, side, 'order'), name, [jax.ShapeDtyp...  1.26 us
    pallas_call x3, Pallas kernels, last_states(): call(functools.partial(last_level_kernel, turn, begin, 'order'), name, [j...  1.23 us
  transfers between devices with their start and end apart: 10, of which 4 were waited for; matrix products, arithmetic and copies ran while one was open for 0% of the time, Pallas kernels for 29%

profile of v6, /device:TPU:0, one launch (start us, length us, event | category | flops | bytes accessed | tf_op | source)
XLA Modules:
  0.0 31.4 jit_solution(14960205052140283477)
XLA Ops:
  0.0 1.9 %leaf.1 = (bf16[16,2,32,128]{3,2,1,0:T(8,128)(2,1)S(1)}, bf16[32,64,256]{2,1,0:T(8,128)(2,1)S(1)}) custom-call(bf16[32,64,256]{2,1,0:T(8,128)(2,1)} %fourier_hbm.1, f32[1,256]{1,0:T(1,128)} %bitcast.4, bf16[32,64,256]{2,1,0:T(8,128)(2,1)} %leaf_hbm.1, bf16[128,64,256]{2,1,0:T(8,128)(2,1)} %root_hbm.3), custom_call_target="tpu_custom_call" | custom-call | flops 67108 | bytes 2097 | tf_op jit(solution)/shard_map/leaf/pallas_call | solution.py:92
  1.9 0.5 %collective-permute-start = (bf16[16,2,32,128]{3,2,1,0:T(8,128)(2,1)S(1)}, bf16[16,2,32,128]{3,2,1,0:T(8,128)(2,1)S(1)}, u32[]{:S(2)}, u32[]{:S(2)}) collective-permute-start(bf16[16,2,32,128]{3,2,1,0:T(8,128)(2,1)S(1)} %get-tuple-element.21.after.state_ref), channel_id=1, source_target_pairs={{0,1},{1,0},{2,3},{3,2},{4,5},{5,4},{6,7},{7,6},{8,9},{9,8},{10,11... | collective-permute-start | bytes 786440 | tf_op jit(solution)/shard_map/ppermute | solution.py:494
  2.5 1.4 %factors.2.weight_ref = bf16[16,128,256]{2,1,0:T(8,128)(2,1)S(1)} custom-call(bf16[32,3,2,1,64,64]{5,4,3,2,1,0:T(8,128)(2,1)} %factor_hbm.3, s32[3,1,32]{2,1,0:T(1,128)} %bitcast.2, bf16[16,2,32,128]{3,2,1,0:T(8,128)(2,1)S(1)} %get-tuple-element.21.after.state_ref), custom_call_target="tpu_custom_call" | custom-call | flops 524 | bytes 2097 | tf_op jit(solution)/shard_map/factors/pallas_call | solution.py:167
  3.9 0.0 collective-permute-done.partner_ref
  3.9 0.5 %level0.1 = (bf16[16,32,128]{2,1,0:T(8,128)(2,1)S(1)}, bf16[16,32,128]{2,1,0:T(8,128)(2,1)S(1)}) custom-call(bf16[16,2,32,128]{3,2,1,0:T(8,128)(2,1)S(1)} %get-tuple-element.21.after.state_ref, bf16[16,2,32,128]{3,2,1,0:T(8,128)(2,1)S(1)} %collective-permute-done.partner_ref, bf16[16,128,256]{2,1,0:T(8,128)(2,1)S(1)} %factors.2.weight_ref), custom_call_target="tpu_custom_call" | custom-call | flops 67108 | bytes 786 | tf_op jit(solution)/shard_map/level0/pallas_call | solution.py:199
  4.4 2.7 %collective-permute-start.2 = (bf16[16,32,128]{2,1,0:T(8,128)(2,1)S(1)}, bf16[16,32,128]{2,1,0:T(8,128)(2,1)S(1)}, u32[]{:S(2)}, u32[]{:S(2)}) collective-permute-start(bf16[16,32,128]{2,1,0:T(8,128)(2,1)S(1)} %get-tuple-element.30.state_ref), channel_id=1, source_target_pairs={{0,2},{1,3},{2,0},{3,1},{4,6},{5,7},{6,4},{7,5},{8,10},{9,11},{10,... | collective-permute-start | bytes 393224 | tf_op jit(solution)/shard_map/ppermute | solution.py:494
  7.1 0.0 copy-start
  7.1 0.1 collective-permute-start.1
  7.2 2.2 %factors.3 = (bf16[16,128,256]{2,1,0:T(8,128)(2,1)S(1)}, bf16[16,64,128]{2,1,0:T(8,128)(2,1)S(1)}, bf16[16,64,128]{2,1,0:T(8,128)(2,1)S(1)}, bf16[2,32,64,256]{3,2,1,0:T(8,128)(2,1)S(1)}) custom-call(bf16[32,3,2,1,64,64]{5,4,3,2,1,0:T(8,128)(2,1)} %factor_hbm.3, s32[3,1,32]{2,1,0:T(1,128)} %bitcast.3, ...), custom_call_target="tpu_custom_call" | custom-call | flops 1048 | bytes 4194 | tf_op jit(solution)/shard_map/factors/pallas_call | solution.py:167
  9.4 1.9 %collective-permute-start.6 = (bf16[16,64,128]{2,1,0:T(8,128)(2,1)S(1)}, bf16[16,64,128]{2,1,0:T(8,128)(2,1)S(1)}, u32[]{:S(2)}, u32[]{:S(2)}) collective-permute-start(bf16[16,64,128]{2,1,0:T(8,128)(2,1)S(1)} %get-tuple-element.31.cross_ref), channel_id=1, source_target_pairs={{0,8},{8,0},{16,24},{24,16},{1,9},{9,1},{17,25},{25,17},{2,10},{10... | collective-permute-start | bytes 786440 | tf_op jit(solution)/shard_map/ppermute | solution.py:494
  11.4 0.1 collective-permute-done.2.partner_ref
  11.5 0.4 %level1_0.1.own_ref = bf16[16,32,128]{2,1,0:T(8,128)(2,1)S(1)} custom-call(bf16[16,32,128]{2,1,0:T(8,128)(2,1)S(1)} %get-tuple-element.30.state_ref, bf16[16,32,128]{2,1,0:T(8,128)(2,1)S(1)} %collective-permute-done.2.partner_ref, bf16[16,128,256]{2,1,0:T(8,128)(2,1)S(1)} %get-tuple-element.23.weight_ref), custom_call_target="tpu_custom_call" | custom-call | flops 33554 | bytes 393 | tf_op jit(solution)/shard_map/level1_0/pallas_call | solution.py:239
  11.9 3.0 %collective-permute-start.3 = (bf16[16,32,128]{2,1,0:T(8,128)(2,1)S(1)}, bf16[16,32,128]{2,1,0:T(8,128)(2,1)S(1)}, u32[]{:S(2)}, u32[]{:S(2)}) collective-permute-start(bf16[16,32,128]{2,1,0:T(8,128)(2,1)S(1)} %level1_0.1.own_ref), channel_id=1, source_target_pairs={{0,4},{1,5},{2,6},{3,7},{4,0},{5,1},{6,2},{7,3},{8,12},{9,13},{10,... | collective-permute-start | bytes 393224 | tf_op jit(solution)/shard_map/ppermute | solution.py:494
  14.9 0.0 collective-permute-done.1.partner_ref
  14.9 0.8 %level1_1.1 = (bf16[16,32,128]{2,1,0:T(8,128)(2,1)S(1)}, bf16[16,16,128]{2,1,0:T(8,128)(2,1)S(1)}, bf16[16,32,128]{2,1,0:T(8,128)(2,1)S(1)}) custom-call(bf16[16,32,128]{2,1,0:T(8,128)(2,1)S(1)} %get-tuple-element.22.after.state_ref, bf16[16,32,128]{2,1,0:T(8,128)(2,1)S(1)} %collective-permute-done.1.partner_ref, ...), custom_call_target="tpu_custom_call" | custom-call | flops 33554 | bytes 393 | tf_op jit(solution)/shard_map/level1_1/pallas_call | solution.py:239
  15.7 1.5 %collective-permute-start.4 = (bf16[16,32,128]{2,1,0:T(8,128)(2,1)S(1)}, bf16[16,32,128]{2,1,0:T(8,128)(2,1)S(1)}, u32[]{:S(2)}, u32[]{:S(2)}) collective-permute-start(bf16[16,32,128]{2,1,0:T(8,128)(2,1)S(1)} %get-tuple-element.33), channel_id=1, source_target_pairs={{0,8},{8,0},{16,24},{24,16},{1,9},{9,1},{17,25},{25,17},{2,10},{10... | collective-permute-start | bytes 393224 | tf_op jit(solution)/shard_map/ppermute | solution.py:494
  17.2 1.9 %collective-permute-start.8 = (bf16[16,16,128]{2,1,0:T(8,128)(2,1)S(1)}, bf16[16,16,128]{2,1,0:T(8,128)(2,1)S(1)}, u32[]{:S(2)}, u32[]{:S(2)}) collective-permute-start(bf16[16,16,128]{2,1,0:T(8,128)(2,1)S(1)} %get-tuple-element.36), channel_id=1, source_target_pairs={{0,12},{1,13},{2,14},{3,15},{4,8},{5,9},{6,10},{7,11},{8,4},{9,5},... | collective-permute-start | bytes 196616 | tf_op jit(solution)/shard_map/ppermute | solution.py:501
  19.2 0.0 copy-done
  19.2 1.8 %places.1 = (bf16[4,32,128]{2,1,0:T(8,128)(2,1)S(1)}, bf16[256,128]{1,0:T(8,128)(2,1)S(1)}, bf16[1,32,64,256]{3,2,1,0:T(8,128)(2,1)S(1)}) custom-call(s32[128]{0:T(128)S(1)} %copy-done, bf16[16,32,128]{2,1,0:T(8,128)(2,1)S(1)} %get-tuple-element.25.after.state_ref, bf16[128,64,256]{2,1,0:T(8,128)(2,1)} %root_hbm.3), custom_call_target="tpu_custom_call" | custom-call | flops 16 | bytes 131 | tf_op jit(solution)/shard_map/places/pallas_call | solution.py:379
  21.0 1.9 %collective-permute-start.5 = (bf16[16,16,128]{2,1,0:T(8,128)(2,1)S(1)}, bf16[16,16,128]{2,1,0:T(8,128)(2,1)S(1)}, u32[]{:S(2)}, u32[]{:S(2)}) collective-permute-start(bf16[16,16,128]{2,1,0:T(8,128)(2,1)S(1)} %late_columns.1), channel_id=1, source_target_pairs={{0,12},{1,13},{2,14},{3,15},{4,8},{5,9},{6,10},{7,11},{8,4},{9,5},... | collective-permute-start | bytes 196616 | tf_op jit(solution)/shard_map/ppermute | solution.py:501
  22.9 0.0 collective-permute-done.3.partner_ref
  22.9 0.5 %last_own.1 = (bf16[256,128]{1,0:T(8,128)(2,1)S(1)}, bf16[256,128]{1,0:T(8,128)(2,1)S(1)}) custom-call(bf16[256,128]{1,0:T(8,128)(2,1)S(1)} %get-tuple-element.27.after.refs_1_.refs_2_, bf16[16,32,128]{2,1,0:T(8,128)(2,1)S(1)} %level1_0.1.own_ref, bf16[16,32,128]{2,1,0:T(8,128)(2,1)S(1)} %collective-permute-done.3.partner_ref, ...), custom_call_target="tpu_custom_call" | custom-call | flops 33554 | bytes 393 | tf_op jit(solution)/shard_map/last_own/pallas_call | solution.py:337
  23.4 1.6 %collective-permute-start.7 = (bf16[256,128]{1,0:T(8,128)(2,1)S(1)}, bf16[256,128]{1,0:T(8,128)(2,1)S(1)}, u32[]{:S(2)}, u32[]{:S(2)}) collective-permute-start(bf16[256,128]{1,0:T(8,128)(2,1)S(1)} %get-tuple-element.34), channel_id=1, source_target_pairs={{0,16},{8,24},{16,0},{24,8},{1,17},{9,25},{17,1},{25,9},{2,18},{10... | collective-permute-start | bytes 196616 | tf_op jit(solution)/shard_map/ppermute | solution.py:494
  25.0 0.0 collective-permute-done.8.partner_ref
  25.0 0.0 collective-permute-done.4.own_ref
  25.0 0.0 collective-permute-done.6.cross_ref
  25.0 0.4 %last_early.1 = bf16[256,128]{1,0:T(8,128)(2,1)S(1)} custom-call(bf16[256,128]{1,0:T(8,128)(2,1)S(1)} %get-tuple-element.27.after.refs_1_.refs_2_, bf16[16,32,128]{2,1,0:T(8,128)(2,1)S(1)} %collective-permute-done.4.own_ref, bf16[16,16,128]{2,1,0:T(8,128)(2,1)S(1)} %collective-permute-done.8.partner_ref, ...), custom_call_target="tpu_custom_call" | custom-call | flops 16777 | bytes 196 | tf_op jit(solution)/shard_map/last_early/pallas_call | solution.py:337
  25.4 0.6 %collective-permute-start.9 = (bf16[256,128]{1,0:T(8,128)(2,1)S(1)}, bf16[256,128]{1,0:T(8,128)(2,1)S(1)}, u32[]{:S(2)}, u32[]{:S(2)}) collective-permute-start(bf16[256,128]{1,0:T(8,128)(2,1)S(1)} %last_early.1), channel_id=1, source_target_pairs={{0,16},{8,24},{16,0},{24,8},{1,17},{9,25},{17,1},{25,9},{2,18},{10... | collective-permute-start | bytes 196616 | tf_op jit(solution)/shard_map/ppermute | solution.py:494
  25.9 1.2 %collective-permute-done.5.partner_ref = bf16[16,16,128]{2,1,0:T(8,128)(2,1)S(1)} collective-permute-done((bf16[16,16,128]{2,1,0:T(8,128)(2,1)S(1)}, bf16[16,16,128]{2,1,0:T(8,128)(2,1)S(1)}, u32[]{:S(2)}, u32[]{:S(2)}) %collective-permute-start.5) | collective-permute-done | bytes 65568 | tf_op jit(solution)/shard_map/ppermute | solution.py:501
  27.1 0.4 %last_late.1.refs_5_ = bf16[256,128]{1,0:T(8,128)(2,1)S(1)} custom-call(bf16[256,128]{1,0:T(8,128)(2,1)S(1)} %get-tuple-element.27.after.refs_1_.refs_2_, bf16[16,32,128]{2,1,0:T(8,128)(2,1)S(1)} %collective-permute-done.4.own_ref, bf16[16,16,128]{2,1,0:T(8,128)(2,1)S(1)} %collective-permute-done.5.partner_ref, ...), custom_call_target="tpu_custom_call" | custom-call | flops 16777 | bytes 196 | tf_op jit(solution)/shard_map/last_late/pallas_call | solution.py:337
  27.5 0.2 collective-permute-done.7.refs_6_
  27.8 1.3 %root.2.refs_0_ = bf16[8,2,256,128]{3,2,1,0:T(8,128)(2,1)S(1)} custom-call(bf16[4,32,128]{2,1,0:T(8,128)(2,1)S(1)} %get-tuple-element.26.refs_0_.refs_1_, bf16[256,128]{1,0:T(8,128)(2,1)S(1)} %get-tuple-element.27.after.refs_1_.refs_2_, bf16[32,64,256]{2,1,0:T(8,128)(2,1)S(1)} %get-tuple-element.28.refs_2_, ...), custom_call_target="tpu_custom_call" | custom-call | flops 50331 | bytes 3145 | tf_op jit(solution)/shard_map/root/pallas_call | solution.py:469
  29.1 0.6 %collective-permute-done.9.refs_4_ = bf16[256,128]{1,0:T(8,128)(2,1)S(1)} collective-permute-done((bf16[256,128]{1,0:T(8,128)(2,1)S(1)}, bf16[256,128]{1,0:T(8,128)(2,1)S(1)}, u32[]{:S(2)}, u32[]{:S(2)}) %collective-permute-start.9) | collective-permute-done | bytes 65568 | tf_op jit(solution)/shard_map/ppermute | solution.py:494
  29.7 1.7 %root.3 = bf16[8,2,256,128]{3,2,1,0:T(8,128)(2,1)} custom-call(bf16[8,2,256,128]{3,2,1,0:T(8,128)(2,1)S(1)} %root.2.refs_0_, bf16[4,32,128]{2,1,0:T(8,128)(2,1)S(1)} %get-tuple-element.26.refs_0_.refs_1_, bf16[256,128]{1,0:T(8,128)(2,1)S(1)} %get-tuple-element.27.after.refs_1_.refs_2_, bf16[1,32,64,256]{3,2,1,0:T(8,128)(2,1)S(1)} %get-tuple-element.35.refs_3_, ...), custom_call_target="tpu_custom_call" | custom-call | flops 16777 | bytes 1048 | tf_op jit(solution)/shard_map/root/pallas_call | solution.py:469
  (1 shorter events, 0.0 us)
Async XLA Ops:
  1.9 2.0 %collective-permute-start = (bf16[16,2,32,128]{3,2,1,0:T(8,128)(2,1)S(1)}, bf16[16,2,32,128]{3,2,1,0:T(8,128)(2,1)S(1)}, u32[]{:S(2)}, u32[]{:S(2)}) collective-permute-start(bf16[16,2,32,128]{3,2,1,0:T(8,128)(2,1)S(1)} %get-tuple-element.21.after.state_ref), channel_id=1, source_target_pairs={{0,1},{1,0},{2,3},{3,2},{4,5},{5,4},{6,7},{7,6},{8,9},{9,8},{10,11... | collective-permute-start | bytes 786440 | tf_op jit(solution)/shard_map/ppermute | solution.py:494
  4.4 7.1 %collective-permute-start.2 = (bf16[16,32,128]{2,1,0:T(8,128)(2,1)S(1)}, bf16[16,32,128]{2,1,0:T(8,128)(2,1)S(1)}, u32[]{:S(2)}, u32[]{:S(2)}) collective-permute-start(bf16[16,32,128]{2,1,0:T(8,128)(2,1)S(1)} %get-tuple-element.30.state_ref), channel_id=1, source_target_pairs={{0,2},{1,3},{2,0},{3,1},{4,6},{5,7},{6,4},{7,5},{8,10},{9,11},{10,... | collective-permute-start | bytes 393224 | tf_op jit(solution)/shard_map/ppermute | solution.py:494
  7.1 12.1 %copy-start = (s32[128]{0:T(128)S(1)}, s32[128]{0:T(128)}, u32[]{:S(2)}) copy-start(s32[128]{0:T(128)} %order_ref.1) | copy-start | bytes 1540
  7.1 7.8 %collective-permute-start.1 = (bf16[16,32,128]{2,1,0:T(8,128)(2,1)S(1)}, bf16[16,32,128]{2,1,0:T(8,128)(2,1)S(1)}, u32[]{:S(2)}, u32[]{:S(2)}) collective-permute-start(bf16[16,32,128]{2,1,0:T(8,128)(2,1)S(1)} %get-tuple-element.22.after.state_ref), channel_id=1, source_target_pairs={{0,2},{1,3},{2,0},{3,1},{4,6},{5,7},{6,4},{7,5},{8,10},{9,11},{10,... | collective-permute-start | bytes 393224 | tf_op jit(solution)/shard_map/ppermute | solution.py:494
  9.4 15.6 %collective-permute-start.6 = (bf16[16,64,128]{2,1,0:T(8,128)(2,1)S(1)}, bf16[16,64,128]{2,1,0:T(8,128)(2,1)S(1)}, u32[]{:S(2)}, u32[]{:S(2)}) collective-permute-start(bf16[16,64,128]{2,1,0:T(8,128)(2,1)S(1)} %get-tuple-element.31.cross_ref), channel_id=1, source_target_pairs={{0,8},{8,0},{16,24},{24,16},{1,9},{9,1},{17,25},{25,17},{2,10},{10... | collective-permute-start | bytes 786440 | tf_op jit(solution)/shard_map/ppermute | solution.py:494
  11.9 11.0 %collective-permute-start.3 = (bf16[16,32,128]{2,1,0:T(8,128)(2,1)S(1)}, bf16[16,32,128]{2,1,0:T(8,128)(2,1)S(1)}, u32[]{:S(2)}, u32[]{:S(2)}) collective-permute-start(bf16[16,32,128]{2,1,0:T(8,128)(2,1)S(1)} %level1_0.1.own_ref), channel_id=1, source_target_pairs={{0,4},{1,5},{2,6},{3,7},{4,0},{5,1},{6,2},{7,3},{8,12},{9,13},{10,... | collective-permute-start | bytes 393224 | tf_op jit(solution)/shard_map/ppermute | solution.py:494
  15.7 9.3 %collective-permute-start.4 = (bf16[16,32,128]{2,1,0:T(8,128)(2,1)S(1)}, bf16[16,32,128]{2,1,0:T(8,128)(2,1)S(1)}, u32[]{:S(2)}, u32[]{:S(2)}) collective-permute-start(bf16[16,32,128]{2,1,0:T(8,128)(2,1)S(1)} %get-tuple-element.33), channel_id=1, source_target_pairs={{0,8},{8,0},{16,24},{24,16},{1,9},{9,1},{17,25},{25,17},{2,10},{10... | collective-permute-start | bytes 393224 | tf_op jit(solution)/shard_map/ppermute | solution.py:494
  17.2 7.8 %collective-permute-start.8 = (bf16[16,16,128]{2,1,0:T(8,128)(2,1)S(1)}, bf16[16,16,128]{2,1,0:T(8,128)(2,1)S(1)}, u32[]{:S(2)}, u32[]{:S(2)}) collective-permute-start(bf16[16,16,128]{2,1,0:T(8,128)(2,1)S(1)} %get-tuple-element.36), channel_id=1, source_target_pairs={{0,12},{1,13},{2,14},{3,15},{4,8},{5,9},{6,10},{7,11},{8,4},{9,5},... | collective-permute-start | bytes 196616 | tf_op jit(solution)/shard_map/ppermute | solution.py:501
  21.0 6.1 %collective-permute-start.5 = (bf16[16,16,128]{2,1,0:T(8,128)(2,1)S(1)}, bf16[16,16,128]{2,1,0:T(8,128)(2,1)S(1)}, u32[]{:S(2)}, u32[]{:S(2)}) collective-permute-start(bf16[16,16,128]{2,1,0:T(8,128)(2,1)S(1)} %late_columns.1), channel_id=1, source_target_pairs={{0,12},{1,13},{2,14},{3,15},{4,8},{5,9},{6,10},{7,11},{8,4},{9,5},... | collective-permute-start | bytes 196616 | tf_op jit(solution)/shard_map/ppermute | solution.py:501
  23.4 4.3 %collective-permute-start.7 = (bf16[256,128]{1,0:T(8,128)(2,1)S(1)}, bf16[256,128]{1,0:T(8,128)(2,1)S(1)}, u32[]{:S(2)}, u32[]{:S(2)}) collective-permute-start(bf16[256,128]{1,0:T(8,128)(2,1)S(1)} %get-tuple-element.34), channel_id=1, source_target_pairs={{0,16},{8,24},{16,0},{24,8},{1,17},{9,25},{17,1},{25,9},{2,18},{10... | collective-permute-start | bytes 196616 | tf_op jit(solution)/shard_map/ppermute | solution.py:494
  25.4 4.3 %collective-permute-start.9 = (bf16[256,128]{1,0:T(8,128)(2,1)S(1)}, bf16[256,128]{1,0:T(8,128)(2,1)S(1)}, u32[]{:S(2)}, u32[]{:S(2)}) collective-permute-start(bf16[256,128]{1,0:T(8,128)(2,1)S(1)} %last_early.1), channel_id=1, source_target_pairs={{0,16},{8,24},{16,0},{24,8},{1,17},{9,25},{17,1},{25,9},{2,18},{10... | collective-permute-start | bytes 196616 | tf_op jit(solution)/shard_map/ppermute | solution.py:494

commit v7 on v2

--- a/solution.py
+++ b/solution.py
@@ -159,7 +159,8 @@
 
 def level_weights(level_factors, present, levels, after, root_basis=None, root_pieces=0):
     slots, last, _, _, rank, _ = level_factors.shape
-    count, pieces = len(levels), 2
+    count = len(levels)
+    pieces = 2 if count == 1 else 1
     roots = []
     if root_pieces:
         here = root_basis.shape[0] // lax.axis_size("order")

time: 31.5 us -> 31.5 us (level)
  no operation moved by 1% of the time
where the time goes in v7:
time: 31.5 us; the launch traced here: 31.3 us
  starting transfers between devices  15.4 us (49%)
  Pallas kernels  13.8 us (44%)
  waiting for transfers between devices  1.95 us (6%)
    ppermute x8, starting transfers between devices, swap(): lax.ppermute(array, axis, [(i, i ^ bits) for i in range(lax.axis_size(axi...  11.5 us
    ppermute x2, starting transfers between devices, swap_both(): return lax.ppermute(array, ('order', 'lat'), pairs)  3.89 us
    pallas_call x2, Pallas kernels, level_weights(): call(functools.partial(factor_kernel, levels, pieces, root_pieces), 'fact...  3.66 us
    pallas_call x2, Pallas kernels, spectra_of(): call(functools.partial(root_kernel, group, first, last), 'root', out, in_...  3.06 us
    pallas_call x4, Pallas kernels, next_states(): call(functools.partial(level_kernel, side, 'order'), name, [jax.ShapeDtyp...  2.14 us
    pallas_call x1, Pallas kernels, leaf_states(): call(functools.partial(leaf_kernel, pieces, group), 'leaf', [jax.ShapeDty...  1.92 us
    pallas_call x1, Pallas kernels, places_of(): call(functools.partial(place_kernel, group), 'places', [jax.ShapeDtypeStr...  1.78 us
    pallas_call x3, Pallas kernels, last_states(): call(functools.partial(last_level_kernel, turn, begin, 'order'), name, [j...  1.23 us
  transfers between devices with their start and end apart: 10, of which 3 were waited for; matrix products, arithmetic and copies ran while one was open for 0% of the time, Pallas kernels for 31%

profile of v7, /device:TPU:0, one launch (start us, length us, event | category | flops | bytes accessed | tf_op | source)
XLA Modules:
  0.0 31.3 jit_solution(8012921622027737209)
XLA Ops:
  0.0 1.9 %leaf.1 = (bf16[16,2,32,128]{3,2,1,0:T(8,128)(2,1)S(1)}, bf16[32,64,256]{2,1,0:T(8,128)(2,1)S(1)}) custom-call(bf16[32,64,256]{2,1,0:T(8,128)(2,1)} %fourier_hbm.1, f32[1,256]{1,0:T(1,128)} %bitcast.4, bf16[32,64,256]{2,1,0:T(8,128)(2,1)} %leaf_hbm.1, bf16[128,64,256]{2,1,0:T(8,128)(2,1)} %root_hbm.3), custom_call_target="tpu_custom_call" | custom-call | flops 67108 | bytes 2097 | tf_op jit(solution)/shard_map/leaf/pallas_call | solution.py:92
  1.9 0.5 %collective-permute-start = (bf16[16,2,32,128]{3,2,1,0:T(8,128)(2,1)S(1)}, bf16[16,2,32,128]{3,2,1,0:T(8,128)(2,1)S(1)}, u32[]{:S(2)}, u32[]{:S(2)}) collective-permute-start(bf16[16,2,32,128]{3,2,1,0:T(8,128)(2,1)S(1)} %get-tuple-element.19.after.state_ref), channel_id=1, source_target_pairs={{0,1},{1,0},{2,3},{3,2},{4,5},{5,4},{6,7},{7,6},{8,9},{9,8},{10,11... | collective-permute-start | bytes 786440 | tf_op jit(solution)/shard_map/ppermute | solution.py:477
  2.5 1.4 %factors.2.weight_ref = bf16[16,128,256]{2,1,0:T(8,128)(2,1)S(1)} custom-call(bf16[32,3,2,1,64,64]{5,4,3,2,1,0:T(8,128)(2,1)} %factor_hbm.3, s32[3,1,32]{2,1,0:T(1,128)} %bitcast.2, bf16[16,2,32,128]{3,2,1,0:T(8,128)(2,1)S(1)} %get-tuple-element.19.after.state_ref), custom_call_target="tpu_custom_call" | custom-call | flops 524 | bytes 2097 | tf_op jit(solution)/shard_map/factors/pallas_call | solution.py:168
  3.9 0.0 collective-permute-done.partner_ref
  3.9 0.4 %level0_0.1.state_ref = bf16[16,32,128]{2,1,0:T(8,128)(2,1)S(1)} custom-call(bf16[16,2,32,128]{3,2,1,0:T(8,128)(2,1)S(1)} %get-tuple-element.19.after.state_ref, bf16[16,2,32,128]{3,2,1,0:T(8,128)(2,1)S(1)} %collective-permute-done.partner_ref, bf16[16,128,256]{2,1,0:T(8,128)(2,1)S(1)} %factors.2.weight_ref), custom_call_target="tpu_custom_call" | custom-call | flops 33554 | bytes 393 | tf_op jit(solution)/shard_map/level0_0/pallas_call | solution.py:219
  4.4 2.7 %collective-permute-start.2 = (bf16[16,32,128]{2,1,0:T(8,128)(2,1)S(1)}, bf16[16,32,128]{2,1,0:T(8,128)(2,1)S(1)}, u32[]{:S(2)}, u32[]{:S(2)}) collective-permute-start(bf16[16,32,128]{2,1,0:T(8,128)(2,1)S(1)} %level0_0.1.state_ref), channel_id=1, source_target_pairs={{0,2},{1,3},{2,0},{3,1},{4,6},{5,7},{6,4},{7,5},{8,10},{9,11},{10,... | collective-permute-start | bytes 393224 | tf_op jit(solution)/shard_map/ppermute | solution.py:477
  7.0 0.4 %level0_1.1.after.state_ref = bf16[16,32,128]{2,1,0:T(8,128)(2,1)S(1)} custom-call(bf16[16,2,32,128]{3,2,1,0:T(8,128)(2,1)S(1)} %get-tuple-element.19.after.state_ref, bf16[16,2,32,128]{3,2,1,0:T(8,128)(2,1)S(1)} %collective-permute-done.partner_ref, bf16[16,128,256]{2,1,0:T(8,128)(2,1)S(1)} %factors.2.weight_ref), custom_call_target="tpu_custom_call" | custom-call | flops 33554 | bytes 393 | tf_op jit(solution)/shard_map/level0_1/pallas_call | solution.py:219
  7.5 0.0 copy-start
  7.5 0.1 collective-permute-start.1
  7.6 2.2 %factors.3 = (bf16[16,128,256]{2,1,0:T(8,128)(2,1)S(1)}, bf16[16,64,128]{2,1,0:T(8,128)(2,1)S(1)}, bf16[16,64,128]{2,1,0:T(8,128)(2,1)S(1)}, bf16[2,32,64,256]{3,2,1,0:T(8,128)(2,1)S(1)}) custom-call(bf16[32,3,2,1,64,64]{5,4,3,2,1,0:T(8,128)(2,1)} %factor_hbm.3, s32[3,1,32]{2,1,0:T(1,128)} %bitcast.3, bf16[16,32,128]{2,1,0:T(8,128)(2,1)S(1)} %level0_1.1.after.state_ref, ...), custom_call_target="tpu_custom_call" | custom-call | flops 1048 | bytes 4194 | tf_op jit(solution)/shard_map/factors/pallas_call | solution.py:168
  9.8 2.0 %collective-permute-start.6 = (bf16[16,64,128]{2,1,0:T(8,128)(2,1)S(1)}, bf16[16,64,128]{2,1,0:T(8,128)(2,1)S(1)}, u32[]{:S(2)}, u32[]{:S(2)}) collective-permute-start(bf16[16,64,128]{2,1,0:T(8,128)(2,1)S(1)} %get-tuple-element.27.cross_ref), channel_id=1, source_target_pairs={{0,8},{8,0},{16,24},{24,16},{1,9},{9,1},{17,25},{25,17},{2,10},{10... | collective-permute-start | bytes 786440 | tf_op jit(solution)/shard_map/ppermute | solution.py:477
  11.8 0.0 collective-permute-done.2.partner_ref
  11.8 0.4 %level1_0.1.own_ref = bf16[16,32,128]{2,1,0:T(8,128)(2,1)S(1)} custom-call(bf16[16,32,128]{2,1,0:T(8,128)(2,1)S(1)} %level0_0.1.state_ref, bf16[16,32,128]{2,1,0:T(8,128)(2,1)S(1)} %collective-permute-done.2.partner_ref, bf16[16,128,256]{2,1,0:T(8,128)(2,1)S(1)} %get-tuple-element.20.weight_ref), custom_call_target="tpu_custom_call" | custom-call | flops 33554 | bytes 393 | tf_op jit(solution)/shard_map/level1_0/pallas_call | solution.py:219
  12.2 2.6 %collective-permute-start.3 = (bf16[16,32,128]{2,1,0:T(8,128)(2,1)S(1)}, bf16[16,32,128]{2,1,0:T(8,128)(2,1)S(1)}, u32[]{:S(2)}, u32[]{:S(2)}) collective-permute-start(bf16[16,32,128]{2,1,0:T(8,128)(2,1)S(1)} %level1_0.1.own_ref), channel_id=1, source_target_pairs={{0,4},{1,5},{2,6},{3,7},{4,0},{5,1},{6,2},{7,3},{8,12},{9,13},{10,... | collective-permute-start | bytes 393224 | tf_op jit(solution)/shard_map/ppermute | solution.py:477
  14.9 0.0 collective-permute-done.1.partner_ref
  14.9 0.8 %level1_1.1 = (bf16[16,32,128]{2,1,0:T(8,128)(2,1)S(1)}, bf16[16,16,128]{2,1,0:T(8,128)(2,1)S(1)}, bf16[16,32,128]{2,1,0:T(8,128)(2,1)S(1)}) custom-call(bf16[16,32,128]{2,1,0:T(8,128)(2,1)S(1)} %level0_1.1.after.state_ref, bf16[16,32,128]{2,1,0:T(8,128)(2,1)S(1)} %collective-permute-done.1.partner_ref, ...), custom_call_target="tpu_custom_call" | custom-call | flops 33554 | bytes 393 | tf_op jit(solution)/shard_map/level1_1/pallas_call | solution.py:219
  15.7 1.5 %collective-permute-start.4 = (bf16[16,32,128]{2,1,0:T(8,128)(2,1)S(1)}, bf16[16,32,128]{2,1,0:T(8,128)(2,1)S(1)}, u32[]{:S(2)}, u32[]{:S(2)}) collective-permute-start(bf16[16,32,128]{2,1,0:T(8,128)(2,1)S(1)} %get-tuple-element.29), channel_id=1, source_target_pairs={{0,8},{8,0},{16,24},{24,16},{1,9},{9,1},{17,25},{25,17},{2,10},{10... | collective-permute-start | bytes 393224 | tf_op jit(solution)/shard_map/ppermute | solution.py:477
  17.2 1.8 %collective-permute-start.8 = (bf16[16,16,128]{2,1,0:T(8,128)(2,1)S(1)}, bf16[16,16,128]{2,1,0:T(8,128)(2,1)S(1)}, u32[]{:S(2)}, u32[]{:S(2)}) collective-permute-start(bf16[16,16,128]{2,1,0:T(8,128)(2,1)S(1)} %get-tuple-element.32), channel_id=1, source_target_pairs={{0,12},{1,13},{2,14},{3,15},{4,8},{5,9},{6,10},{7,11},{8,4},{9,5},... | collective-permute-start | bytes 196616 | tf_op jit(solution)/shard_map/ppermute | solution.py:484
  19.0 0.0 copy-done
  19.0 1.8 %places.1 = (bf16[4,32,128]{2,1,0:T(8,128)(2,1)S(1)}, bf16[256,128]{1,0:T(8,128)(2,1)S(1)}, bf16[1,32,64,256]{3,2,1,0:T(8,128)(2,1)S(1)}) custom-call(s32[128]{0:T(128)S(1)} %copy-done, bf16[16,32,128]{2,1,0:T(8,128)(2,1)S(1)} %get-tuple-element.22.after.state_ref, bf16[128,64,256]{2,1,0:T(8,128)(2,1)} %root_hbm.3), custom_call_target="tpu_custom_call" | custom-call | flops 16 | bytes 131 | tf_op jit(solution)/shard_map/places/pallas_call | solution.py:359
  20.8 2.1 %collective-permute-start.5 = (bf16[16,16,128]{2,1,0:T(8,128)(2,1)S(1)}, bf16[16,16,128]{2,1,0:T(8,128)(2,1)S(1)}, u32[]{:S(2)}, u32[]{:S(2)}) collective-permute-start(bf16[16,16,128]{2,1,0:T(8,128)(2,1)S(1)} %late_columns.1), channel_id=1, source_target_pairs={{0,12},{1,13},{2,14},{3,15},{4,8},{5,9},{6,10},{7,11},{8,4},{9,5},... | collective-permute-start | bytes 196616 | tf_op jit(solution)/shard_map/ppermute | solution.py:484
  22.9 0.0 collective-permute-done.3.partner_ref
  22.9 0.5 %last_own.1 = (bf16[256,128]{1,0:T(8,128)(2,1)S(1)}, bf16[256,128]{1,0:T(8,128)(2,1)S(1)}) custom-call(bf16[256,128]{1,0:T(8,128)(2,1)S(1)} %get-tuple-element.24.after.refs_1_.refs_2_, bf16[16,32,128]{2,1,0:T(8,128)(2,1)S(1)} %level1_0.1.own_ref, bf16[16,32,128]{2,1,0:T(8,128)(2,1)S(1)} %collective-permute-done.3.partner_ref, ...), custom_call_target="tpu_custom_call" | custom-call | flops 33554 | bytes 393 | tf_op jit(solution)/shard_map/last_own/pallas_call | solution.py:317
  23.4 1.6 %collective-permute-start.7 = (bf16[256,128]{1,0:T(8,128)(2,1)S(1)}, bf16[256,128]{1,0:T(8,128)(2,1)S(1)}, u32[]{:S(2)}, u32[]{:S(2)}) collective-permute-start(bf16[256,128]{1,0:T(8,128)(2,1)S(1)} %get-tuple-element.30), channel_id=1, source_target_pairs={{0,16},{8,24},{16,0},{24,8},{1,17},{9,25},{17,1},{25,9},{2,18},{10... | collective-permute-start | bytes 196616 | tf_op jit(solution)/shard_map/ppermute | solution.py:477
  24.9 0.0 collective-permute-done.8.partner_ref
  24.9 0.0 collective-permute-done.4.own_ref
  25.0 0.0 collective-permute-done.6.cross_ref
  25.0 0.4 %last_early.1 = bf16[256,128]{1,0:T(8,128)(2,1)S(1)} custom-call(bf16[256,128]{1,0:T(8,128)(2,1)S(1)} %get-tuple-element.24.after.refs_1_.refs_2_, bf16[16,32,128]{2,1,0:T(8,128)(2,1)S(1)} %collective-permute-done.4.own_ref, bf16[16,16,128]{2,1,0:T(8,128)(2,1)S(1)} %collective-permute-done.8.partner_ref, ...), custom_call_target="tpu_custom_call" | custom-call | flops 16777 | bytes 196 | tf_op jit(solution)/shard_map/last_early/pallas_call | solution.py:317
  25.3 0.5 %collective-permute-start.9 = (bf16[256,128]{1,0:T(8,128)(2,1)S(1)}, bf16[256,128]{1,0:T(8,128)(2,1)S(1)}, u32[]{:S(2)}, u32[]{:S(2)}) collective-permute-start(bf16[256,128]{1,0:T(8,128)(2,1)S(1)} %last_early.1), channel_id=1, source_target_pairs={{0,16},{8,24},{16,0},{24,8},{1,17},{9,25},{17,1},{25,9},{2,18},{10... | collective-permute-start | bytes 196616 | tf_op jit(solution)/shard_map/ppermute | solution.py:477
  25.9 1.1 %collective-permute-done.5.partner_ref = bf16[16,16,128]{2,1,0:T(8,128)(2,1)S(1)} collective-permute-done((bf16[16,16,128]{2,1,0:T(8,128)(2,1)S(1)}, bf16[16,16,128]{2,1,0:T(8,128)(2,1)S(1)}, u32[]{:S(2)}, u32[]{:S(2)}) %collective-permute-start.5) | collective-permute-done | bytes 65568 | tf_op jit(solution)/shard_map/ppermute | solution.py:484
  27.0 0.4 %last_late.1.refs_5_ = bf16[256,128]{1,0:T(8,128)(2,1)S(1)} custom-call(bf16[256,128]{1,0:T(8,128)(2,1)S(1)} %get-tuple-element.24.after.refs_1_.refs_2_, bf16[16,32,128]{2,1,0:T(8,128)(2,1)S(1)} %collective-permute-done.4.own_ref, bf16[16,16,128]{2,1,0:T(8,128)(2,1)S(1)} %collective-permute-done.5.partner_ref, ...), custom_call_target="tpu_custom_call" | custom-call | flops 16777 | bytes 196 | tf_op jit(solution)/shard_map/last_late/pallas_call | solution.py:317
  27.3 0.4 %collective-permute-done.7.refs_6_ = bf16[256,128]{1,0:T(8,128)(2,1)S(1)} collective-permute-done((bf16[256,128]{1,0:T(8,128)(2,1)S(1)}, bf16[256,128]{1,0:T(8,128)(2,1)S(1)}, u32[]{:S(2)}, u32[]{:S(2)}) %collective-permute-start.7) | collective-permute-done | bytes 65568 | tf_op jit(solution)/shard_map/ppermute | solution.py:477
  27.7 1.4 %root.2.refs_0_ = bf16[8,2,256,128]{3,2,1,0:T(8,128)(2,1)S(1)} custom-call(bf16[4,32,128]{2,1,0:T(8,128)(2,1)S(1)} %get-tuple-element.23.refs_0_.refs_1_, bf16[256,128]{1,0:T(8,128)(2,1)S(1)} %get-tuple-element.24.after.refs_1_.refs_2_, bf16[32,64,256]{2,1,0:T(8,128)(2,1)S(1)} %get-tuple-element.25.refs_2_, ...), custom_call_target="tpu_custom_call" | custom-call | flops 50331 | bytes 3145 | tf_op jit(solution)/shard_map/root/pallas_call | solution.py:452
  29.1 0.5 %collective-permute-done.9.refs_4_ = bf16[256,128]{1,0:T(8,128)(2,1)S(1)} collective-permute-done((bf16[256,128]{1,0:T(8,128)(2,1)S(1)}, bf16[256,128]{1,0:T(8,128)(2,1)S(1)}, u32[]{:S(2)}, u32[]{:S(2)}) %collective-permute-start.9) | collective-permute-done | bytes 65568 | tf_op jit(solution)/shard_map/ppermute | solution.py:477
  29.6 1.6 %root.3 = bf16[8,2,256,128]{3,2,1,0:T(8,128)(2,1)} custom-call(bf16[8,2,256,128]{3,2,1,0:T(8,128)(2,1)S(1)} %root.2.refs_0_, bf16[4,32,128]{2,1,0:T(8,128)(2,1)S(1)} %get-tuple-element.23.refs_0_.refs_1_, bf16[256,128]{1,0:T(8,128)(2,1)S(1)} %get-tuple-element.24.after.refs_1_.refs_2_, bf16[1,32,64,256]{3,2,1,0:T(8,128)(2,1)S(1)} %get-tuple-element.31.refs_3_, ...), custom_call_target="tpu_custom_call" | custom-call | flops 16777 | bytes 1048 | tf_op jit(solution)/shard_map/root/pallas_call | solution.py:452
  (1 shorter events, 0.0 us)
Async XLA Ops:
  1.9 2.0 %collective-permute-start = (bf16[16,2,32,128]{3,2,1,0:T(8,128)(2,1)S(1)}, bf16[16,2,32,128]{3,2,1,0:T(8,128)(2,1)S(1)}, u32[]{:S(2)}, u32[]{:S(2)}) collective-permute-start(bf16[16,2,32,128]{3,2,1,0:T(8,128)(2,1)S(1)} %get-tuple-element.19.after.state_ref), channel_id=1, source_target_pairs={{0,1},{1,0},{2,3},{3,2},{4,5},{5,4},{6,7},{7,6},{8,9},{9,8},{10,11... | collective-permute-start | bytes 786440 | tf_op jit(solution)/shard_map/ppermute | solution.py:477
  4.4 7.5 %collective-permute-start.2 = (bf16[16,32,128]{2,1,0:T(8,128)(2,1)S(1)}, bf16[16,32,128]{2,1,0:T(8,128)(2,1)S(1)}, u32[]{:S(2)}, u32[]{:S(2)}) collective-permute-start(bf16[16,32,128]{2,1,0:T(8,128)(2,1)S(1)} %level0_0.1.state_ref), channel_id=1, source_target_pairs={{0,2},{1,3},{2,0},{3,1},{4,6},{5,7},{6,4},{7,5},{8,10},{9,11},{10,... | collective-permute-start | bytes 393224 | tf_op jit(solution)/shard_map/ppermute | solution.py:477
  7.5 11.5 %copy-start = (s32[128]{0:T(128)S(1)}, s32[128]{0:T(128)}, u32[]{:S(2)}) copy-start(s32[128]{0:T(128)} %order_ref.1) | copy-start | bytes 1540
  7.5 7.4 %collective-permute-start.1 = (bf16[16,32,128]{2,1,0:T(8,128)(2,1)S(1)}, bf16[16,32,128]{2,1,0:T(8,128)(2,1)S(1)}, u32[]{:S(2)}, u32[]{:S(2)}) collective-permute-start(bf16[16,32,128]{2,1,0:T(8,128)(2,1)S(1)} %level0_1.1.after.state_ref), channel_id=1, source_target_pairs={{0,2},{1,3},{2,0},{3,1},{4,6},{5,7},{6,4},{7,5},{8,10},{9,11},{10,... | collective-permute-start | bytes 393224 | tf_op jit(solution)/shard_map/ppermute | solution.py:477
  9.8 15.1 %collective-permute-start.6 = (bf16[16,64,128]{2,1,0:T(8,128)(2,1)S(1)}, bf16[16,64,128]{2,1,0:T(8,128)(2,1)S(1)}, u32[]{:S(2)}, u32[]{:S(2)}) collective-permute-start(bf16[16,64,128]{2,1,0:T(8,128)(2,1)S(1)} %get-tuple-element.27.cross_ref), channel_id=1, source_target_pairs={{0,8},{8,0},{16,24},{24,16},{1,9},{9,1},{17,25},{25,17},{2,10},{10... | collective-permute-start | bytes 786440 | tf_op jit(solution)/shard_map/ppermute | solution.py:477
  12.2 10.6 %collective-permute-start.3 = (bf16[16,32,128]{2,1,0:T(8,128)(2,1)S(1)}, bf16[16,32,128]{2,1,0:T(8,128)(2,1)S(1)}, u32[]{:S(2)}, u32[]{:S(2)}) collective-permute-start(bf16[16,32,128]{2,1,0:T(8,128)(2,1)S(1)} %level1_0.1.own_ref), channel_id=1, source_target_pairs={{0,4},{1,5},{2,6},{3,7},{4,0},{5,1},{6,2},{7,3},{8,12},{9,13},{10,... | collective-permute-start | bytes 393224 | tf_op jit(solution)/shard_map/ppermute | solution.py:477
  15.7 9.2 %collective-permute-start.4 = (bf16[16,32,128]{2,1,0:T(8,128)(2,1)S(1)}, bf16[16,32,128]{2,1,0:T(8,128)(2,1)S(1)}, u32[]{:S(2)}, u32[]{:S(2)}) collective-permute-start(bf16[16,32,128]{2,1,0:T(8,128)(2,1)S(1)} %get-tuple-element.29), channel_id=1, source_target_pairs={{0,8},{8,0},{16,24},{24,16},{1,9},{9,1},{17,25},{25,17},{2,10},{10... | collective-permute-start | bytes 393224 | tf_op jit(solution)/shard_map/ppermute | solution.py:477
  17.2 7.8 %collective-permute-start.8 = (bf16[16,16,128]{2,1,0:T(8,128)(2,1)S(1)}, bf16[16,16,128]{2,1,0:T(8,128)(2,1)S(1)}, u32[]{:S(2)}, u32[]{:S(2)}) collective-permute-start(bf16[16,16,128]{2,1,0:T(8,128)(2,1)S(1)} %get-tuple-element.32), channel_id=1, source_target_pairs={{0,12},{1,13},{2,14},{3,15},{4,8},{5,9},{6,10},{7,11},{8,4},{9,5},... | collective-permute-start | bytes 196616 | tf_op jit(solution)/shard_map/ppermute | solution.py:484
  20.8 6.1 %collective-permute-start.5 = (bf16[16,16,128]{2,1,0:T(8,128)(2,1)S(1)}, bf16[16,16,128]{2,1,0:T(8,128)(2,1)S(1)}, u32[]{:S(2)}, u32[]{:S(2)}) collective-permute-start(bf16[16,16,128]{2,1,0:T(8,128)(2,1)S(1)} %late_columns.1), channel_id=1, source_target_pairs={{0,12},{1,13},{2,14},{3,15},{4,8},{5,9},{6,10},{7,11},{8,4},{9,5},... | collective-permute-start | bytes 196616 | tf_op jit(solution)/shard_map/ppermute | solution.py:484
  23.4 4.3 %collective-permute-start.7 = (bf16[256,128]{1,0:T(8,128)(2,1)S(1)}, bf16[256,128]{1,0:T(8,128)(2,1)S(1)}, u32[]{:S(2)}, u32[]{:S(2)}) collective-permute-start(bf16[256,128]{1,0:T(8,128)(2,1)S(1)} %get-tuple-element.30), channel_id=1, source_target_pairs={{0,16},{8,24},{16,0},{24,8},{1,17},{9,25},{17,1},{25,9},{2,18},{10... | collective-permute-start | bytes 196616 | tf_op jit(solution)/shard_map/ppermute | solution.py:477
  25.3 4.3 %collective-permute-start.9 = (bf16[256,128]{1,0:T(8,128)(2,1)S(1)}, bf16[256,128]{1,0:T(8,128)(2,1)S(1)}, u32[]{:S(2)}, u32[]{:S(2)}) collective-permute-start(bf16[256,128]{1,0:T(8,128)(2,1)S(1)} %last_early.1), channel_id=1, source_target_pairs={{0,16},{8,24},{16,0},{24,8},{1,17},{9,25},{17,1},{25,9},{2,18},{10... | collective-permute-start | bytes 196616 | tf_op jit(solution)/shard_map/ppermute | solution.py:477
